TPU v7x, 32 devices: a whole 2x2x4 slice. The times are simulated.
32 devices in a mesh: lat: 2 (over y), ma: 16 (over z, x, core).
Axes of the slice: x: 2, y: 2, z: 4, core: 2. Of those that a mesh axis runs over, the one named last changes fastest.
Arguments:
- inputs: float32 [2, 384, 32, 73], P(None, 'ma', 'lat'), may hold values from -5 to 5
- targets: float32 [2, 2, 384, 32, 73], P(None, None, 'ma', 'lat'), may hold values from -5 to 5
- mask: int32 [2, 384, 32], P(None, 'ma', 'lat'), may hold values 0 or 1
- var_weight: int32 [73], replicated, may hold values from 1 to 4
- step_count: int32 [1], replicated, may hold values from 2 to 20
- spec_w: float32 [3, 96, 2, 256, 256], P(None, 'ma', None, None, 'lat'), may hold values from -1 to 1
- spec_m: float32 [3, 96, 2, 256, 256], P(None, 'ma', None, None, 'lat'), may hold values from -1.335144e-05 to 1.335144e-05
- spec_v: float32 [3, 96, 2, 256, 256], P(None, 'ma', None, None, 'lat'), may hold values from 6.481165e-14 to 2.592466e-13
- encdec_w: float32 [2, 73, 256], replicated, may hold values from -0.5 to 0.5
- encdec_m: float32 [2, 73, 256], replicated, may hold values from -1.335144e-05 to 1.335144e-05
- encdec_v: float32 [2, 73, 256], replicated, may hold values from 6.481165e-14 to 2.592466e-13
- mlp_w: float32 [3, 2, 256, 512], replicated, may hold values from -0.375 to 0.375
- mlp_m: float32 [3, 2, 256, 512], replicated, may hold values from -1.335144e-05 to 1.335144e-05
- mlp_v: float32 [3, 2, 256, 512], replicated, may hold values from 6.481165e-14 to 2.592466e-13
- gain_w: float32 [3, 256], replicated, may hold values from 0.5 to 1.5
- gain_m: float32 [3, 256], replicated, may hold values from -1.335144e-05 to 1.335144e-05
- gain_v: float32 [3, 256], replicated, may hold values from 6.481165e-14 to 2.592466e-13
Outputs:
- loss: float32 [], replicated
- grad_norm: float32 [], replicated
- matrix_norms: float32 [14, 2], replicated
- spec_new: float32 [3, 96, 2, 256, 256], P(None, 'ma', None, None, 'lat')
- spec_m_new: float32 [3, 96, 2, 256, 256], P(None, 'ma', None, None, 'lat')
- spec_v_new: float32 [3, 96, 2, 256, 256], P(None, 'ma', None, None, 'lat')
- spec_low: bfloat16 [3, 96, 2, 256, 256], P(None, 'ma', None, None, 'lat')
- encdec_new: float32 [2, 73, 256], replicated
- encdec_m_new: float32 [2, 73, 256], replicated
- encdec_v_new: float32 [2, 73, 256], replicated
- encdec_low: bfloat16 [2, 73, 256], replicated
- mlp_new: float32 [3, 2, 256, 512], replicated
- mlp_m_new: float32 [3, 2, 256, 512], replicated
- mlp_v_new: float32 [3, 2, 256, 512], replicated
- mlp_low: bfloat16 [3, 2, 256, 512], replicated
- gain_new: float32 [3, 256], replicated
- gain_m_new: float32 [3, 256], replicated
- gain_v_new: float32 [3, 256], replicated
- gain_low: bfloat16 [3, 256], replicated
All inputs are finite; a program needn't handle non-finite values. No bound on the sum of `mask` on one device may be relied on, other than what follows from the above.
Results may differ from a plain program's by a relative error of at most 0.011.
Values may be sent and summed in bfloat16 or wider, within the bound.
A program may use at most 256 MiB of HBM per device.

v0:
```python
import math

import jax
import jax.numpy as jnp
from jax import lax
from jax.sharding import PartitionSpec as P

E = 256
C = 73
L = 96
NB = 3
ROLL = 2


beta_first = 0.9
beta_second = 0.999
adam_eps = 1e-08
weight_decay = 0.01
learn_rate = 0.4
clip_norm = 0.05
norm_eps = 1e-05


def legendre(orders, angles):
    cosines = jnp.cos(angles)[None, :]
    sines = jnp.sin(angles)[None, :]
    order_col = orders[:, None]
    log_start = 0.5 * (
        jnp.log((2.0 * order_col + 1.0) / (4.0 * math.pi))
        + lax.lgamma(2.0 * order_col + 1.0)
        - 2.0 * lax.lgamma(order_col + 1.0)
        - order_col * math.log(4.0)
    ) + order_col * jnp.log(sines)
    starting = jnp.exp(log_start)

    def advance(carry, degree):
        previous, earlier = carry
        upper = jnp.maximum(degree * degree - order_col * order_col, 1.0)
        factor = jnp.sqrt(jnp.maximum(4.0 * degree * degree - 1.0, 1.0) / upper)
        lower = jnp.maximum((degree - 1.0) ** 2 - order_col * order_col, 0.0)
        shrink = jnp.sqrt(lower / jnp.maximum(4.0 * (degree - 1.0) ** 2 - 1.0, 1.0))
        stepped = factor * (cosines * previous - shrink * earlier)
        second = jnp.sqrt(2.0 * order_col + 3.0) * cosines * starting
        value = jnp.where(
            degree < order_col,
            0.0,
            jnp.where(
                degree == order_col, starting, jnp.where(degree == order_col + 1.0, second, stepped)
            ),
        )
        return ((value, previous), value)

    zero_rows = jnp.zeros_like(starting)
    unused, table = lax.scan(advance, (zero_rows, zero_rows), jnp.arange(L, dtype=jnp.float32))
    return table


def dft_tables(orders, count_lon):
    phases = orders[:, None] * jnp.arange(count_lon, dtype=jnp.int32)[None, :] % count_lon
    phase = phases.astype(jnp.float32) * (2.0 * math.pi / count_lon)
    cosines = jnp.cos(phase)
    sines = jnp.sin(phase)
    number = orders.shape[0]
    forward = jnp.stack([cosines, -sines], 1).reshape(2 * number, count_lon)
    factor = jnp.where(orders == 0, 1.0, 2.0)[:, None] / math.sqrt(2.0 * math.pi)
    inverse = jnp.stack([factor * cosines, -factor * sines], 1).reshape(2 * number, count_lon).T
    return (forward, inverse)


def adaptive(weight, first, second, grad, step_float):
    first_new = beta_first * first + (1.0 - beta_first) * grad
    second_new = beta_second * second + (1.0 - beta_second) * grad * grad
    direction = (
        first_new
        / (1.0 - beta_first**step_float)
        / (jnp.sqrt(second_new / (1.0 - beta_second**step_float)) + adam_eps)
        + weight_decay * weight
    )
    return (first_new, second_new, direction)


def lamb_dense(weight, first, second, grad, step_float, groups):
    first_new, second_new, direction = adaptive(weight, first, second, grad, step_float)
    flat_weight = weight.reshape(groups, -1)
    flat_dir = direction.reshape(groups, -1)
    weight_norm = jnp.sqrt(jnp.sum(flat_weight * flat_weight, 1))
    dir_norm = jnp.sqrt(jnp.sum(flat_dir * flat_dir, 1))
    trust = weight_norm / (dir_norm + 1e-06)
    new_weight = (flat_weight - learn_rate * trust[:, None] * flat_dir).reshape(weight.shape)
    return (new_weight, first_new, second_new, jnp.stack([weight_norm, dir_norm], 1))


def norm_forward(hidden, gain_vec):
    centre = jnp.mean(hidden, -1, keepdims=True)
    centred = hidden - centre
    inv_std = lax.rsqrt(jnp.mean(centred * centred, -1, keepdims=True) + norm_eps)
    normal = centred * inv_std
    return ((normal * gain_vec).astype(jnp.bfloat16), normal, inv_std)


def norm_backward(d_normed, normal, inv_std, gain_vec):
    scaled = d_normed * gain_vec
    d_gain = jnp.sum(d_normed * normal, axis=(0, 1, 2))
    d_hidden = inv_std * (
        scaled
        - jnp.mean(scaled, -1, keepdims=True)
        - normal * jnp.mean(scaled * normal, -1, keepdims=True)
    )
    return (d_hidden, d_gain)


def mlp_forward(merged, weights):
    merged_low = merged.astype(jnp.bfloat16)
    pre_act = jnp.einsum(
        "jibe,ef->jibf", merged_low, weights[0], preferred_element_type=jnp.float32
    )
    gelu_out = jax.nn.gelu(pre_act).astype(jnp.bfloat16)
    hidden = merged + jnp.einsum(
        "jibf,ef->jibe", gelu_out, weights[1], preferred_element_type=jnp.float32
    )
    return (hidden, (merged_low, pre_act, gelu_out))


def mlp_backward(d_hidden, stored, weights):
    merged_low, pre_act, gelu_out = stored
    d_branch = d_hidden.astype(jnp.bfloat16)
    d_gelu = jnp.einsum("jibe,ef->jibf", d_branch, weights[1], preferred_element_type=jnp.float32)
    unused, pullback = jax.vjp(jax.nn.gelu, pre_act)
    d_pre = pullback(d_gelu)[0].astype(jnp.bfloat16)
    grad_out = jnp.einsum("jibf,jibe->ef", gelu_out, d_branch, preferred_element_type=jnp.float32)
    grad_in = jnp.einsum("jibe,jibf->ef", merged_low, d_pre, preferred_element_type=jnp.float32)
    d_merged = d_hidden + jnp.einsum(
        "jibf,ef->jibe", d_pre, weights[0], preferred_element_type=jnp.float32
    )
    return (d_merged, jnp.stack([grad_in, grad_out], 0))


def local(
    inputs,
    targets,
    mask,
    var_weight,
    step_count,
    spec_w,
    spec_m,
    spec_v,
    encdec_w,
    encdec_m,
    encdec_v,
    mlp_w,
    mlp_m,
    mlp_v,
    gain_w,
    gain_m,
    gain_v,
):
    n_ma = lax.axis_size("ma")
    n_lat = lax.axis_size("lat")
    ma_pos = lax.axis_index("ma")
    lat_pos = lax.axis_index("lat")
    batch = inputs.shape[0]
    lon_loc = inputs.shape[1]
    lat_loc = inputs.shape[2]
    nlon_all = lon_loc * n_ma
    nlat_all = lat_loc * n_lat
    orders_loc = L // n_ma
    angles = (jnp.arange(nlat_all, dtype=jnp.float32) + 0.5) * (math.pi / nlat_all)
    local_orders = ma_pos * orders_loc + jnp.arange(orders_loc, dtype=jnp.int32)
    table = legendre(local_orders.astype(jnp.float32), angles)
    quadrature = jnp.sin(angles) * (math.sqrt(2.0 * math.pi) / nlon_all * math.pi / nlat_all)
    fwd_leg = (table * quadrature[None, None, :]).astype(jnp.bfloat16)
    inv_leg = table.astype(jnp.bfloat16)
    fwd_table, inv_table = dft_tables(jnp.arange(L, dtype=jnp.int32), nlon_all)
    fwd_four = fwd_table.astype(jnp.bfloat16)
    inv_four = inv_table.astype(jnp.bfloat16)
    fwd_back = fwd_four.T
    inv_back = inv_four.T
    sines = jnp.sin(angles)
    area = sines / jnp.mean(sines)
    area_rows = lax.dynamic_slice_in_dim(area, lat_pos * lat_loc, lat_loc)
    mask_grid = jnp.transpose(mask, (1, 2, 0)).astype(jnp.float32)
    pixel_weight = (
        area_rows[None, :, None, None]
        * var_weight.astype(jnp.float32)[None, None, None, :]
        * mask_grid[:, :, :, None]
    )
    grid_targets = jnp.transpose(targets, (0, 2, 3, 1, 4))
    denom = float(batch * nlon_all * nlat_all * C)

    def apply_table(table_full, block_in):
        whole_out = jnp.einsum(
            "ok,kibe->oibe",
            table_full,
            lax.all_to_all(block_in, "ma", split_axis=3, concat_axis=0, tiled=True),
            preferred_element_type=jnp.float32,
        )
        return lax.all_to_all(
            whole_out.astype(jnp.bfloat16), "ma", split_axis=0, concat_axis=3, tiled=True
        ).astype(whole_out.dtype)

    def spectral_backward(d_filtered, owned, weight_blk):
        d_rows = apply_table(inv_back, d_filtered.astype(jnp.bfloat16)).astype(jnp.bfloat16)
        d_spec = lax.all_to_all(d_rows, "lat", split_axis=3, concat_axis=1, tiled=True)
        out_width = d_spec.shape[3]
        d_mixed = jnp.einsum(
            "lmi,mpibo->lmpbo",
            inv_leg,
            d_spec.reshape(orders_loc, 2, nlat_all, batch, out_width),
            preferred_element_type=jnp.float32,
        ).astype(jnp.bfloat16)
        d_own = lax.all_to_all(d_mixed, "ma", split_axis=0, concat_axis=1, tiled=True)
        real_w = weight_blk[:, 0]
        imag_w = weight_blk[:, 1]
        d_real = d_own[:, :, 0]
        d_imag = d_own[:, :, 1]
        d_coef_real = jnp.einsum(
            "lmbo,leo->lmbe", d_real, real_w, preferred_element_type=jnp.float32
        ) + jnp.einsum("lmbo,leo->lmbe", d_imag, imag_w, preferred_element_type=jnp.float32)
        d_coef_imag = jnp.einsum(
            "lmbo,leo->lmbe", d_imag, real_w, preferred_element_type=jnp.float32
        ) - jnp.einsum("lmbo,leo->lmbe", d_real, imag_w, preferred_element_type=jnp.float32)
        grad_real = jnp.einsum(
            "lmbe,lmbo->leo", owned[:, :, 0], d_real, preferred_element_type=jnp.float32
        ) + jnp.einsum("lmbe,lmbo->leo", owned[:, :, 1], d_imag, preferred_element_type=jnp.float32)
        grad_imag = jnp.einsum(
            "lmbe,lmbo->leo", owned[:, :, 0], d_imag, preferred_element_type=jnp.float32
        ) - jnp.einsum("lmbe,lmbo->leo", owned[:, :, 1], d_real, preferred_element_type=jnp.float32)
        d_owned = jnp.stack([d_coef_real, d_coef_imag], 2)
        d_coeffs = lax.all_to_all(
            d_owned.astype(jnp.bfloat16), "ma", split_axis=1, concat_axis=0, tiled=True
        ).astype(d_owned.dtype)
        d_full = jnp.einsum(
            "lmi,lmpbe->mpibe",
            fwd_leg.astype(jnp.float32),
            d_coeffs,
            precision=lax.Precision.HIGHEST,
        ).reshape(2 * orders_loc, nlat_all, batch, E)
        d_spec_rows = lax.psum_scatter(
            d_full.astype(jnp.bfloat16), "lat", scatter_dimension=1, tiled=True
        )
        return (apply_table(fwd_back, d_spec_rows), jnp.stack([grad_real, grad_imag], 1))

    spec_bf = spec_w.astype(jnp.bfloat16)
    encdec_bf = encdec_w.astype(jnp.bfloat16)
    mlp_bf = mlp_w.astype(jnp.bfloat16)

    def model_backward(d_pred, stored):
        state_low, hidden_low, records = stored
        d_dec = d_pred.astype(jnp.bfloat16)
        grad_dec = jnp.einsum(
            "jibe,jibc->ce", hidden_low, d_dec, preferred_element_type=jnp.float32
        )
        d_hidden = jnp.einsum(
            "jibc,ce->jibe", d_dec, encdec_bf[1], preferred_element_type=jnp.float32
        )
        spec_grads = [None] * NB
        mlp_grads = [None] * NB
        gain_grads = [None] * NB
        for block_idx in reversed(range(NB)):
            normal, inv_std, owned, mlp_kept = records[block_idx]
            d_merged, mlp_grads[block_idx] = mlp_backward(d_hidden, mlp_kept, mlp_bf[block_idx])
            d_normed, spec_grads[block_idx] = spectral_backward(d_merged, owned, spec_bf[block_idx])
            d_norm_in, gain_grads[block_idx] = norm_backward(
                d_normed, normal, inv_std, gain_w[block_idx]
            )
            d_hidden = d_merged + d_norm_in
        d_enc = d_hidden.astype(jnp.bfloat16)
        grad_enc = jnp.einsum("jibc,jibe->ce", state_low, d_enc, preferred_element_type=jnp.float32)
        d_state = d_pred + jnp.einsum(
            "jibe,ce->jibc", d_enc, encdec_bf[0], preferred_element_type=jnp.float32
        )
        return (
            d_state,
            (
                jnp.stack([grad_enc, grad_dec], 0),
                jnp.stack(spec_grads, 0),
                jnp.stack(mlp_grads, 0),
                jnp.stack(gain_grads, 0),
            ),
        )

    state = jnp.transpose(inputs, (1, 2, 0, 3))
    history = []
    loss_part = jnp.zeros((), jnp.float32)
    for section_idx in range(ROLL):
        model_state_low = state.astype(jnp.bfloat16)
        hidden = jnp.einsum(
            "jibc,ce->jibe", model_state_low, encdec_bf[0], preferred_element_type=jnp.float32
        )
        model_records = []
        for model_block_idx in range(NB):
            model_normed, model_normal, model_inv_std = norm_forward(
                hidden, gain_w[model_block_idx]
            )
            spectral_weight_blk = spec_bf[model_block_idx]
            spec_rows = apply_table(fwd_four, model_normed).astype(jnp.bfloat16)
            piece = lax.all_gather(spec_rows, "lat", axis=1, tiled=True)
            row_width = piece.shape[1]
            paired = piece.reshape(orders_loc, 2, row_width, piece.shape[2], piece.shape[3])
            coeffs = jnp.einsum(
                "lmi,mpibe->lmpbe", fwd_leg, paired, preferred_element_type=jnp.float32
            ).astype(jnp.bfloat16)
            spectral_owned = lax.all_to_all(coeffs, "ma", split_axis=0, concat_axis=1, tiled=True)
            spectral_real_w = spectral_weight_blk[:, 0]
            spectral_imag_w = spectral_weight_blk[:, 1]
            mixed_real = jnp.einsum(
                "lmbe,leo->lmbo",
                spectral_owned[:, :, 0],
                spectral_real_w,
                preferred_element_type=jnp.float32,
            ) - jnp.einsum(
                "lmbe,leo->lmbo",
                spectral_owned[:, :, 1],
                spectral_imag_w,
                preferred_element_type=jnp.float32,
            )
            mixed_imag = jnp.einsum(
                "lmbe,leo->lmbo",
                spectral_owned[:, :, 0],
                spectral_imag_w,
                preferred_element_type=jnp.float32,
            ) + jnp.einsum(
                "lmbe,leo->lmbo",
                spectral_owned[:, :, 1],
                spectral_real_w,
                preferred_element_type=jnp.float32,
            )
            mixed_owned = jnp.stack([mixed_real, mixed_imag], 2).astype(jnp.bfloat16)
            mixed = lax.all_to_all(mixed_owned, "ma", split_axis=1, concat_axis=0, tiled=True)
            spec_out = jnp.einsum(
                "lmi,lmpbo->mpibo", inv_leg, mixed, preferred_element_type=jnp.float32
            )
            spec_out = spec_out.astype(jnp.bfloat16).reshape(
                2 * orders_loc, nlat_all, batch, mixed.shape[4]
            )
            rows_out = lax.all_to_all(spec_out, "lat", split_axis=1, concat_axis=3, tiled=True)
            filtered = apply_table(inv_four, rows_out)
            hidden, model_mlp_kept = mlp_forward(hidden + filtered, mlp_bf[model_block_idx])
            model_records.append((model_normal, model_inv_std, spectral_owned, model_mlp_kept))
        model_hidden_low = hidden.astype(jnp.bfloat16)
        prediction = state + jnp.einsum(
            "jibe,ce->jibc", model_hidden_low, encdec_bf[1], preferred_element_type=jnp.float32
        )
        prediction, stored = (prediction, (model_state_low, model_hidden_low, model_records))
        misfit = prediction - grid_targets[section_idx]
        loss_part = loss_part + jnp.sum(pixel_weight * misfit * misfit) / denom
        history.append((stored, misfit))
        state = prediction
    d_state = jnp.zeros_like(state)
    totals = None
    for section_idx in reversed(range(ROLL)):
        stored, misfit = history[section_idx]
        d_pred = 2.0 * pixel_weight * misfit / denom + d_state
        d_state, section_grads = model_backward(d_pred, stored)
        totals = section_grads if totals is None else jax.tree.map(jnp.add, totals, section_grads)
    grad_encdec, spec_grad, grad_mlp, grad_gain = totals
    grad_encdec, grad_mlp, grad_gain, loss_value, spec_square, weight_square = lax.psum(
        (
            grad_encdec,
            grad_mlp,
            grad_gain,
            loss_part,
            jnp.sum(spec_grad * spec_grad),
            jnp.sum(spec_w * spec_w, axis=(1, 2, 3, 4)),
        ),
        ("lat", "ma"),
    )
    total_square = (
        spec_square
        + jnp.sum(grad_encdec * grad_encdec)
        + jnp.sum(grad_mlp * grad_mlp)
        + jnp.sum(grad_gain * grad_gain)
    )
    grad_norm = jnp.sqrt(total_square)
    scale = clip_norm / jnp.maximum(grad_norm, clip_norm)
    step_float = step_count[0].astype(jnp.float32)
    spec_m_new, spec_v_new, direction = adaptive(
        spec_w, spec_m, spec_v, spec_grad * scale, step_float
    )
    dir_square = lax.psum(jnp.sum(direction * direction, axis=(1, 2, 3, 4)), ("lat", "ma"))
    weight_norm = jnp.sqrt(weight_square)
    dir_norm = jnp.sqrt(dir_square)
    trust = weight_norm / (dir_norm + 1e-06)
    spec_new = spec_w - learn_rate * trust[:, None, None, None, None] * direction
    encdec_new, encdec_m_new, encdec_v_new, encdec_norms = lamb_dense(
        encdec_w, encdec_m, encdec_v, grad_encdec * scale, step_float, 2
    )
    mlp_new, mlp_m_new, mlp_v_new, mlp_norms = lamb_dense(
        mlp_w, mlp_m, mlp_v, grad_mlp * scale, step_float, 2 * NB
    )
    gain_new, gain_m_new, gain_v_new, gain_norms = lamb_dense(
        gain_w, gain_m, gain_v, grad_gain * scale, step_float, NB
    )
    matrix_norms = jnp.concatenate(
        [jnp.stack([weight_norm, dir_norm], 1), encdec_norms, mlp_norms, gain_norms], 0
    )
    return (
        loss_value,
        grad_norm,
        matrix_norms,
        spec_new,
        spec_m_new,
        spec_v_new,
        spec_new.astype(jnp.bfloat16),
        encdec_new,
        encdec_m_new,
        encdec_v_new,
        encdec_new.astype(jnp.bfloat16),
        mlp_new,
        mlp_m_new,
        mlp_v_new,
        mlp_new.astype(jnp.bfloat16),
        gain_new,
        gain_m_new,
        gain_v_new,
        gain_new.astype(jnp.bfloat16),
    )


def solution(mesh):
    placed = (
        P(None, "ma", "lat", None),
        P(None, None, "ma", "lat", None),
        P(None, "ma", "lat"),
        P(),
        P(),
        P(None, "ma", None, None, "lat"),
        P(None, "ma", None, None, "lat"),
        P(None, "ma", None, None, "lat"),
        P(),
        P(),
        P(),
        P(),
        P(),
        P(),
        P(),
        P(),
        P(),
    )
    return jax.shard_map(
        local,
        mesh=mesh,
        in_specs=placed,
        out_specs=(
            P(),
            P(),
            P(),
            P(None, "ma", None, None, "lat"),
            P(None, "ma", None, None, "lat"),
            P(None, "ma", None, None, "lat"),
            P(None, "ma", None, None, "lat"),
            P(),
            P(),
            P(),
            P(),
            P(),
            P(),
            P(),
            P(),
            P(),
            P(),
            P(),
            P(),
        ),
        check_vma=False,
    )
```

profile of v0, /device:TPU:0, one launch (start us, length us, event | category | flops | bytes accessed | tf_op | source)
XLA Modules:
  0.0 3929.7 jit_solution(17833496216274131718)
XLA Ops:
  61.1 513.1 %while.21 = (s32[]{:T(128)}, f32[6,32]{1,0:T(8,128)S(1)}, f32[6,32]{1,0:T(8,128)S(1)}, f32[96,6,32]{2,1,0:T(8,128)S(1)}, f32[96]{0:T(128)S(1)}, /*index=5*/s32[]...) while((s32[]{:T(128)}, f32[6,32]{1,0:T(8,128)S(1)}, ...), condition=%wide.region_4.5_spmd.clone.clone.clone.clone, body=%wide.region_3.4_spmd.clone.clone.clone.clone.sunk | while | flops 2513 | bytes 26145 | solution.py:54
  599.8 22.5 all-to-all-done.2
  627.3 24.6 all_to_all.1386
  782.4 16.8 all_to_all.1387
  860.6 32.3 all_to_all.1389
  896.8 20.8 all_to_all.1390
  1123.2 32.3 all_to_all.1396
  1159.4 20.5 all_to_all.1397
  1387.4 32.3 all_to_all.1403
  1423.6 20.6 all_to_all.1404
  1612.3 32.3 all_to_all.1410
  1648.3 20.4 all_to_all.1411
  1855.3 32.3 all_to_all.1417
  1891.4 20.6 all_to_all.1418
  2132.2 19.9 all_to_all.1424
  2155.7 32.5 all_to_all.1425
  2191.8 22.3 all-reduce.17.cloned.1.call-done
  2425.3 20.0 all_to_all.1430
  2448.9 32.3 all_to_all.1431
  2483.5 23.6 all-reduce.19.cloned.1.call-done
  2698.8 20.1 all_to_all.1436
  2722.5 32.3 all_to_all.1437
  2757.1 23.6 all-reduce.21.cloned.1.call-done
  2976.1 20.0 all_to_all.1442
  2999.8 32.3 all_to_all.1443
  3034.3 23.6 all-reduce.23.cloned.1.call-done
  3242.1 20.0 all_to_all.1449
  3302.0 25.6 all-reduce.25.cloned.1.call-done
  3568.7 24.6 all-reduce.27.cloned.1.call-done
  3703.7 39.1 all-reduce.7
  3743.3 86.2 %all-reduce.29.cloned.1.call-done = (f32[2,73,256]{2,1,0:T(8,128)}, f32[3,2,256,512]{3,2,1,0:T(8,128)}) async-done(((f32[2,73,256]{2,1,0:T(8,128)}, f32[3,2,256,512]{3,2,1,0:T(8,128)}), (f32[2,73,256]{2,1,0:T(8,128)}, f32[3,2,256,512]{3,2,1,0:T(8,128)})) %all-reduce.29.cloned.1.call-update) | async-done | bytes 3295248 | tf_op jit(solution)/shard_map/psum | solution.py:357
  3859.9 39.9 %all-reduce.6 = (f32[]{:T(128)}, f32[3]{0:T(128)S(1)}, f32[3]{0:T(128)S(1)}) all-reduce(f32[]{:T(128)S(6)} %multiply.204, f32[3]{0:T(128)S(1)} %get-tuple-element.473, f32[3]{0:T(128)S(1)} %copy-done.213), channel_id=1, replica_groups=mesh['lat'=2,'ma'=16] {'lat','ma'}, use_global_device_ids=true, to_apply=%region_17.18 | all-reduce | flops 7 | bytes 56 | tf_op jit(solution)/shard_map/psum | solution.py:357
  (1922 shorter events, 2722.9 us)
Async XLA Ops:
  9.1 1288.0 %copy-start.198 = (f32[1,256]{1,0:T(1,128)}, f32[1,256]{1,0:T(1,128)S(1)}, u32[]{:S(2)}) copy-start(f32[1,256]{1,0:T(1,128)S(1)} %get-tuple-element.538) | copy-start | bytes 3076
  9.1 1526.3 %copy-start.195 = (f32[1,256]{1,0:T(1,128)}, f32[1,256]{1,0:T(1,128)S(1)}, u32[]{:S(2)}) copy-start(f32[1,256]{1,0:T(1,128)S(1)} %get-tuple-element.537) | copy-start | bytes 3076
  11.4 753.0 %copy-start.9 = (f32[24,16,2,256]{3,1,2,0:T(8,128)}, f32[24,16,2,256]{3,1,2,0:T(8,128)S(1)}, u32[]{:S(2)}) copy-start(f32[24,16,2,256]{3,1,2,0:T(8,128)S(1)} %get-tuple-element.552) | copy-start | bytes 2359300
  21.2 19.6 all-to-all-start
  57.1 517.5 %all-to-all-start.1 = ((bf16[16,2,3072]{2,1,0:T(2,128)(2,1)}), bf16[16,2,3072]{2,1,0:T(2,128)(2,1)S(1)}, u32[]{:S(2)}, u32[]{:S(2)}) async-start(bf16[16,2,3072]{2,1,0:T(2,128)(2,1)} %reshape.1210), calls=%async_computation.1 | async-start | bytes 393216 | tf_op jit(solution)/shard_map/all_to_all | solution.py:197
  591.2 31.0 all-to-all-start.2
  599.8 823.0 %copy-start = (bf16[6,2,256,128]{3,2,0,1:T(8,128)(2,1)}, bf16[6,2,256,128]{3,2,0,1:T(8,128)(2,1)S(1)}, u32[]{:S(2)}) copy-start(bf16[6,2,256,128]{3,2,0,1:T(8,128)(2,1)S(1)} %get-tuple-element.507) | copy-start | bytes 2359300
  653.3 9.4 all-to-all-start.4
  674.6 13.2 all-to-all-start.5
  725.1 16.6 all-to-all-start.6
  1032.1 256.7 %copy-start.5 = (f32[24,16,2,256]{3,1,2,0:T(8,128)}, f32[24,16,2,256]{3,1,2,0:T(8,128)S(1)}, u32[]{:S(2)}) copy-start(f32[24,16,2,256]{3,1,2,0:T(8,128)S(1)} %get-tuple-element.560) | copy-start | bytes 2359300
  1981.6 16.4 all-to-all-start.41
  1985.8 228.3 %all-reduce.17.cloned.1.call-start = ((), (), s32[]{:S(2)}) async-start(), calls=%async_computation.84 | async-start | bytes 786432
  2278.8 16.4 all-to-all-start.48
  2283.0 224.0 %all-reduce.19.cloned.1.call-start = ((), (), s32[]{:S(2)}) async-start(), calls=%async_computation.85 | async-start | bytes 786432
  2564.2 15.7 all-to-all-start.55
  2567.8 212.9 %all-reduce.21.cloned.1.call-start = ((), (), s32[]{:S(2)}) async-start(), calls=%async_computation.86 | async-start | bytes 786432
  2837.9 15.7 all-to-all-start.62
  2841.5 216.4 %all-reduce.23.cloned.1.call-start = ((), (), s32[]{:S(2)}) async-start(), calls=%async_computation.87 | async-start | bytes 786432
  3266.7 29.5 all-to-all-start.74
  3271.1 56.4 %all-reduce.25.cloned.1.call-start = ((), (), s32[]{:S(2)}) async-start(), calls=%async_computation.88 | async-start | bytes 786432
  3332.5 14.8 all-to-all-start.75
  3374.0 16.0 all-to-all-start.76
  3432.2 15.7 all-to-all-start.77
  3464.2 12.8 all-to-all-start.78
  3491.3 8.2 all-to-all-start.79
  3508.7 19.1 all-to-all-start.80
  3532.3 29.6 all-to-all-start.81
  3536.8 56.5 %all-reduce.27.cloned.1.call-start = ((), (), s32[]{:S(2)}) async-start(), calls=%async_computation.89 | async-start | bytes 786432
  3603.3 15.0 all-to-all-start.82
  3647.2 15.7 all-to-all-start.83
  3650.8 178.7 %all-reduce.29.cloned.1.call-start = ((), (), s32[]{:S(2)}) async-start(), calls=%async_computation.90 | async-start | bytes 6619136 | tf_op jit(solution)/shard_map/psum | solution.py:357
  (219 other events, 1228.9 us)
Sparse Core Ops, SparseCore 0:
  2190.7 23.3 all-reduce.16
  2483.6 23.3 all-reduce.18
  2757.3 23.4 all-reduce.20
  3034.5 23.3 all-reduce.22
  3299.9 27.5 all-reduce.24
  3565.7 27.5 all-reduce.26
  3692.9 136.5 all-reduce.28
where the time goes:
time: 3970 us; the launch traced here: 3930 us
  local copies, waits for them, and re-layouts  1490 us (38%)
  blocking collectives  1210 us (30%)
  waiting for transfers between devices  406 us (10%)
  loops' own time  315 us (8%)
  other arithmetic  258 us (6%)
  matrix products  135 us (3%)
  starting transfers between devices  89.9 us (2%)
    unnamed x597, local copies, waits for them, and re-layouts  694 us
    another operation x1, loops' own time, legendre(): lax.scan(advance, (zero_rows, zero_rows), jnp.arange(L, dtype=jnp.float32))  315 us
    all_to_all x19, blocking collectives, apply_table(): lax.all_to_all(block_in, 'ma', split_axis=3, concat_axis=0, tiled=True)  284 us
    all_to_all x15, blocking collectives, apply_table(): lax.all_to_all(whole_out.astype(jnp.bfloat16), 'ma', split_axis=0, concat...  208 us
    convert_element_type x30, local copies, waits for them, and re-layouts, apply_table(): return lax.all_to_all(whole_out.astype(jnp.bfloat16), 'ma', split_axis=0,...  197 us
    all_to_all x5, blocking collectives, local(): lax.all_to_all(coeffs, 'ma', split_axis=0, concat_axis=1, tiled=True)  162 us
    unnamed x13, waiting for transfers between devices  143 us
    all_to_all x24, local copies, waits for them, and re-layouts, apply_table(): lax.all_to_all(block_in, 'ma', split_axis=3, concat_axis=0, tiled=True)  137 us
  transfers between devices with their start and end apart: 27, of which 26 were waited for; matrix products, arithmetic and copies ran while one was open for 7% of the time, Pallas kernels for 0%

commit v1 on v0

--- a/solution.py
+++ b/solution.py
@@ -1,8 +1,13 @@
+import functools
 import math
 
 import jax
 import jax.numpy as jnp
+import ml_dtypes
+import numpy as np
 from jax import lax
+from jax.experimental import pallas as pl
+from jax.experimental.pallas import tpu as pltpu
 from jax.sharding import PartitionSpec as P
 
 E = 256
@@ -135,7 +140,7 @@
     return (d_merged, jnp.stack([grad_in, grad_out], 0))
 
 
-def local(
+def general(
     inputs,
     targets,
     mask,
@@ -417,6 +422,581 @@
     )
 
 
+RANKS = 16
+ORDS = L // RANKS
+SLOTS = 8
+F32 = jnp.float32
+BF16 = jnp.bfloat16
+
+
+def legendre_f64(nlat):
+    theta = (np.arange(nlat) + 0.5) * (math.pi / nlat)
+    cosines, sines = np.cos(theta), np.sin(theta)
+    table = np.zeros((L, L, nlat))
+    for m in range(L):
+        log_start = 0.5 * (
+            math.log((2.0 * m + 1.0) / (4.0 * math.pi))
+            + math.lgamma(2.0 * m + 1.0)
+            - 2.0 * math.lgamma(m + 1.0)
+            - m * math.log(4.0)
+        ) + m * np.log(sines)
+        table[m, m] = np.exp(log_start)
+        if m + 1 < L:
+            table[m + 1, m] = math.sqrt(2.0 * m + 3.0) * cosines * table[m, m]
+        for k in range(m + 2, L):
+            factor = math.sqrt((4.0 * k * k - 1.0) / (k * k - m * m))
+            shrink = math.sqrt(((k - 1.0) ** 2 - m * m) / (4.0 * (k - 1.0) ** 2 - 1.0))
+            table[k, m] = factor * (cosines * table[k - 1, m] - shrink * table[k - 2, m])
+    return table, sines
+
+
+def low_np(array):
+    return array.astype(np.float32).astype(ml_dtypes.bfloat16)
+
+
+def slot_map():
+    degree = np.full((RANKS, 3, SLOTS), -1)
+    order = np.full((RANKS, SLOTS), -1)
+    for d in range(RANKS):
+        y, w, xc = d // 8, (d // 4) % 2, d % 4
+        lo, hi = 4 * w + xc, 4 * (3 - w) + xc
+        n_lo, n_hi = (6 * lo + 5) // RANKS + 1, (6 * hi + 5) // RANKS + 1
+        for group, first, count in ((hi, 0, n_hi), (lo, SLOTS - n_lo, n_lo)):
+            for r in range(count):
+                order[d, first + r] = r
+                for t in range(3):
+                    degree[d, t, first + r] = 6 * group + 3 * y + t
+    return degree, order
+
+
+def make_tables(nlat, nlon):
+    table, sines = legendre_f64(nlat)
+    quadrature = sines * (math.sqrt(2.0 * math.pi) / nlon * math.pi / nlat)
+    fwd_leg = np.asarray(low_np(table * quadrature[None, None, :]))
+    inv_leg = np.asarray(low_np(table))
+    degree, order = slot_map()
+    shape = (RANKS, RANKS, 3, 2, SLOTS, RANKS, ORDS, 2, 2)
+    fwd = np.zeros(shape, ml_dtypes.bfloat16)
+    inv = np.zeros(shape, ml_dtypes.bfloat16)
+    for g in range(RANKS):
+        for d in range(RANKS):
+            for slot in range(SLOTS):
+                r = order[d, slot]
+                if r < 0:
+                    continue
+                for t in range(3):
+                    k, m = degree[d, t, slot], g + RANKS * r
+                    for p in range(2):
+                        fwd[g, d, t, p, slot, :, r, p, :] = fwd_leg[k, m].reshape(RANKS, 2)
+                        inv[g, d, t, p, slot, :, r, p, :] = inv_leg[k, m].reshape(RANKS, 2)
+    rows = RANKS * 3 * 2 * SLOTS
+    cols = RANKS * ORDS * 2 * 2
+    fwd = fwd.reshape(RANKS, rows, cols)
+    inv = inv.reshape(RANKS, rows, cols).transpose(0, 2, 1)
+    phase = 2.0 * math.pi * (np.arange(L)[:, None] * np.arange(nlon)[None, :] % nlon) / nlon
+    scale = np.where(np.arange(L) == 0, 1.0, 2.0)[:, None] / math.sqrt(2.0 * math.pi)
+    four = low_np(np.stack([np.cos(phase), -np.sin(phase)], 1))
+    back = low_np(np.stack([scale * np.cos(phase), -scale * np.sin(phase)], 1))
+    def wide(small):
+        out = np.zeros((RANKS, ORDS, 2, 2, 2, nlon), ml_dtypes.bfloat16)
+        ordered = small.reshape(ORDS, RANKS, 2, nlon).transpose(1, 0, 2, 3)
+        for il in range(2):
+            out[:, :, :, il, il, :] = ordered
+        return out.reshape(cols, 2 * nlon)
+    return fwd, np.ascontiguousarray(inv), wide(four), np.ascontiguousarray(wide(back).T)
+
+
+def place():
+    ma = lax.axis_index("ma")
+    y = lax.axis_index("lat")
+    z = ma // 4
+    zh = z // 2
+    w = z + zh * (3 - 2 * z)
+    return zh, y, w, 8 * y + 4 * w + ma % 4
+
+
+def device_of(zh, q):
+    w = (q // 4) % 2
+    z = w + zh * (3 - 2 * w)
+    return {"lat": q // 8, "ma": 4 * z + q % 4}
+
+
+def enter(zh, q):
+    barrier = pltpu.get_barrier_semaphore()
+
+    def greet(s, carry):
+        pl.semaphore_signal(
+            barrier, inc=1, device_id=device_of(zh, (q + s) % RANKS), device_id_type=pl.DeviceIdType.MESH
+        )
+        return carry
+
+    lax.fori_loop(1, RANKS, greet, 0)
+    pl.semaphore_wait(barrier, RANKS - 1)
+
+
+def exchange(send, recv, send_sem, recv_sem, zh, q):
+    pltpu.make_async_copy(send.at[q], recv.at[q], recv_sem).start()
+
+    def push(s, carry):
+        d = (q + s) % RANKS
+        pltpu.make_async_remote_copy(
+            src_ref=send.at[d],
+            dst_ref=recv.at[q],
+            send_sem=send_sem,
+            recv_sem=recv_sem,
+            device_id=device_of(zh, d),
+            device_id_type=pl.DeviceIdType.MESH,
+        ).start()
+        return carry
+
+    lax.fori_loop(1, RANKS, push, 0)
+    pltpu.make_async_copy(send, recv, recv_sem).wait()
+    rest = pl.ds(0, RANKS - 1)
+    pltpu.make_async_copy(send.at[rest], recv.at[rest], send_sem).wait()
+
+
+def nn(a, b):
+    return lax.dot_general(a, b, (((1,), (0,)), ((), ())), preferred_element_type=F32)
+
+
+def nt(a, b):
+    return lax.dot_general(a, b, (((1,), (1,)), ((), ())), preferred_element_type=F32)
+
+
+def tn(a, b):
+    return lax.dot_general(a, b, (((0,), (0,)), ((), ())), preferred_element_type=F32)
+
+
+def piece_of(kind, half, zh, y):
+    return 2 - 2 * ((kind + zh) % 2) + (half + y) % 2
+
+
+def weight_of(w_ref, kind, t, part, zh, y):
+    return jnp.concatenate(
+        [w_ref[piece_of(kind, half, zh, y), t, part] for half in range(2)], axis=1
+    )
+
+
+def hi_rows(w):
+    slot = lax.broadcasted_iota(jnp.int32, (RANKS * 2 * SLOTS, 1), 0) % SLOTS
+    return slot < 6 - w
+
+
+GELU_A = math.sqrt(2.0 / math.pi)
+GELU_B = 0.044715
+
+
+def normal_of(hidden):
+    centre = jnp.mean(hidden, -1, keepdims=True)
+    centred = hidden - centre
+    inv_std = lax.rsqrt(jnp.mean(centred * centred, -1, keepdims=True) + norm_eps)
+    return centred * inv_std, inv_std
+
+
+def rows_loop(total, step, body):
+    def one(k, carry):
+        body(pl.ds(pl.multiple_of(k * step, step), step))
+        return carry
+
+    lax.fori_loop(0, total // step, one, 0)
+
+
+def block_fwd(h_ref, gain_ref, ftx, pfx, pix, itx, w_ref, w0, w1, h_out, v_low, a_own,
+              u_buf, s_send, s_recv, a_send, b_recv, send_sem, recv_sem):
+    zh, y, w, q = place()
+    enter(zh, q)
+    pixels, chans = h_ref.shape
+    gain = gain_ref[...]
+
+    def norm_rows(rows):
+        normal, unused = normal_of(h_ref[rows, :])
+        u_buf[rows, :] = (normal * gain).astype(BF16)
+
+    rows_loop(pixels, 128, norm_rows)
+    s_send[...] = nn(ftx[...], u_buf[...]).astype(BF16).reshape(s_send.shape)
+    exchange(s_send, s_recv, send_sem.at[0], recv_sem.at[0], zh, q)
+    a_send[...] = nn(pfx[...], s_recv[...].reshape(pix.shape[0], chans)).astype(BF16).reshape(a_send.shape)
+    exchange(a_send, a_own, send_sem.at[1], recv_sem.at[1], zh, q)
+    hi = hi_rows(w)
+    for t in range(3):
+        coef = a_own[:, t].reshape(RANKS * 2 * SLOTS, chans)
+
+        def times(part):
+            return jnp.where(
+                hi,
+                nn(coef, weight_of(w_ref, 0, t, part, zh, y)),
+                nn(coef, weight_of(w_ref, 1, t, part, zh, y)),
+            ).reshape(RANKS, 2, SLOTS, chans)
+
+        by_real, by_imag = times(0), times(1)
+        mixed = jnp.stack(
+            [by_real[:, 0] - by_imag[:, 1], by_real[:, 1] + by_imag[:, 0]], 1
+        )
+        a_send[:, t] = mixed.reshape(RANKS, 2 * SLOTS, chans).astype(BF16)
+    exchange(a_send, b_recv, send_sem.at[2], recv_sem.at[2], zh, q)
+    s_send[...] = nn(pix[...], b_recv[...].reshape(pfx.shape[0], chans)).astype(BF16).reshape(s_send.shape)
+    exchange(s_send, s_recv, send_sem.at[3], recv_sem.at[3], zh, q)
+    spectrum = s_recv[...].reshape(pix.shape[0], chans)
+
+    def mlp_rows(rows):
+        merged = h_ref[rows, :] + nn(itx[rows, :], spectrum)
+        merged_low = merged.astype(BF16)
+        v_low[rows, :] = merged_low
+        pre = nn(merged_low, w0[...])
+        act = (0.5 * pre * (1.0 + jnp.tanh(GELU_A * (pre + GELU_B * pre * pre * pre)))).astype(BF16)
+        h_out[rows, :] = merged + nt(act, w1[...])
+
+    rows_loop(pixels, 256, mlp_rows)
+
+
+def block_bwd(dh_ref, h_ref, v_low, a_own, gain_ref, itxt, pixt, pfxt, ftxt, w_ref, w0, w1,
+              dh_out, dw_out, dmlp, dgain,
+              dv_buf, dv_low, y_send, y_recv, b_send, b_recv, c_recv, send_sem, recv_sem):
+    zh, y, w, q = place()
+    enter(zh, q)
+    pixels, chans = h_ref.shape
+    gain = gain_ref[...]
+    dmlp[...] = jnp.zeros_like(dmlp)
+    dgain[...] = jnp.zeros_like(dgain)
+
+    def mlp_rows(rows):
+        d_hidden = dh_ref[rows, :]
+        d_branch = d_hidden.astype(BF16)
+        merged_low = v_low[rows, :]
+        pre = nn(merged_low, w0[...])
+        tan = jnp.tanh(GELU_A * (pre + GELU_B * pre * pre * pre))
+        act = (0.5 * pre * (1.0 + tan)).astype(BF16)
+        slope = 0.5 * (1.0 + tan) + 0.5 * pre * (1.0 - tan * tan) * (GELU_A * (1.0 + 3.0 * GELU_B * pre * pre))
+        d_pre = (nn(d_branch, w1[...]) * slope).astype(BF16)
+        dmlp[0] += tn(merged_low, d_pre)
+        dmlp[1] += tn(d_branch, act)
+        d_merged = d_hidden + nt(d_pre, w0[...])
+        dv_buf[rows, :] = d_merged
+        dv_low[rows, :] = d_merged.astype(BF16)
+
+    rows_loop(pixels, 256, mlp_rows)
+    y_send[...] = nn(itxt[...], dv_low[...]).astype(BF16).reshape(y_send.shape)
+    exchange(y_send, y_recv, send_sem.at[0], recv_sem.at[0], zh, q)
+    b_send[...] = nn(pixt[...], y_recv[...].reshape(itxt.shape[0], chans)).astype(BF16).reshape(b_send.shape)
+    exchange(b_send, b_recv, send_sem.at[1], recv_sem.at[1], zh, q)
+    hi = hi_rows(w)
+    for t in range(3):
+        rows = RANKS * 2 * SLOTS
+        d_mixed = b_recv[:, t].reshape(rows, chans)
+        wide = d_mixed.astype(F32).reshape(RANKS, 2, SLOTS, chans)
+        turned = jnp.stack([wide[:, 1], -wide[:, 0]], 1).reshape(rows, chans).astype(BF16)
+
+        def times(part):
+            return jnp.where(
+                hi,
+                nt(d_mixed, weight_of(w_ref, 0, t, part, zh, y)),
+                nt(d_mixed, weight_of(w_ref, 1, t, part, zh, y)),
+            ).reshape(RANKS, 2, SLOTS, chans)
+
+        by_real, by_imag = times(0), times(1)
+        d_coef = jnp.stack([by_real[:, 0] + by_imag[:, 1], by_real[:, 1] - by_imag[:, 0]], 1)
+        b_send[:, t] = d_coef.reshape(RANKS, 2 * SLOTS, chans).astype(BF16)
+        coef = a_own[:, t].reshape(rows, chans).astype(F32)
+        for kind in range(2):
+            keep = hi if kind == 0 else jnp.logical_not(hi)
+            kept = jnp.where(keep, coef, 0.0).astype(BF16)
+            for part, other in enumerate((d_mixed, turned)):
+                grad = tn(kept, other)
+                for half in range(2):
+                    width = chans // 2
+                    dw_out[piece_of(kind, half, zh, y), t, part] = grad[:, half * width : (half + 1) * width]
+    exchange(b_send, c_recv, send_sem.at[2], recv_sem.at[2], zh, q)
+    y_send[...] = nn(pfxt[...], c_recv[...].reshape(pixt.shape[0], chans)).astype(BF16).reshape(y_send.shape)
+    exchange(y_send, y_recv, send_sem.at[3], recv_sem.at[3], zh, q)
+    spectrum = y_recv[...].reshape(itxt.shape[0], chans)
+
+    def norm_rows(rows):
+        normal, inv_std = normal_of(h_ref[rows, :])
+        d_normed = nn(ftxt[rows, :], spectrum)
+        scaled = d_normed * gain
+        dgain[...] += jnp.sum(d_normed * normal, axis=0, keepdims=True)
+        d_norm_in = inv_std * (
+            scaled
+            - jnp.mean(scaled, -1, keepdims=True)
+            - normal * jnp.mean(scaled * normal, -1, keepdims=True)
+        )
+        dh_out[rows, :] = dv_buf[rows, :] + d_norm_in
+
+    rows_loop(pixels, 256, norm_rows)
+
+
+VMEM = pltpu.VMEM
+PARTS = (RANKS, 3, 2 * SLOTS)
+
+
+def call_fwd(hidden, gain, tables, pieces, mlp):
+    pixels, chans = hidden.shape
+    narrow = VMEM((RANKS, 4 * ORDS, chans), BF16)
+    wide = VMEM((*PARTS, chans), BF16)
+    return pl.pallas_call(
+        block_fwd,
+        out_shape=(
+            jax.ShapeDtypeStruct((pixels, chans), F32),
+            jax.ShapeDtypeStruct((pixels, chans), BF16),
+            jax.ShapeDtypeStruct((*PARTS, chans), BF16),
+        ),
+        in_specs=[pl.BlockSpec(memory_space=VMEM)] * 9,
+        out_specs=[pl.BlockSpec(memory_space=VMEM)] * 3,
+        scratch_shapes=[
+            VMEM((pixels, chans), BF16),
+            narrow,
+            narrow,
+            wide,
+            wide,
+            pltpu.SemaphoreType.DMA((4,)),
+            pltpu.SemaphoreType.DMA((4,)),
+        ],
+        compiler_params=pltpu.CompilerParams(
+            collective_id=0, has_side_effects=True, vmem_limit_bytes=48 << 20
+        ),
+    )(hidden, gain[None], *tables, pieces, mlp[0], mlp[1])
+
+
+def call_bwd(d_hidden, hidden, merged_low, owned, gain, tables, pieces, mlp):
+    pixels, chans = hidden.shape
+    narrow = VMEM((RANKS, 4 * ORDS, chans), BF16)
+    wide = VMEM((*PARTS, chans), BF16)
+    return pl.pallas_call(
+        block_bwd,
+        out_shape=(
+            jax.ShapeDtypeStruct((pixels, chans), F32),
+            jax.ShapeDtypeStruct(pieces.shape, F32),
+            jax.ShapeDtypeStruct(mlp.shape, F32),
+            jax.ShapeDtypeStruct((1, chans), F32),
+        ),
+        in_specs=[pl.BlockSpec(memory_space=VMEM)] * 12,
+        out_specs=[pl.BlockSpec(memory_space=VMEM)] * 4,
+        scratch_shapes=[
+            VMEM((pixels, chans), F32),
+            VMEM((pixels, chans), BF16),
+            narrow,
+            narrow,
+            wide,
+            wide,
+            wide,
+            pltpu.SemaphoreType.DMA((4,)),
+            pltpu.SemaphoreType.DMA((4,)),
+        ],
+        compiler_params=pltpu.CompilerParams(
+            collective_id=1, has_side_effects=True, vmem_limit_bytes=48 << 20
+        ),
+    )(d_hidden, hidden, merged_low, owned, gain[None], *tables, pieces, mlp[0], mlp[1])
+
+
+def regroup(field):
+    extra = field.shape[3:]
+    items, lon, lat = field.shape[:3]
+    pairs = lat // 2
+    chunks = jnp.moveaxis(field.reshape(items, lon, pairs, 2, *extra), 1, 3)
+    chunks = jnp.concatenate([chunks[0], jnp.roll(chunks[1], pairs // 2, 0)], 0)
+    swapped = lax.all_to_all(chunks, "ma", split_axis=0, concat_axis=0, tiled=True)
+    return jnp.moveaxis(swapped, 1, 0).reshape(2 * lon * lax.axis_size("ma"), *extra)
+
+
+def partners(kind):
+    pairs = []
+    for y in range(2):
+        for ma in range(16):
+            other_y = 1 - y if kind in (1, 3) else y
+            other_ma = 4 * (3 - ma // 4) + ma % 4 if kind in (2, 3) else ma
+            pairs.append((16 * y + ma, 16 * other_y + other_ma))
+    return pairs
+
+
+def send_to(kind, array):
+    return lax.ppermute(array, ("lat", "ma"), partners(kind))
+
+
+def special(
+    inputs,
+    targets,
+    mask,
+    var_weight,
+    step_count,
+    spec_w,
+    spec_m,
+    spec_v,
+    encdec_w,
+    encdec_m,
+    encdec_v,
+    mlp_w,
+    mlp_m,
+    mlp_v,
+    gain_w,
+    gain_m,
+    gain_v,
+):
+    zh, y, w, q = place()
+    batch = inputs.shape[0]
+    nlon = inputs.shape[1] * lax.axis_size("ma")
+    nlat = inputs.shape[2] * lax.axis_size("lat")
+    fwd_leg, inv_leg, fwd_four, inv_four = make_tables(nlat, nlon)
+    pfx = lax.dynamic_index_in_dim(jnp.asarray(fwd_leg), q, 0, keepdims=False)
+    pix = lax.dynamic_index_in_dim(jnp.asarray(inv_leg), q, 0, keepdims=False)
+    ftx, itx = jnp.asarray(fwd_four), jnp.asarray(inv_four)
+    fwd_tables = (ftx, pfx, pix, itx)
+    bwd_tables = (itx.T, pix.T, pfx.T, ftx.T)
+    denom = float(batch * nlon * nlat * C)
+
+    encdec_bf = encdec_w.astype(BF16)
+    mlp_bf = mlp_w.astype(BF16)
+    state = regroup(inputs)
+
+    third = spec_w.shape[1] // 2
+    low = spec_w.astype(BF16)
+    pieces = []
+    for block in range(NB):
+        mine = lax.dynamic_slice_in_dim(low[block], third * y, third, 0)
+        other = lax.dynamic_slice_in_dim(low[block], third * (1 - y), third, 0)
+        pieces.append(
+            jnp.stack([mine, send_to(1, other), send_to(2, mine), send_to(3, other)], 0)
+        )
+
+    angles = (jnp.arange(nlat, dtype=F32) + 0.5) * (math.pi / nlat)
+    sines = jnp.sin(angles)
+    area = lax.dynamic_slice_in_dim(sines / jnp.mean(sines), 2 * q, 2)
+    rest = jnp.concatenate(
+        [targets[0], targets[1], mask.astype(F32)[..., None]], -1
+    )
+    rest = regroup(rest)
+    goals = (rest[:, :C], rest[:, C : 2 * C])
+    pixel_weight = (
+        jnp.repeat(area, nlon)[:, None] * rest[:, 2 * C :] * var_weight.astype(F32)[None, :]
+    )
+
+    kept = []
+    loss_part = jnp.zeros((), F32)
+    for step in range(ROLL):
+        state_low = state.astype(BF16)
+        hidden = nn(state_low, encdec_bf[0])
+        records = []
+        for block in range(NB):
+            out, merged_low, owned = call_fwd(hidden, gain_w[block], fwd_tables, pieces[block], mlp_bf[block])
+            records.append((hidden, merged_low, owned))
+            hidden = out
+        hidden_low = hidden.astype(BF16)
+        state = state + nt(hidden_low, encdec_bf[1])
+        misfit = state - goals[step]
+        loss_part = loss_part + jnp.sum(pixel_weight * misfit * misfit) / denom
+        kept.append((state_low, hidden_low, records, misfit))
+
+    spec_sum = [None] * NB
+    mlp_sum = [None] * NB
+    gain_sum = [None] * NB
+    encdec_sum = None
+    d_state = None
+
+    def plus(total, term):
+        return term if total is None else total + term
+
+    for step in reversed(range(ROLL)):
+        state_low, hidden_low, records, misfit = kept[step]
+        d_pred = plus(d_state, 2.0 * pixel_weight * misfit / denom)
+        d_dec = d_pred.astype(BF16)
+        grad_dec = tn(d_dec, hidden_low)
+        d_hidden = nn(d_dec, encdec_bf[1])
+        for block in reversed(range(NB)):
+            hidden, merged_low, owned = records[block]
+            d_hidden, dw, dmlp, dgain = call_bwd(
+                d_hidden, hidden, merged_low, owned, gain_w[block], bwd_tables, pieces[block], mlp_bf[block]
+            )
+            spec_sum[block] = plus(spec_sum[block], dw)
+            mlp_sum[block] = plus(mlp_sum[block], dmlp)
+            gain_sum[block] = plus(gain_sum[block], dgain[0])
+        d_enc = d_hidden.astype(BF16)
+        encdec_sum = plus(encdec_sum, jnp.stack([tn(state_low, d_enc), grad_dec], 0))
+        if step:
+            d_state = d_pred + nt(d_enc, encdec_bf[0])
+
+    spec_grad = []
+    for block in range(NB):
+        total = spec_sum[block]
+        sent = total[1:].astype(BF16)
+        near, far, cross = send_to(1, sent[0]), send_to(2, sent[1]), send_to(3, sent[2])
+        same = total[0] + far.astype(F32)
+        other = near.astype(F32) + cross.astype(F32)
+        spec_grad.append(jnp.where(y == 0, jnp.concatenate([same, other], 0), jnp.concatenate([other, same], 0)))
+    spec_grad = jnp.stack(spec_grad, 0)
+    grad_encdec, grad_mlp, grad_gain, loss_value, spec_square, weight_square = lax.psum(
+        (
+            encdec_sum,
+            jnp.stack(mlp_sum, 0),
+            jnp.stack(gain_sum, 0),
+            loss_part,
+            jnp.sum(spec_grad * spec_grad),
+            jnp.sum(spec_w * spec_w, axis=(1, 2, 3, 4)),
+        ),
+        ("lat", "ma"),
+    )
+    total_square = (
+        spec_square
+        + jnp.sum(grad_encdec * grad_encdec)
+        + jnp.sum(grad_mlp * grad_mlp)
+        + jnp.sum(grad_gain * grad_gain)
+    )
+    grad_norm = jnp.sqrt(total_square)
+    scale = clip_norm / jnp.maximum(grad_norm, clip_norm)
+    step_float = step_count[0].astype(jnp.float32)
+    spec_m_new, spec_v_new, direction = adaptive(
+        spec_w, spec_m, spec_v, spec_grad * scale, step_float
+    )
+    dir_square = lax.psum(jnp.sum(direction * direction, axis=(1, 2, 3, 4)), ("lat", "ma"))
+    weight_norm = jnp.sqrt(weight_square)
+    dir_norm = jnp.sqrt(dir_square)
+    trust = weight_norm / (dir_norm + 1e-06)
+    spec_new = spec_w - learn_rate * trust[:, None, None, None, None] * direction
+    encdec_new, encdec_m_new, encdec_v_new, encdec_norms = lamb_dense(
+        encdec_w, encdec_m, encdec_v, grad_encdec * scale, step_float, 2
+    )
+    mlp_new, mlp_m_new, mlp_v_new, mlp_norms = lamb_dense(
+        mlp_w, mlp_m, mlp_v, grad_mlp * scale, step_float, 2 * NB
+    )
+    gain_new, gain_m_new, gain_v_new, gain_norms = lamb_dense(
+        gain_w, gain_m, gain_v, grad_gain * scale, step_float, NB
+    )
+    matrix_norms = jnp.concatenate(
+        [jnp.stack([weight_norm, dir_norm], 1), encdec_norms, mlp_norms, gain_norms], 0
+    )
+    return (
+        loss_value,
+        grad_norm,
+        matrix_norms,
+        spec_new,
+        spec_m_new,
+        spec_v_new,
+        spec_new.astype(jnp.bfloat16),
+        encdec_new,
+        encdec_m_new,
+        encdec_v_new,
+        encdec_new.astype(jnp.bfloat16),
+        mlp_new,
+        mlp_m_new,
+        mlp_v_new,
+        mlp_new.astype(jnp.bfloat16),
+        gain_new,
+        gain_m_new,
+        gain_v_new,
+        gain_new.astype(jnp.bfloat16),
+    )
+
+
+def local(mesh, *args):
+    inputs, spec_w = args[0], args[5]
+    lat = inputs.shape[2] * mesh.shape["lat"]
+    fits = (
+        dict(mesh.shape) == {"lat": 2, "ma": RANKS}
+        and inputs.shape[0] == 2
+        and lat == 2 * RANKS
+        and spec_w.shape[1] * RANKS == L
+    )
+    return (special if fits else general)(*args)
+
+
 def solution(mesh):
     placed = (
         P(None, "ma", "lat", None),
@@ -438,7 +1018,7 @@
         P(),
     )
     return jax.shard_map(
-        local,
+        functools.partial(local, mesh),
         mesh=mesh,
         in_specs=placed,
         out_specs=(

time: 3970 us -> 871 us (0.22)
  local copies, waits for them, and re-layouts: 1490 us -> 46 us
  blocking collectives: 1210 us -> 142 us
  Pallas kernels: 0 us -> 392 us
  waiting for transfers between devices: 406 us -> 79.2 us
  loops' own time: 315 us -> 0 us
  other arithmetic: 258 us -> 85.8 us
  matrix products: 135 us -> 9.02 us
    all_to_all x64 -> x0, blocking collectives: 1090 us -> none  [the longest x19 284 us: apply_table(): lax.all_to_all(block_in, 'ma', split_axis=3, concat_axis=0, tiled=True)]
    unnamed x597 -> x213, local copies, waits for them, and re-layouts: 694 us -> 25.4 us
    convert_element_type x87 -> x1, local copies, waits for them, and re-layouts: 396 us -> 0.7 us  [special(): state_low = state.astype(BF16)]
    pallas_call x0 -> x12, Pallas kernels: none -> 392 us  [the longest x6 203 us: call_bwd(): pl.pallas_call(block_bwd, out_shape=(jax.ShapeDtypeStruct((pixels, chans)...]
    another operation x1 -> x0, loops' own time: 315 us -> none  [legendre(): lax.scan(advance, (zero_rows, zero_rows), jnp.arange(L, dtype=jnp.float32))]
    all_to_all x90 -> x0, local copies, waits for them, and re-layouts: 293 us -> none  [the longest x24 137 us: apply_table(): lax.all_to_all(block_in, 'ma', split_axis=3, concat_axis=0, tiled=True)]
    all_to_all x20 -> x2, waiting for transfers between devices: 176 us -> 0.01 us  [regroup(): lax.all_to_all(chunks, 'ma', split_axis=0, concat_axis=0, tiled=True)]
    unnamed x13 -> x1, waiting for transfers between devices: 143 us -> 0.02 us
  transfers between devices with their start and end apart: 27 -> 21, of which waited for: 26 -> 8; matrix products, arithmetic and copies ran while one was open for 7% -> 6% of each run, Pallas kernels for 0% -> 22%
where the time goes in v1:
time: 871 us; the launch traced here: 864 us
  Pallas kernels  392 us (45%)
  blocking collectives  142 us (16%)
  starting transfers between devices  88 us (10%)
  other arithmetic  85.8 us (10%)
  waiting for transfers between devices  79.2 us (9%)
  local copies, waits for them, and re-layouts  46 us (5%)
  between operations  22.1 us (3%)
  matrix products  9.02 us (1%)
    pallas_call x6, Pallas kernels, call_bwd(): pl.pallas_call(block_bwd, out_shape=(jax.ShapeDtypeStruct((pixels, chans)...  203 us
    pallas_call x6, Pallas kernels, call_fwd(): pl.pallas_call(block_fwd, out_shape=(jax.ShapeDtypeStruct((pixels, chans)...  188 us
    psum x2, blocking collectives, special(): lax.psum((encdec_sum, jnp.stack(mlp_sum, 0), jnp.stack(gain_sum, 0), loss...  142 us
    ppermute x18, waiting for transfers between devices, send_to(): return lax.ppermute(array, ('lat', 'ma'), partners(kind))  51.8 us
    all_to_all x2, starting transfers between devices, regroup(): lax.all_to_all(chunks, 'ma', split_axis=0, concat_axis=0, tiled=True)  51.5 us
    ppermute x18, starting transfers between devices, send_to(): return lax.ppermute(array, ('lat', 'ma'), partners(kind))  36.5 us
    psum x1, waiting for transfers between devices, special(): lax.psum((encdec_sum, jnp.stack(mlp_sum, 0), jnp.stack(gain_sum, 0), loss...  27.4 us
    unnamed x213, local copies, waits for them, and re-layouts  25.4 us
  transfers between devices with their start and end apart: 21, of which 8 were waited for; matrix products, arithmetic and copies ran while one was open for 6% of the time, Pallas kernels for 22%

profile of v1, /device:TPU:0, one launch (start us, length us, event | category | flops | bytes accessed | tf_op | source)
XLA Modules:
  0.0 863.9 jit_solution(17979422810655534206)
XLA Ops:
  7.2 5.3 multiply_reduce_fusion.1
  13.6 6.0 collective-permute-start.8
  21.1 4.2 all-to-all-start.1
  25.3 3.6 collective-permute-start.7
  30.1 4.5 collective-permute-start.5
  41.8 5.1 multiply_reduce_fusion.4
  63.4 16.3 %collective-permute-done.3 = bf16[3,2,256,128]{3,2,1,0:T(8,128)(2,1)S(1)} collective-permute-done((bf16[3,2,256,128]{3,2,1,0:T(8,128)(2,1)}, bf16[3,2,256,128]{3,2,1,0:T(8,128)(2,1)S(1)}, u32[]{:S(2)}, u32[]{:S(2)}) %collective-permute-start.3) | collective-permute-done | bytes 393248 | tf_op jit(solution)/shard_map/ppermute | solution.py:812
  82.2 5.8 collective-permute-done
  89.3 47.2 %all-to-all-start = ((f32[16,2,24,147]{3,2,1,0:T(8,128)}), f32[16,2,24,147]{3,2,1,0:T(8,128)}, u32[]{:S(2)}, u32[]{:S(2)}) async-start(f32[16,2,24,147]{3,2,1,0:T(8,128)} %pad_maximum_fusion.5), calls=%async_computation | async-start | bytes 1572864 | tf_op jit(solution)/shard_map/all_to_all | solution.py:797
  145.3 33.4 %shard_map.348 = (f32[768,256]{1,0:T(8,128)S(1)}, bf16[768,256]{1,0:T(8,128)(2,1)S(1)}, bf16[16,3,16,256]{3,2,1,0:T(8,128)(2,1)S(1)}) custom-call(f32[768,256]{1,0:T(8,128)S(1)} %fusion.33.h_ref, f32[1,256]{1,0:T(1,128)S(1)} %get-tuple-element.280.gain_ref, bf16[384,768]{1,0:T(8,128)(2,1)S(1)} %copy-done.3, bf16[768,384]{1,0:T(8,128)(2,1)S(1)} %copy.161.pfx, ...), custom_call_target="tpu_custom_call" | custom-call | tf_op jit(solution)/shard_map/pallas_call | solution.py:736
  179.6 30.9 %shard_map.349 = (f32[768,256]{1,0:T(8,128)S(1)}, bf16[768,256]{1,0:T(8,128)(2,1)S(1)}, bf16[16,3,16,256]{3,2,1,0:T(8,128)(2,1)S(1)}) custom-call(f32[768,256]{1,0:T(8,128)S(1)} %get-tuple-element.61.h_ref, f32[1,256]{1,0:T(1,128)S(1)} %get-tuple-element.279.gain_ref, bf16[384,768]{1,0:T(8,128)(2,1)S(1)} %copy-done.3, bf16[768,384]{1,0:T(8,128)(2,1)S(1)} %copy.161.pfx, ...), custom_call_target="tpu_custom_call" | custom-call | tf_op jit(solution)/shard_map/pallas_call | solution.py:736
  212.1 31.4 %shard_map.350 = (f32[768,256]{1,0:T(8,128)S(1)}, bf16[768,256]{1,0:T(8,128)(2,1)S(1)}, bf16[16,3,16,256]{3,2,1,0:T(8,128)(2,1)S(1)}) custom-call(f32[768,256]{1,0:T(8,128)S(1)} %get-tuple-element.62.h_ref, f32[1,256]{1,0:T(1,128)S(1)} %get-tuple-element.278.gain_ref, bf16[384,768]{1,0:T(8,128)(2,1)S(1)} %copy-done.3, bf16[768,384]{1,0:T(8,128)(2,1)S(1)} %copy.161.pfx, ...), custom_call_target="tpu_custom_call" | custom-call | tf_op jit(solution)/shard_map/pallas_call | solution.py:736
  245.0 30.7 %shard_map.351 = (f32[768,256]{1,0:T(8,128)S(1)}, bf16[768,256]{1,0:T(8,128)(2,1)S(1)}, bf16[16,3,16,256]{3,2,1,0:T(8,128)(2,1)S(1)}) custom-call(f32[768,256]{1,0:T(8,128)S(1)} %fusion.31.h_ref, f32[1,256]{1,0:T(1,128)S(1)} %get-tuple-element.280.gain_ref, bf16[384,768]{1,0:T(8,128)(2,1)S(1)} %copy-done.3, bf16[768,384]{1,0:T(8,128)(2,1)S(1)} %copy.161.pfx, ...), custom_call_target="tpu_custom_call" | custom-call | tf_op jit(solution)/shard_map/pallas_call | solution.py:736
  278.1 31.0 %shard_map.352 = (f32[768,256]{1,0:T(8,128)S(1)}, bf16[768,256]{1,0:T(8,128)(2,1)S(1)}, bf16[16,3,16,256]{3,2,1,0:T(8,128)(2,1)S(1)}) custom-call(f32[768,256]{1,0:T(8,128)S(1)} %get-tuple-element.64.h_ref, f32[1,256]{1,0:T(1,128)S(1)} %get-tuple-element.279.gain_ref, bf16[384,768]{1,0:T(8,128)(2,1)S(1)} %copy-done.3, bf16[768,384]{1,0:T(8,128)(2,1)S(1)} %copy.161.pfx, ...), custom_call_target="tpu_custom_call" | custom-call | tf_op jit(solution)/shard_map/pallas_call | solution.py:736
  310.6 30.8 %shard_map.353 = (f32[768,256]{1,0:T(8,128)S(1)}, bf16[768,256]{1,0:T(8,128)(2,1)S(1)}, bf16[16,3,16,256]{3,2,1,0:T(8,128)(2,1)S(1)}) custom-call(f32[768,256]{1,0:T(8,128)S(1)} %get-tuple-element.65.h_ref, f32[1,256]{1,0:T(1,128)S(1)} %get-tuple-element.278.gain_ref, bf16[384,768]{1,0:T(8,128)(2,1)S(1)} %copy-done.3, bf16[768,384]{1,0:T(8,128)(2,1)S(1)} %copy.161.pfx, ...), custom_call_target="tpu_custom_call" | custom-call | tf_op jit(solution)/shard_map/pallas_call | solution.py:736
  359.3 34.0 %shard_map.354 = (f32[768,256]{1,0:T(8,128)S(1)}, f32[4,3,2,256,128]{4,3,2,1,0:T(8,128)}, f32[2,256,512]{2,1,0:T(8,128)}, f32[1,256]{1,0:T(1,128)S(1)}) custom-call(f32[768,256]{1,0:T(8,128)S(1)} %fusion.35.dh_ref, f32[768,256]{1,0:T(8,128)S(1)} %copy-done.31, bf16[768,256]{1,0:T(8,128)(2,1)S(1)} %copy-done.53, bf16[16,3,16,256]{3,2,1,0:T(8,128)(2,1)S(1)} %copy-done.55, ...), custom_call_target="tpu_custom_call" | custom-call | tf_op jit(solution)/shard_map/pallas_call | solution.py:764
  393.4 33.9 %shard_map.355 = (f32[768,256]{1,0:T(8,128)S(1)}, f32[4,3,2,256,128]{4,3,2,1,0:T(8,128)}, f32[2,256,512]{2,1,0:T(8,128)}, f32[1,256]{1,0:T(1,128)S(1)}) custom-call(f32[768,256]{1,0:T(8,128)S(1)} %get-tuple-element.69.dh_ref, f32[768,256]{1,0:T(8,128)S(1)} %copy-done.29, bf16[768,256]{1,0:T(8,128)(2,1)S(1)} %copy-done.49, ...), custom_call_target="tpu_custom_call" | custom-call | tf_op jit(solution)/shard_map/pallas_call | solution.py:764
  427.3 33.9 %shard_map.356 = (f32[768,256]{1,0:T(8,128)S(1)}, f32[4,3,2,256,128]{4,3,2,1,0:T(8,128)}, f32[2,256,512]{2,1,0:T(8,128)}, f32[1,256]{1,0:T(1,128)S(1)}) custom-call(f32[768,256]{1,0:T(8,128)S(1)} %get-tuple-element.72.dh_ref, f32[768,256]{1,0:T(8,128)S(1)} %copy-done.7, bf16[768,256]{1,0:T(8,128)(2,1)S(1)} %copy-done.45, ...), custom_call_target="tpu_custom_call" | custom-call | tf_op jit(solution)/shard_map/pallas_call | solution.py:764
  462.7 33.9 %shard_map.357 = (f32[768,256]{1,0:T(8,128)S(1)}, f32[4,3,2,256,128]{4,3,2,1,0:T(8,128)}, f32[2,256,512]{2,1,0:T(8,128)}, f32[1,256]{1,0:T(1,128)S(1)}) custom-call(f32[768,256]{1,0:T(8,128)S(1)} %fusion.34.dh_ref, f32[768,256]{1,0:T(8,128)S(1)} %copy-done.27, bf16[768,256]{1,0:T(8,128)(2,1)S(1)} %copy-done.41, bf16[16,3,16,256]{3,2,1,0:T(8,128)(2,1)S(1)} %copy-done.43, ...), custom_call_target="tpu_custom_call" | custom-call | tf_op jit(solution)/shard_map/pallas_call | solution.py:764
  496.7 33.9 %shard_map.358 = (f32[768,256]{1,0:T(8,128)S(1)}, f32[4,3,2,256,128]{4,3,2,1,0:T(8,128)}, f32[2,256,512]{2,1,0:T(8,128)}, f32[1,256]{1,0:T(1,128)S(1)}) custom-call(f32[768,256]{1,0:T(8,128)S(1)} %get-tuple-element.79.dh_ref, f32[768,256]{1,0:T(8,128)S(1)} %copy-done.25, bf16[768,256]{1,0:T(8,128)(2,1)S(1)} %copy-done.37, ...), custom_call_target="tpu_custom_call" | custom-call | tf_op jit(solution)/shard_map/pallas_call | solution.py:764
  530.6 33.9 %shard_map.359 = (f32[768,256]{1,0:T(8,128)S(1)}, f32[4,3,2,256,128]{4,3,2,1,0:T(8,128)}, f32[2,256,512]{2,1,0:T(8,128)}, f32[1,256]{1,0:T(1,128)S(1)}) custom-call(f32[768,256]{1,0:T(8,128)S(1)} %get-tuple-element.82.dh_ref, f32[768,256]{1,0:T(8,128)S(1)} %copy-done.5, bf16[768,256]{1,0:T(8,128)(2,1)S(1)} %copy-done.33, ...), custom_call_target="tpu_custom_call" | custom-call | tf_op jit(solution)/shard_map/pallas_call | solution.py:764
  564.5 4.3 fusion.53
  603.4 10.1 %collective-permute-done.14 = bf16[3,2,256,128]{3,2,1,0:T(8,128)(2,1)} collective-permute-done((bf16[3,2,256,128]{3,2,1,0:T(8,128)(2,1)S(1)}, bf16[3,2,256,128]{3,2,1,0:T(8,128)(2,1)}, u32[]{:S(2)}, u32[]{:S(2)}) %collective-permute-start.14) | collective-permute-done | bytes 393248 | tf_op jit(solution)/shard_map/ppermute | solution.py:812
  613.5 4.3 collective-permute-done.13
  619.0 14.5 %collective-permute-done.17 = bf16[3,2,256,128]{3,2,1,0:T(8,128)(2,1)S(1)} collective-permute-done((bf16[3,2,256,128]{3,2,1,0:T(8,128)(2,1)S(1)}, bf16[3,2,256,128]{3,2,1,0:T(8,128)(2,1)S(1)}, u32[]{:S(2)}, u32[]{:S(2)}) %collective-permute-start.17) | collective-permute-done | bytes 393248 | tf_op jit(solution)/shard_map/ppermute | solution.py:812
  638.0 102.4 %all-reduce.1 = (f32[]{:T(128)}, f32[3,256]{1,0:T(4,128)S(1)}) all-reduce(f32[]{:T(128)} %multiply_reduce_fusion.2, f32[3,256]{1,0:T(4,128)S(1)} %pad_maximum_fusion.7), channel_id=1, replica_groups=mesh['lat'=2,'ma'=16] {'lat','ma'}, use_global_device_ids=true, to_apply=%region_5.6 | all-reduce | flops 769 | bytes 6152 | tf_op jit(solution)/shard_map/psum | solution.py:925
  741.0 27.4 %all-reduce.5.cloned.1.call-done = (f32[2,73,256]{2,1,0:T(8,128)}, f32[3,2,256,512]{3,2,1,0:T(8,128)}) async-done(((f32[2,73,256]{2,1,0:T(8,128)}, f32[3,2,256,512]{3,2,1,0:T(8,128)}), (f32[2,73,256]{2,1,0:T(8,128)}, f32[3,2,256,512]{3,2,1,0:T(8,128)})) %all-reduce.5.cloned.1.call-update) | async-done | bytes 3295248 | tf_op jit(solution)/shard_map/psum | solution.py:925
  780.4 8.2 multiply_reduce_fusion.3
  790.3 5.4 fusion.45
  796.6 10.6 %multiply_reduce_fusion = (f32[3]{0:T(128)S(1)}, f32[3,6,2,256,128]{4,3,2,1,0:T(8,128)}, f32[3,6,2,256,128]{4,3,2,1,0:T(8,128)}, f32[3,6,2,256,128]{4,3,2,1,0:T(8,128)}) fusion(f32[3,6,2,256,128]{4,3,2,1,0:T(8,128)S(1)} %bitcast.164, f32[]{:T(128)} %bitcast.74, f32[]{:T(128)} %bitcast.73, f32[]{:T(128)S(6)} %div.128, ...), kind=kLoop, calls=%fused_computation.5 | loop fusion | flops 21233660 | bytes 33030168 | tf_op jit(solution)/shard_map/reduce_sum | solution.py:948
  807.2 39.8 %all-reduce = (f32[]{:T(128)}, f32[3]{0:T(128)S(1)}, f32[3]{0:T(128)S(1)}) all-reduce(f32[]{:T(128)S(6)} %multiply.21, f32[3]{0:T(128)S(1)} %get-tuple-element.227, f32[3]{0:T(128)S(1)} %copy-done.97), channel_id=1, replica_groups=mesh['lat'=2,'ma'=16] {'lat','ma'}, use_global_device_ids=true, to_apply=%region_3.4 | all-reduce | flops 7 | bytes 56 | tf_op jit(solution)/shard_map/psum | solution.py:925
  847.0 8.1 fusion.47
  (332 shorter events, 117.2 us)
Async XLA Ops:
  13.6 40.7 %collective-permute-start.8 = (bf16[3,2,256,128]{3,2,1,0:T(8,128)(2,1)}, bf16[3,2,256,128]{3,2,1,0:T(8,128)(2,1)}, u32[]{:S(2)}, u32[]{:S(2)}) collective-permute-start(bf16[3,2,256,128]{3,2,1,0:T(8,128)(2,1)} %get-tuple-element.266), channel_id=1, source_target_pairs={{0,28},{1,29},{2,30},{3,31},{4,24},{5,25},{6,26},{7,27},{8,20},{9,... | collective-permute-start | bytes 1179656 | tf_op jit(solution)/shard_map/ppermute | solution.py:812
  19.6 35.9 %collective-permute-start.6 = (bf16[3,2,256,128]{3,2,1,0:T(8,128)(2,1)}, bf16[3,2,256,128]{3,2,1,0:T(8,128)(2,1)}, u32[]{:S(2)}, u32[]{:S(2)}) collective-permute-start(bf16[3,2,256,128]{3,2,1,0:T(8,128)(2,1)} %get-tuple-element.266), channel_id=1, source_target_pairs={{0,16},{1,17},{2,18},{3,19},{4,20},{5,21},{6,22},{7,23},{8,24},{9,... | collective-permute-start | bytes 1179656 | tf_op jit(solution)/shard_map/ppermute | solution.py:812
  21.1 68.3 %all-to-all-start.1 = ((f32[16,2,24,73]{3,2,1,0:T(8,128)}), f32[16,2,24,73]{3,2,1,0:T(8,128)}, u32[]{:S(2)}, u32[]{:S(2)}) async-start(f32[16,2,24,73]{3,2,1,0:T(8,128)} %pad_maximum_fusion.6), calls=%async_computation.1 | async-start | bytes 786432 | tf_op jit(solution)/shard_map/all_to_all | solution.py:797
  25.3 28.4 %collective-permute-start.7 = (bf16[3,2,256,128]{3,2,1,0:T(8,128)(2,1)}, bf16[3,2,256,128]{3,2,1,0:T(8,128)(2,1)}, u32[]{:S(2)}, u32[]{:S(2)}) collective-permute-start(bf16[3,2,256,128]{3,2,1,0:T(8,128)(2,1)} %bitcast.37), channel_id=1, source_target_pairs={{0,12},{1,13},{2,14},{3,15},{4,8},{5,9},{6,10},{7,11},{8,4},{9,5},... | collective-permute-start | bytes 1179656 | tf_op jit(solution)/shard_map/ppermute | solution.py:812
  29.8 26.2 %collective-permute-start.4 = (bf16[3,2,256,128]{3,2,1,0:T(8,128)(2,1)}, bf16[3,2,256,128]{3,2,1,0:T(8,128)(2,1)}, u32[]{:S(2)}, u32[]{:S(2)}) collective-permute-start(bf16[3,2,256,128]{3,2,1,0:T(8,128)(2,1)} %bitcast.30), channel_id=1, source_target_pairs={{0,12},{1,13},{2,14},{3,15},{4,8},{5,9},{6,10},{7,11},{8,4},{9,5},... | collective-permute-start | bytes 1179656 | tf_op jit(solution)/shard_map/ppermute | solution.py:812
  30.1 33.3 %collective-permute-start.5 = (bf16[3,2,256,128]{3,2,1,0:T(8,128)(2,1)}, bf16[3,2,256,128]{3,2,1,0:T(8,128)(2,1)}, u32[]{:S(2)}, u32[]{:S(2)}) collective-permute-start(bf16[3,2,256,128]{3,2,1,0:T(8,128)(2,1)} %get-tuple-element.268), channel_id=1, source_target_pairs={{0,28},{1,29},{2,30},{3,31},{4,24},{5,25},{6,26},{7,27},{8,20},{9,... | collective-permute-start | bytes 1179656 | tf_op jit(solution)/shard_map/ppermute | solution.py:812
  53.7 26.0 %collective-permute-start.3 = (bf16[3,2,256,128]{3,2,1,0:T(8,128)(2,1)}, bf16[3,2,256,128]{3,2,1,0:T(8,128)(2,1)S(1)}, u32[]{:S(2)}, u32[]{:S(2)}) collective-permute-start(bf16[3,2,256,128]{3,2,1,0:T(8,128)(2,1)} %get-tuple-element.268), channel_id=1, source_target_pairs={{0,16},{1,17},{2,18},{3,19},{4,20},{5,21},{6,22},{7,23},{8,24},{9,... | collective-permute-start | bytes 1179656 | tf_op jit(solution)/shard_map/ppermute | solution.py:812
  54.3 28.0 %collective-permute-start.2 = (bf16[3,2,256,128]{3,2,1,0:T(8,128)(2,1)S(1)}, bf16[3,2,256,128]{3,2,1,0:T(8,128)(2,1)S(1)}, u32[]{:S(2)}, u32[]{:S(2)}) collective-permute-start(bf16[3,2,256,128]{3,2,1,0:T(8,128)(2,1)S(1)} %get-tuple-element.270), channel_id=1, source_target_pairs={{0,28},{1,29},{2,30},{3,31},{4,24},{5,25},{6,26},{7,27},{8,20},{9,... | collective-permute-start | bytes 1179656 | tf_op jit(solution)/shard_map/ppermute | solution.py:812
  55.6 32.4 %collective-permute-start = (bf16[3,2,256,128]{3,2,1,0:T(8,128)(2,1)S(1)}, bf16[3,2,256,128]{3,2,1,0:T(8,128)(2,1)S(1)}, u32[]{:S(2)}, u32[]{:S(2)}) collective-permute-start(bf16[3,2,256,128]{3,2,1,0:T(8,128)(2,1)S(1)} %get-tuple-element.270), channel_id=1, source_target_pairs={{0,16},{1,17},{2,18},{3,19},{4,20},{5,21},{6,22},{7,23},{8,24},{9,... | collective-permute-start | bytes 1179656 | tf_op jit(solution)/shard_map/ppermute | solution.py:812
  56.1 26.2 %collective-permute-start.1 = (bf16[3,2,256,128]{3,2,1,0:T(8,128)(2,1)S(1)}, bf16[3,2,256,128]{3,2,1,0:T(8,128)(2,1)S(1)}, u32[]{:S(2)}, u32[]{:S(2)}) collective-permute-start(bf16[3,2,256,128]{3,2,1,0:T(8,128)(2,1)S(1)} %bitcast.169), channel_id=1, source_target_pairs={{0,12},{1,13},{2,14},{3,15},{4,8},{5,9},{6,10},{7,11},{8,4},{9,5},... | collective-permute-start | bytes 1179656 | tf_op jit(solution)/shard_map/ppermute | solution.py:812
  89.3 53.9 %copy-start.2 = (bf16[768,384]{1,0:T(8,128)(2,1)S(1)}, bf16[768,384]{1,0:T(8,128)(2,1)}, u32[]{:S(2)}) copy-start(bf16[768,384]{1,0:T(8,128)(2,1)} %constant.148.clone.itx) | copy-start | bytes 1769476
  89.3 53.9 %copy-start.3 = (bf16[384,768]{1,0:T(8,128)(2,1)S(1)}, bf16[384,768]{1,0:T(8,128)(2,1)}, u32[]{:S(2)}) copy-start(bf16[384,768]{1,0:T(8,128)(2,1)} %constant.147.clone.ftx) | copy-start | bytes 1769476
  89.3 255.4 %all-to-all-start = ((f32[16,2,24,147]{3,2,1,0:T(8,128)}), f32[16,2,24,147]{3,2,1,0:T(8,128)}, u32[]{:S(2)}, u32[]{:S(2)}) async-start(f32[16,2,24,147]{3,2,1,0:T(8,128)} %pad_maximum_fusion.5), calls=%async_computation | async-start | bytes 1572864 | tf_op jit(solution)/shard_map/all_to_all | solution.py:797
  136.6 631.8 %all-reduce.5.cloned.1.call-start = ((), (), s32[]{:S(2)}) async-start(), calls=%async_computation.2 | async-start | bytes 6619136 | tf_op jit(solution)/shard_map/psum | solution.py:925
  142.0 37.6 %copy-start.13 = (bf16[256,512]{1,0:T(8,128)(2,1)S(1)}, bf16[256,512]{1,0:T(8,128)(2,1)}, u32[]{:S(2)}) copy-start(bf16[256,512]{1,0:T(8,128)(2,1)} %get-tuple-element.259.w1) | copy-start | bytes 786436
  142.0 37.6 %copy-start.15 = (bf16[256,512]{1,0:T(8,128)(2,1)S(1)}, bf16[256,512]{1,0:T(8,128)(2,1)}, u32[]{:S(2)}) copy-start(bf16[256,512]{1,0:T(8,128)(2,1)} %get-tuple-element.260.w0) | copy-start | bytes 786436
  143.2 67.3 %copy-start.4 = (f32[768,256]{1,0:T(8,128)}, f32[768,256]{1,0:T(8,128)S(1)}, u32[]{:S(2)}) copy-start(f32[768,256]{1,0:T(8,128)S(1)} %fusion.33.h_ref) | copy-start | bytes 2359300
  359.2 34.1 %copy-start.14 = (bf16[256,512]{1,0:T(8,128)(2,1)S(1)}, bf16[256,512]{1,0:T(8,128)(2,1)}, u32[]{:S(2)}) copy-start(bf16[256,512]{1,0:T(8,128)(2,1)} %get-tuple-element.259.w1) | copy-start | bytes 786436
  359.2 34.1 %copy-start.16 = (bf16[256,512]{1,0:T(8,128)(2,1)S(1)}, bf16[256,512]{1,0:T(8,128)(2,1)}, u32[]{:S(2)}) copy-start(bf16[256,512]{1,0:T(8,128)(2,1)} %get-tuple-element.260.w0) | copy-start | bytes 786436
  569.8 22.9 %collective-permute-start.9 = (bf16[3,2,256,128]{3,2,1,0:T(8,128)(2,1)}, bf16[3,2,256,128]{3,2,1,0:T(8,128)(2,1)}, u32[]{:S(2)}, u32[]{:S(2)}) collective-permute-start(bf16[3,2,256,128]{3,2,1,0:T(8,128)(2,1)} %get-tuple-element.248), channel_id=1, source_target_pairs={{0,12},{1,13},{2,14},{3,15},{4,8},{5,9},{6,10},{7,11},{8,4},{9,5},... | collective-permute-start | bytes 1179656 | tf_op jit(solution)/shard_map/ppermute | solution.py:812
  572.9 22.1 %collective-permute-start.11 = (bf16[3,2,256,128]{3,2,1,0:T(8,128)(2,1)}, bf16[3,2,256,128]{3,2,1,0:T(8,128)(2,1)}, u32[]{:S(2)}, u32[]{:S(2)}) collective-permute-start(bf16[3,2,256,128]{3,2,1,0:T(8,128)(2,1)} %get-tuple-element.249), channel_id=1, source_target_pairs={{0,28},{1,29},{2,30},{3,31},{4,24},{5,25},{6,26},{7,27},{8,20},{9,... | collective-permute-start | bytes 1179656 | tf_op jit(solution)/shard_map/ppermute | solution.py:812
  574.2 24.0 %collective-permute-start.10 = (bf16[3,2,256,128]{3,2,1,0:T(8,128)(2,1)}, bf16[3,2,256,128]{3,2,1,0:T(8,128)(2,1)}, u32[]{:S(2)}, u32[]{:S(2)}) collective-permute-start(bf16[3,2,256,128]{3,2,1,0:T(8,128)(2,1)} %get-tuple-element.250), channel_id=1, source_target_pairs={{0,16},{1,17},{2,18},{3,19},{4,20},{5,21},{6,22},{7,23},{8,24},{9,... | collective-permute-start | bytes 1179656 | tf_op jit(solution)/shard_map/ppermute | solution.py:812
  578.2 23.2 %collective-permute-start.12 = (bf16[3,2,256,128]{3,2,1,0:T(8,128)(2,1)}, bf16[3,2,256,128]{3,2,1,0:T(8,128)(2,1)}, u32[]{:S(2)}, u32[]{:S(2)}) collective-permute-start(bf16[3,2,256,128]{3,2,1,0:T(8,128)(2,1)} %get-tuple-element.251), channel_id=1, source_target_pairs={{0,12},{1,13},{2,14},{3,15},{4,8},{5,9},{6,10},{7,11},{8,4},{9,5},... | collective-permute-start | bytes 1179656 | tf_op jit(solution)/shard_map/ppermute | solution.py:812
  581.3 32.2 %collective-permute-start.14 = (bf16[3,2,256,128]{3,2,1,0:T(8,128)(2,1)S(1)}, bf16[3,2,256,128]{3,2,1,0:T(8,128)(2,1)}, u32[]{:S(2)}, u32[]{:S(2)}) collective-permute-start(bf16[3,2,256,128]{3,2,1,0:T(8,128)(2,1)S(1)} %get-tuple-element.252), channel_id=1, source_target_pairs={{0,28},{1,29},{2,30},{3,31},{4,24},{5,25},{6,26},{7,27},{8,20},{9,... | collective-permute-start | bytes 1179656 | tf_op jit(solution)/shard_map/ppermute | solution.py:812
  592.7 25.1 %collective-permute-start.13 = (bf16[3,2,256,128]{3,2,1,0:T(8,128)(2,1)S(1)}, bf16[3,2,256,128]{3,2,1,0:T(8,128)(2,1)S(1)}, u32[]{:S(2)}, u32[]{:S(2)}) collective-permute-start(bf16[3,2,256,128]{3,2,1,0:T(8,128)(2,1)S(1)} %get-tuple-element.253), channel_id=1, source_target_pairs={{0,16},{1,17},{2,18},{3,19},{4,20},{5,21},{6,22},{7,23},{8,24},{9,... | collective-permute-start | bytes 1179656 | tf_op jit(solution)/shard_map/ppermute | solution.py:812
  595.0 38.6 %collective-permute-start.15 = (bf16[3,2,256,128]{3,2,1,0:T(8,128)(2,1)S(1)}, bf16[3,2,256,128]{3,2,1,0:T(8,128)(2,1)S(1)}, u32[]{:S(2)}, u32[]{:S(2)}) collective-permute-start(bf16[3,2,256,128]{3,2,1,0:T(8,128)(2,1)S(1)} %get-tuple-element.254), channel_id=1, source_target_pairs={{0,12},{1,13},{2,14},{3,15},{4,8},{5,9},{6,10},{7,11},{8,4},{9,5},... | collective-permute-start | bytes 1179656 | tf_op jit(solution)/shard_map/ppermute | solution.py:812
  598.2 35.3 %collective-permute-start.17 = (bf16[3,2,256,128]{3,2,1,0:T(8,128)(2,1)S(1)}, bf16[3,2,256,128]{3,2,1,0:T(8,128)(2,1)S(1)}, u32[]{:S(2)}, u32[]{:S(2)}) collective-permute-start(bf16[3,2,256,128]{3,2,1,0:T(8,128)(2,1)S(1)} %copy-done.86), channel_id=1, source_target_pairs={{0,28},{1,29},{2,30},{3,31},{4,24},{5,25},{6,26},{7,27},{8,20},{9,... | collective-permute-start | bytes 1179656 | tf_op jit(solution)/shard_map/ppermute | solution.py:812
  600.8 34.2 %copy-start.57 = (f32[1,6,2,256,128]{4,3,2,1,0:T(8,128)}, f32[1,6,2,256,128]{4,3,2,1,0:T(8,128)S(1)}, u32[]{:S(2)}) copy-start(f32[1,6,2,256,128]{4,3,2,1,0:T(8,128)S(1)} %maximum_select_fusion) | copy-start | bytes 4718596
  601.4 32.1 %collective-permute-start.16 = (bf16[3,2,256,128]{3,2,1,0:T(8,128)(2,1)S(1)}, bf16[3,2,256,128]{3,2,1,0:T(8,128)(2,1)S(1)}, u32[]{:S(2)}, u32[]{:S(2)}) collective-permute-start(bf16[3,2,256,128]{3,2,1,0:T(8,128)(2,1)S(1)} %copy-done.85), channel_id=1, source_target_pairs={{0,16},{1,17},{2,18},{3,19},{4,20},{5,21},{6,22},{7,23},{8,24},{9,... | collective-permute-start | bytes 1179656 | tf_op jit(solution)/shard_map/ppermute | solution.py:812
  636.2 139.8 %copy-start.72 = (f32[2,73,256]{2,0,1:T(2,128)S(1)}, f32[2,73,256]{2,0,1:T(2,128)}, u32[]{:S(2)}) copy-start(f32[2,73,256]{2,0,1:T(2,128)} %param.29) | copy-start | bytes 448516
  638.0 139.2 %copy-start.96 = (f32[2]{0:T(128)S(1)}, f32[2]{0:T(128)}, u32[]{:S(2)}) copy-start(f32[2]{0:T(128)} %multiply_reduce_fusion.8) | copy-start | bytes 28
  638.0 142.3 %copy-start.56 = (f32[3,2,256,512]{3,2,1,0:T(8,128)S(1)}, f32[3,2,256,512]{3,2,1,0:T(8,128)}, u32[]{:S(2)}) copy-start(f32[3,2,256,512]{3,2,1,0:T(8,128)} %param.32) | copy-start | bytes 9437188
  (90 other events, 1283.3 us)
Sparse Core Ops, SparseCore 0:
  592.8 175.5 all-reduce.4

commit v2 on v0

--- a/solution.py
+++ b/solution.py
@@ -1,8 +1,13 @@
+import functools
 import math
 
 import jax
 import jax.numpy as jnp
+import ml_dtypes
+import numpy as np
 from jax import lax
+from jax.experimental import pallas as pl
+from jax.experimental.pallas import tpu as pltpu
 from jax.sharding import PartitionSpec as P
 
 E = 256
@@ -135,7 +140,7 @@
     return (d_merged, jnp.stack([grad_in, grad_out], 0))
 
 
-def local(
+def general(
     inputs,
     targets,
     mask,
@@ -417,6 +422,802 @@
     )
 
 
+RANKS = 16
+ORDS = L // RANKS
+SLOTS = 8
+F32 = jnp.float32
+BF16 = jnp.bfloat16
+
+
+def legendre_f64(nlat):
+    theta = (np.arange(nlat) + 0.5) * (math.pi / nlat)
+    cosines, sines = np.cos(theta), np.sin(theta)
+    table = np.zeros((L, L, nlat))
+    for m in range(L):
+        log_start = 0.5 * (
+            math.log((2.0 * m + 1.0) / (4.0 * math.pi))
+            + math.lgamma(2.0 * m + 1.0)
+            - 2.0 * math.lgamma(m + 1.0)
+            - m * math.log(4.0)
+        ) + m * np.log(sines)
+        table[m, m] = np.exp(log_start)
+        if m + 1 < L:
+            table[m + 1, m] = math.sqrt(2.0 * m + 3.0) * cosines * table[m, m]
+        for k in range(m + 2, L):
+            factor = math.sqrt((4.0 * k * k - 1.0) / (k * k - m * m))
+            shrink = math.sqrt(((k - 1.0) ** 2 - m * m) / (4.0 * (k - 1.0) ** 2 - 1.0))
+            table[k, m] = factor * (cosines * table[k - 1, m] - shrink * table[k - 2, m])
+    return table, sines
+
+
+def low_np(array):
+    return array.astype(np.float32).astype(ml_dtypes.bfloat16)
+
+
+def slot_map():
+    degree = np.full((RANKS, 3, SLOTS), -1)
+    order = np.full((RANKS, SLOTS), -1)
+    for d in range(RANKS):
+        y, w, xc = d // 8, (d // 4) % 2, d % 4
+        lo, hi = 4 * w + xc, 4 * (3 - w) + xc
+        n_lo, n_hi = (6 * lo + 5) // RANKS + 1, (6 * hi + 5) // RANKS + 1
+        for group, first, count in ((hi, 0, n_hi), (lo, SLOTS - n_lo, n_lo)):
+            for r in range(count):
+                order[d, first + r] = r
+                for t in range(3):
+                    degree[d, t, first + r] = 6 * group + 3 * y + t
+    return degree, order
+
+
+def make_tables(nlat, nlon):
+    table, sines = legendre_f64(nlat)
+    quadrature = sines * (math.sqrt(2.0 * math.pi) / nlon * math.pi / nlat)
+    fwd_leg = np.asarray(low_np(table * quadrature[None, None, :]))
+    inv_leg = np.asarray(low_np(table))
+    degree, order = slot_map()
+    shape = (RANKS, RANKS, 3, 2, SLOTS, RANKS, ORDS, 2, 2)
+    fwd = np.zeros(shape, ml_dtypes.bfloat16)
+    inv = np.zeros(shape, ml_dtypes.bfloat16)
+    for g in range(RANKS):
+        for d in range(RANKS):
+            for slot in range(SLOTS):
+                r = order[d, slot]
+                if r < 0:
+                    continue
+                for t in range(3):
+                    k, m = degree[d, t, slot], g + RANKS * r
+                    for p in range(2):
+                        fwd[g, d, t, p, slot, :, r, p, :] = fwd_leg[k, m].reshape(RANKS, 2)
+                        inv[g, d, t, p, slot, :, r, p, :] = inv_leg[k, m].reshape(RANKS, 2)
+    rows = RANKS * 3 * 2 * SLOTS
+    cols = RANKS * ORDS * 2 * 2
+    fwd = fwd.reshape(RANKS, rows, cols)
+    inv = inv.reshape(RANKS, rows, cols)
+    phase = 2.0 * math.pi * (np.arange(L)[:, None] * np.arange(nlon)[None, :] % nlon) / nlon
+    scale = np.where(np.arange(L) == 0, 1.0, 2.0)[:, None] / math.sqrt(2.0 * math.pi)
+    four = low_np(np.stack([np.cos(phase), -np.sin(phase)], 1))
+    back = low_np(np.stack([scale * np.cos(phase), -scale * np.sin(phase)], 1))
+    def wide(small):
+        out = np.zeros((RANKS, ORDS, 2, 2, 2, nlon), ml_dtypes.bfloat16)
+        ordered = small.reshape(ORDS, RANKS, 2, nlon).transpose(1, 0, 2, 3)
+        for il in range(2):
+            out[:, :, :, il, il, :] = ordered
+        return out.reshape(cols, 2 * nlon)
+
+    def turn(array):
+        return np.ascontiguousarray(np.swapaxes(array, -1, -2))
+
+    four, back = wide(four), wide(back)
+    return (fwd, turn(inv), turn(fwd), inv), (four, turn(back), turn(four), back)
+
+
+def place():
+    ma = lax.axis_index("ma")
+    y = lax.axis_index("lat")
+    z = ma // 4
+    zh = z // 2
+    w = z + zh * (3 - 2 * z)
+    return zh, y, w, 8 * y + 4 * w + ma % 4
+
+
+def device_of(zh, q):
+    w = (q // 4) % 2
+    z = w + zh * (3 - 2 * w)
+    return {"lat": q // 8, "ma": 4 * z + q % 4}
+
+
+def nn(a, b):
+    return lax.dot_general(a, b, (((1,), (0,)), ((), ())), preferred_element_type=F32)
+
+
+def nt(a, b):
+    return lax.dot_general(a, b, (((1,), (1,)), ((), ())), preferred_element_type=F32)
+
+
+def tn(a, b):
+    return lax.dot_general(a, b, (((0,), (0,)), ((), ())), preferred_element_type=F32)
+
+
+def piece_of(kind, half, zh, y):
+    return 2 - 2 * ((kind + zh) % 2) + (half + y) % 2
+
+
+def weight_of(w_all, block, kind, t, part, zh, y):
+    return jnp.concatenate(
+        [w_all[block, piece_of(kind, half, zh, y), t, part] for half in range(2)], axis=1
+    )
+
+
+def hi_rows(w):
+    slot = lax.broadcasted_iota(jnp.int32, (RANKS * 2 * SLOTS, 1), 0) % SLOTS
+    return slot < 6 - w
+
+
+GELU_A = math.sqrt(2.0 / math.pi)
+GELU_B = 0.044715
+
+
+def normal_of(hidden):
+    centre = jnp.mean(hidden, -1, keepdims=True)
+    centred = hidden - centre
+    inv_std = lax.rsqrt(jnp.mean(centred * centred, -1, keepdims=True) + norm_eps)
+    return centred * inv_std, inv_std
+
+
+def rows_loop(total, step, body):
+    def one(k, carry):
+        body(pl.ds(pl.multiple_of(k * step, step), step))
+        return carry
+
+    lax.fori_loop(0, total // step, one, 0)
+
+
+MESH = pl.DeviceIdType.MESH
+LANES = 128
+MASK_LANE = LANES - 1
+
+
+def greet_all():
+    barrier = pltpu.get_barrier_semaphore()
+    me = 2 * RANKS // 2 * lax.axis_index("lat") + lax.axis_index("ma")
+
+    def greet(s, carry):
+        other = (me + s) % (2 * RANKS)
+        pl.semaphore_signal(
+            barrier, inc=1, device_id={"lat": other // RANKS, "ma": other % RANKS}, device_id_type=MESH
+        )
+        return carry
+
+    lax.fori_loop(1, 2 * RANKS, greet, 0)
+    pl.semaphore_wait(barrier, 2 * RANKS - 1)
+
+
+def remote(src, dst, send_sem, recv_sem, device):
+    return pltpu.make_async_remote_copy(
+        src_ref=src,
+        dst_ref=dst,
+        send_sem=send_sem,
+        recv_sem=recv_sem,
+        device_id=device,
+        device_id_type=MESH,
+    )
+
+
+def bytes_wait(ref, sem):
+    pltpu.make_async_copy(ref, ref, sem).wait()
+
+
+def push_blocks(source_of, landing, send_sem, recv_sem, zh, q):
+    pltpu.make_async_copy(source_of(q), landing, recv_sem).start()
+
+    def push(s, carry):
+        d = (q + s) % RANKS
+        remote(source_of(d), landing, send_sem, recv_sem, device_of(zh, d)).start()
+        return carry
+
+    lax.fori_loop(1, RANKS, push, 0)
+
+
+def exchange_start(send, recv, send_sem, recv_sem, zh, q):
+    push_blocks(lambda d: send.at[d], recv.at[q], send_sem, recv_sem, zh, q)
+
+
+def exchange_wait(send, recv, send_sem, recv_sem):
+    bytes_wait(recv, recv_sem)
+    bytes_wait(send.at[pl.ds(0, RANKS - 1)], send_sem)
+
+
+def exchange(send, recv, send_sem, recv_sem, zh, q):
+    exchange_start(send, recv, send_sem, recv_sem, zh, q)
+    exchange_wait(send, recv, send_sem, recv_sem)
+
+
+def lane_sums(array):
+    return jnp.sum(array.reshape(-1, LANES), axis=0, keepdims=True)
+
+
+def train(
+    x_chunks, t_chunks, spec_w, mlp_w, r0, r1, r2, r3, f0, f1, f2, f3,
+    encdec, gain, area, var_row,
+    g_spec, g_mlp, g_small, scalars,
+    pfx, pix, pfxt, pixt, ftx, itx, ftxt, itxt, w_all, w_other, mlp_bf, mlp_stage, code_bf,
+    x_recv, goals, weight, x_low, misfit, d_state, h_all, hid_low, v_low, u_buf, dv_buf, dh_buf,
+    n_send, s_recv, y_recv, w_send, b_recv, a_own, d_mix,
+    dwf, dw_send, dw_recv, dw_own, dmlp, rs_send, rs_recv, mir_send, mir_recv, ag_src,
+    d_small, d_gain, sm_send, sm_recv, sm_mir_send, sm_mir_recv, sm_src, scal, scal_recv,
+    load_sem, stage_sem, once_send, once_recv, w_send_sem, w_recv_sem, x_send, x_recv_sem,
+    g_send_sem, g_recv_sem, rs_sem, mir_send_sem, mir_recv_sem, ag_send_sem, ag_recv_sem, sm_sem,
+):
+    zh, y, w, q = place()
+    ma = lax.axis_index("ma")
+    xc = ma % 4
+    mirror_ma = 4 * (3 - ma // 4) + xc
+    near, far, cross = {"lat": 1 - y, "ma": ma}, {"lat": y, "ma": mirror_ma}, {"lat": 1 - y, "ma": mirror_ma}
+    pixels, chans = dh_buf.shape
+    spectra = pix.shape[0]
+    triples = pfx.shape[0]
+    third = 3
+
+    loads = [
+        pltpu.make_async_copy(src.at[q], dst, load_sem.at[k])
+        for k, (src, dst) in enumerate(((r0, pfx), (r1, pix), (r2, pfxt), (r3, pixt)))
+    ] + [
+        pltpu.make_async_copy(src, dst, load_sem.at[4 + k])
+        for k, (src, dst) in enumerate(((f0, ftx), (f1, itx), (f2, ftxt), (f3, itxt)))
+    ]
+    stage = dwf
+
+    class SpecLoad:
+        def __init__(self, b):
+            self.copies = [
+                pltpu.make_async_copy(
+                    spec_w.at[b, pl.ds(third * k, third)], stage.at[2 * (b % 2) + k], stage_sem.at[2 * b + k]
+                )
+                for k in range(2)
+            ]
+
+        def start(self):
+            for copy in self.copies:
+                copy.start()
+
+        def wait(self):
+            for copy in self.copies:
+                copy.wait()
+
+    spec_loads = [SpecLoad(b) for b in range(NB)]
+    mlp_loads = [pltpu.make_async_copy(mlp_w.at[b], mlp_stage.at[b % 2], stage_sem.at[2 * NB + b]) for b in range(NB)]
+    spec_loads[0].start()
+    spec_loads[1].start()
+    loads[4].start()
+    loads[0].start()
+    scal[...] = jnp.zeros_like(scal)
+    d_small[...] = jnp.zeros_like(d_small)
+    d_gain[...] = jnp.zeros_like(d_gain)
+    d_state[...] = jnp.zeros_like(d_state)
+    code_bf[...] = encdec[...].astype(BF16)
+    greet_all()
+
+    def chunk_to(chunks, landing, sems):
+        pltpu.make_async_copy(chunks.at[ma], landing, sems[1]).start()
+
+        def push(s, carry):
+            other = (ma + s) % RANKS
+            remote(chunks.at[other], landing, sems[0], sems[1], {"lat": y, "ma": other}).start()
+            return carry
+
+        lax.fori_loop(1, RANKS, push, 0)
+
+    chunk_to(x_chunks, x_recv.at[:, ma], (once_send.at[0], once_recv.at[0]))
+
+    for b in range(NB):
+        spec_loads[b].wait()
+        for t in range(third):
+            for own, target in ((y, w_all.at[b, 0]), (1 - y, w_other.at[b])):
+                value = stage[2 * (b % 2) + own, t]
+                scal[2 + b : 3 + b] += lane_sums(value * value)
+                target[t] = value.astype(BF16)
+        if b + 2 < NB:
+            spec_loads[b + 2].start()
+        sems = (w_send_sem.at[b], w_recv_sem.at[b])
+        remote(w_other.at[b], w_all.at[b, 3], *sems, cross).start()
+        remote(w_all.at[b, 0], w_all.at[b, 2], *sems, far).start()
+        remote(w_other.at[b], w_all.at[b, 1], *sems, near).start()
+        if b == 0:
+            mlp_loads[0].start()
+            mlp_loads[1].start()
+            for k in (1, 2, 3, 5, 6, 7):
+                loads[k].start()
+    chunk_to(t_chunks, goals.at[:, :, ma], (once_send.at[1], once_recv.at[1]))
+    for b in range(NB):
+        mlp_loads[b].wait()
+        mlp_bf[b] = mlp_stage[b % 2].astype(BF16)
+        if b + 2 < NB:
+            mlp_loads[b + 2].start()
+    for copy in loads:
+        copy.wait()
+    bytes_wait(x_recv, once_recv.at[0])
+    bytes_wait(x_chunks.at[pl.ds(0, RANKS - 1)], once_send.at[0])
+
+    hi = hi_rows(w)
+    rows_mix = RANKS * 2 * SLOTS
+
+    def mixed_by(source, product, block, t, part):
+        return jnp.where(
+            hi,
+            product(source, weight_of(w_all, block, 0, t, part, zh, y)),
+            product(source, weight_of(w_all, block, 1, t, part, zh, y)),
+        ).reshape(RANKS, 2, SLOTS, chans)
+
+    def narrow(value):
+        return value.astype(BF16).reshape(n_send.shape)
+
+    def broad(value):
+        return value.astype(BF16).reshape(w_send.shape)
+
+    def fwd_block(step, block):
+        slot, idx = 4 * step + block, NB * step + block
+        gain_row = gain[block]
+
+        def norm_rows(rows):
+            normal, unused = normal_of(h_all[slot, rows, :])
+            u_buf[rows, :] = (normal * gain_row).astype(BF16)
+
+        rows_loop(pixels, 128, norm_rows)
+        n_send[...] = narrow(nn(ftx[...], u_buf[...]))
+        exchange(n_send, s_recv, x_send.at[0], x_recv_sem.at[0], zh, q)
+        w_send[...] = broad(nn(pfx[...], s_recv[...].reshape(spectra, chans)))
+        exchange(w_send, a_own.at[idx], x_send.at[1], x_recv_sem.at[1], zh, q)
+
+        @pl.when(step == 0)
+        def _():
+            bytes_wait(w_all.at[block, pl.ds(1, 3)], w_recv_sem.at[block])
+
+        for t in range(3):
+            coef = a_own[idx, :, t].reshape(rows_mix, chans)
+            by_real, by_imag = (mixed_by(coef, nn, block, t, part) for part in range(2))
+            mixed = jnp.stack([by_real[:, 0] - by_imag[:, 1], by_real[:, 1] + by_imag[:, 0]], 1)
+            w_send[:, t] = mixed.reshape(RANKS, 2 * SLOTS, chans).astype(BF16)
+        exchange(w_send, b_recv, x_send.at[2], x_recv_sem.at[2], zh, q)
+        n_send[...] = narrow(nn(pix[...], b_recv[...].reshape(triples, chans)))
+        exchange(n_send, y_recv, x_send.at[3], x_recv_sem.at[3], zh, q)
+        spectrum = y_recv[...].reshape(spectra, chans)
+
+        def mlp_rows(rows):
+            merged = h_all[slot, rows, :] + nn(itx[rows, :], spectrum)
+            merged_low = merged.astype(BF16)
+            v_low[idx, rows, :] = merged_low
+            pre = nn(merged_low, mlp_bf[block, 0])
+            act = (0.5 * pre * (1.0 + jnp.tanh(GELU_A * (pre + GELU_B * pre * pre * pre)))).astype(BF16)
+            h_all[slot + 1, rows, :] = merged + nt(act, mlp_bf[block, 1])
+
+        rows_loop(pixels, 256, mlp_rows)
+
+    denom = float(pixels * RANKS * C * 2)
+
+    def fwd_step(step, carry):
+        state = x_recv[...].reshape(pixels, LANES)
+        state_low = state.astype(BF16)
+        x_low[step] = state_low
+        h_all[4 * step] = nn(state_low, code_bf[0])
+
+        def one(block, inner):
+            fwd_block(step, block)
+            return inner
+
+        lax.fori_loop(0, NB, one, 0)
+        hidden_low = h_all[4 * step + 3].astype(BF16)
+        hid_low[step] = hidden_low
+        prediction = state + nt(hidden_low, code_bf[1])
+        x_recv[...] = prediction.reshape(x_recv.shape)
+
+        @pl.when(step == 0)
+        def _():
+            bytes_wait(goals, once_recv.at[1])
+            bytes_wait(t_chunks.at[pl.ds(0, RANKS - 1)], once_send.at[1])
+            for il in range(2):
+                valid = goals[0, il].reshape(pixels // 2, LANES)[:, MASK_LANE:]
+                rows = slice(il * pixels // 2, (il + 1) * pixels // 2)
+                weight[rows, :] = valid * (area[il] * var_row[...])
+
+        miss = prediction - goals[step].reshape(pixels, LANES)
+        weighted = weight[...] * miss
+        scal[0:1] += lane_sums(weighted * miss / denom)
+        misfit[step] = 2.0 * weighted / denom
+        return carry
+
+    lax.fori_loop(0, ROLL, fwd_step, 0)
+    for b in range(NB):
+        bytes_wait(w_all.at[b, pl.ds(1, 3)], w_send_sem.at[b])
+
+    def settle(block):
+        bytes_wait(dw_recv.at[block], g_recv_sem.at[block])
+        for t in range(third):
+            for own, one, two in (
+                (y, dw_own[block, t], dw_recv[block, 1, t]),
+                (1 - y, dw_recv[block, 0, t], dw_recv[block, 2, t]),
+            ):
+                total = one.astype(F32) + two.astype(F32)
+                scal[1:2] += lane_sums(total * total)
+                g_spec[block, third * own + t] = total
+
+    def bwd_block(lap, step, block):
+        slot, idx = 4 * step + block, NB * step + block
+        gain_row = gain[block]
+
+        @pl.when(lap == 0)
+        def _():
+            dmlp[block] = jnp.zeros(dmlp.shape[1:], F32)
+
+        def mlp_rows(rows):
+            d_hidden = dh_buf[rows, :]
+            d_branch = d_hidden.astype(BF16)
+            merged_low = v_low[idx, rows, :]
+            pre = nn(merged_low, mlp_bf[block, 0])
+            tan = jnp.tanh(GELU_A * (pre + GELU_B * pre * pre * pre))
+            act = (0.5 * pre * (1.0 + tan)).astype(BF16)
+            slope = 0.5 * (1.0 + tan) + 0.5 * pre * (1.0 - tan * tan) * (
+                GELU_A * (1.0 + 3.0 * GELU_B * pre * pre)
+            )
+            d_pre = (nn(d_branch, mlp_bf[block, 1]) * slope).astype(BF16)
+            dmlp[block, 0] += tn(merged_low, d_pre)
+            dmlp[block, 1] += tn(d_branch, act)
+            d_merged = d_hidden + nt(d_pre, mlp_bf[block, 0])
+            dv_buf[rows, :] = d_merged
+            u_buf[rows, :] = d_merged.astype(BF16)
+
+        rows_loop(pixels, 256, mlp_rows)
+        n_send[...] = narrow(nn(itxt[...], u_buf[...]))
+        exchange_start(n_send, s_recv, x_send.at[4], x_recv_sem.at[4], zh, q)
+
+        @pl.when(lap == 1)
+        def _():
+            rs_send[...] = dmlp[block].astype(BF16).reshape(rs_send.shape)
+            exchange_start(rs_send, rs_recv, rs_sem.at[0], rs_sem.at[1], zh, q)
+
+        exchange_wait(n_send, s_recv, x_send.at[4], x_recv_sem.at[4])
+        w_send[...] = broad(nn(pixt[...], s_recv[...].reshape(spectra, chans)))
+        which = NB * lap + block
+        exchange_start(w_send, d_mix.at[which], x_send.at[5], x_recv_sem.at[5], zh, q)
+
+        @pl.when(lap == 1)
+        def _():
+            exchange_wait(rs_send, rs_recv, rs_sem.at[0], rs_sem.at[1])
+            share = rs_recv[0].astype(F32)
+            for k in range(1, RANKS):
+                share = share + rs_recv[k].astype(F32)
+            mir_send[block] = share
+            remote(mir_send.at[block], mir_recv.at[block], mir_send_sem.at[block], mir_recv_sem.at[block], far).start()
+
+        exchange_wait(w_send, d_mix.at[which], x_send.at[5], x_recv_sem.at[5])
+
+        def turned_of(d_mixed):
+            wide = d_mixed.astype(F32).reshape(RANKS, 2, SLOTS, chans)
+            return jnp.stack([wide[:, 1], -wide[:, 0]], 1).reshape(rows_mix, chans).astype(BF16)
+
+        for t in range(3):
+            d_mixed = d_mix[which, :, t].reshape(rows_mix, chans)
+            by_real, by_imag = (mixed_by(d_mixed, nt, block, t, part) for part in range(2))
+            d_coef = jnp.stack([by_real[:, 0] + by_imag[:, 1], by_real[:, 1] - by_imag[:, 0]], 1)
+            w_send[:, t] = d_coef.reshape(RANKS, 2 * SLOTS, chans).astype(BF16)
+        exchange_start(w_send, b_recv, x_send.at[6], x_recv_sem.at[6], zh, q)
+
+        @pl.when(lap == 1)
+        def _():
+            for t in range(3):
+                others = []
+                for turn in range(ROLL):
+                    d_mixed = d_mix[NB * turn + block, :, t].reshape(rows_mix, chans)
+                    others.append((d_mixed, turned_of(d_mixed)))
+                for kind in range(2):
+                    keep = hi if kind == 0 else jnp.logical_not(hi)
+                    kept = [
+                        jnp.where(
+                            keep, a_own[NB * (1 - turn) + block, :, t].reshape(rows_mix, chans).astype(F32), 0.0
+                        ).astype(BF16)
+                        for turn in range(ROLL)
+                    ]
+                    for part in range(2):
+                        grad = tn(kept[0], others[0][part]) + tn(kept[1], others[1][part])
+                        for half in range(2):
+                            dwf[piece_of(kind, half, zh, y), t, part] = grad[
+                                :, half * LANES : (half + 1) * LANES
+                            ]
+            dw_own[block] = dwf[0]
+            for k in range(3):
+                dw_send[block, k] = dwf[1 + k].astype(BF16)
+            sems = (g_send_sem.at[block], g_recv_sem.at[block])
+            remote(dw_send.at[block, 2], dw_recv.at[block, 2], *sems, cross).start()
+            remote(dw_send.at[block, 1], dw_recv.at[block, 1], *sems, far).start()
+            remote(dw_send.at[block, 0], dw_recv.at[block, 0], *sems, near).start()
+            bytes_wait(mir_recv.at[block], mir_recv_sem.at[block])
+            total = mir_send[block] + mir_recv[block]
+            scal[1:2] += 0.5 * lane_sums(total * total)
+            ag_src[block] = total.astype(BF16)
+            push_blocks(lambda d: ag_src.at[block], g_mlp.at[block, q], ag_send_sem.at[block], ag_recv_sem.at[block], zh, q)
+
+        exchange_wait(w_send, b_recv, x_send.at[6], x_recv_sem.at[6])
+        n_send[...] = narrow(nn(pfxt[...], b_recv[...].reshape(triples, chans)))
+        exchange(n_send, y_recv, x_send.at[7], x_recv_sem.at[7], zh, q)
+        spectrum = y_recv[...].reshape(spectra, chans)
+
+        def norm_rows(rows):
+            normal, inv_std = normal_of(h_all[slot, rows, :])
+            d_normed = nn(ftxt[rows, :], spectrum)
+            scaled = d_normed * gain_row
+            d_gain[block] += jnp.sum(d_normed * normal, axis=0, keepdims=True)
+            d_norm_in = inv_std * (
+                scaled
+                - jnp.mean(scaled, -1, keepdims=True)
+                - normal * jnp.mean(scaled * normal, -1, keepdims=True)
+            )
+            dh_buf[rows, :] = dv_buf[rows, :] + d_norm_in
+
+        rows_loop(pixels, 256, norm_rows)
+
+        @pl.when(jnp.logical_and(lap == 1, block < NB - 1))
+        def _():
+            settle(block + 1)
+
+    def bwd_step(lap, carry):
+        step = ROLL - 1 - lap
+        d_pred = misfit[step] + d_state[...]
+        d_dec = d_pred.astype(BF16)
+        d_small[LANES:] += tn(d_dec, hid_low[step])
+        dh_buf[...] = nn(d_dec, code_bf[1])
+
+        def one(k, inner):
+            bwd_block(lap, step, NB - 1 - k)
+            return inner
+
+        lax.fori_loop(0, NB, one, 0)
+        d_enc = dh_buf[...].astype(BF16)
+        d_small[:LANES] += tn(x_low[step], d_enc)
+
+        @pl.when(lap == 0)
+        def _():
+            d_state[...] = d_pred + nt(d_enc, code_bf[0])
+
+        return carry
+
+    lax.fori_loop(0, ROLL, bwd_step, 0)
+
+    for b in range(NB):
+        d_small[LANES - NB + b : LANES - NB + b + 1] = d_gain[b]
+    sm_send[...] = d_small[...].reshape(sm_send.shape)
+    exchange(sm_send, sm_recv, sm_sem.at[0], sm_sem.at[1], zh, q)
+    share = sm_recv[0]
+    for k in range(1, RANKS):
+        share = share + sm_recv[k]
+    sm_mir_send[...] = share
+    swap = remote(sm_mir_send, sm_mir_recv, sm_sem.at[2], sm_sem.at[3], far)
+    swap.start()
+    swap.wait()
+    total = sm_mir_send[...] + sm_mir_recv[...]
+    scal[1:2] += 0.5 * lane_sums(total * total)
+    sm_src[...] = total
+    push_blocks(lambda d: sm_src, g_small.at[q], sm_sem.at[4], sm_sem.at[5], zh, q)
+    settle(0)
+
+    me = RANKS * y + ma
+    pltpu.make_async_copy(scal, scal_recv.at[me], sm_sem.at[7]).start()
+
+    def spread(s, carry):
+        other = (me + s) % (2 * RANKS)
+        remote(
+            scal, scal_recv.at[me], sm_sem.at[6], sm_sem.at[7], {"lat": other // RANKS, "ma": other % RANKS}
+        ).start()
+        return carry
+
+    lax.fori_loop(1, 2 * RANKS, spread, 0)
+    bytes_wait(g_small, sm_sem.at[5])
+    bytes_wait(g_small.at[pl.ds(0, RANKS - 1)], sm_sem.at[4])
+    for b in range(NB):
+        bytes_wait(g_mlp.at[b], ag_recv_sem.at[b])
+        bytes_wait(g_mlp.at[b, pl.ds(0, RANKS - 1)], ag_send_sem.at[b])
+        bytes_wait(mir_send.at[b], mir_send_sem.at[b])
+        bytes_wait(dw_send.at[b], g_send_sem.at[b])
+    bytes_wait(scal_recv, sm_sem.at[7])
+    bytes_wait(scal_recv.at[pl.ds(0, 2 * RANKS - 1)], sm_sem.at[6])
+    total = scal_recv[0]
+    for k in range(1, 2 * RANKS):
+        total = total + scal_recv[k]
+    scalars[...] = total
+
+
+def call_train(x_chunks, t_chunks, spec_w, mlp_w, tables, encdec, gain, area, var_row):
+    vmem = pltpu.VMEM
+    dma = pltpu.SemaphoreType.DMA
+    lon = x_chunks.shape[2]
+    pixels, chans = 2 * RANKS * lon, gain.shape[-1]
+    third = spec_w.shape[1] // 2
+    triple = (third, 2, chans, LANES)
+    narrow, wide = (RANKS, 4 * ORDS, chans), (RANKS, 3, 2 * SLOTS, chans)
+    triples, spectra = RANKS * 6 * SLOTS, RANKS * 4 * ORDS
+    mlp_shape = mlp_w.shape[1:]
+    chunk = (mlp_shape[0] * mlp_shape[1] // RANKS, mlp_shape[2])
+    small = (2 * LANES // RANKS, chans)
+    b16 = lambda *shape: vmem(shape, BF16)
+    f32 = lambda *shape: vmem(shape, F32)
+    everywhere = pl.BlockSpec(memory_space=pl.ANY)
+    inside = pl.BlockSpec(memory_space=vmem)
+    return pl.pallas_call(
+        train,
+        out_shape=(
+            jax.ShapeDtypeStruct(spec_w.shape, F32),
+            jax.ShapeDtypeStruct((NB, RANKS, *chunk), BF16),
+            jax.ShapeDtypeStruct((RANKS, *small), F32),
+            jax.ShapeDtypeStruct((8, LANES), F32),
+        ),
+        in_specs=[everywhere] * 12 + [inside] * 4,
+        out_specs=[inside] * 4,
+        scratch_shapes=[
+            b16(triples, spectra), b16(spectra, triples), b16(spectra, triples), b16(triples, spectra),
+            b16(spectra, pixels), b16(pixels, spectra), b16(pixels, spectra), b16(spectra, pixels),
+            b16(NB, 4, *triple), b16(NB, *triple), b16(*mlp_w.shape), f32(2, *mlp_shape),
+            b16(*encdec.shape),
+            f32(2, RANKS, lon, LANES), f32(ROLL, 2, RANKS, lon, LANES), f32(pixels, LANES), b16(ROLL, pixels, LANES),
+            f32(ROLL, pixels, LANES), f32(pixels, LANES), f32(4 * ROLL, pixels, chans), b16(ROLL, pixels, chans),
+            b16(NB * ROLL, pixels, chans), b16(pixels, chans), f32(pixels, chans), f32(pixels, chans),
+            b16(*narrow), b16(*narrow), b16(*narrow), b16(*wide), b16(*wide), b16(NB * ROLL, *wide), b16(NB * ROLL, *wide),
+            f32(4, *triple), b16(NB, 3, *triple), b16(NB, 3, *triple), f32(NB, *triple), f32(NB, *mlp_shape),
+            b16(RANKS, *chunk), b16(RANKS, *chunk), f32(NB, *chunk), f32(NB, *chunk), b16(NB, *chunk),
+            f32(2 * LANES, chans), f32(NB, 1, chans), f32(RANKS, *small), f32(RANKS, *small), f32(*small), f32(*small),
+            f32(*small), f32(8, LANES), f32(2 * RANKS, 8, LANES),
+            dma((8,)), dma((3 * NB,)), dma((2,)), dma((2,)), dma((NB,)), dma((NB,)), dma((8,)), dma((8,)),
+            dma((NB,)), dma((NB,)), dma((2,)), dma((NB,)), dma((NB,)), dma((NB,)), dma((NB,)), dma((8,)),
+        ],
+        compiler_params=pltpu.CompilerParams(
+            collective_id=0, has_side_effects=True, vmem_limit_bytes=61 << 20
+        ),
+    )(x_chunks, t_chunks, spec_w, mlp_w, *tables, encdec, gain, area, var_row)
+
+
+def sum_all(value_ref, out_ref, recv, send_sem, recv_sem):
+    greet_all()
+    me = RANKS * lax.axis_index("lat") + lax.axis_index("ma")
+    pltpu.make_async_copy(value_ref, recv.at[me], recv_sem).start()
+
+    def spread(s, carry):
+        other = (me + s) % (2 * RANKS)
+        remote(value_ref, recv.at[me], send_sem, recv_sem, {"lat": other // RANKS, "ma": other % RANKS}).start()
+        return carry
+
+    lax.fori_loop(1, 2 * RANKS, spread, 0)
+    bytes_wait(recv, recv_sem)
+    bytes_wait(recv.at[pl.ds(0, 2 * RANKS - 1)], send_sem)
+    total = recv[0]
+    for k in range(1, 2 * RANKS):
+        total = total + recv[k]
+    out_ref[...] = total
+
+
+def call_sum(value):
+    inside = pl.BlockSpec(memory_space=pltpu.VMEM)
+    return pl.pallas_call(
+        sum_all,
+        out_shape=jax.ShapeDtypeStruct(value.shape, F32),
+        in_specs=[inside],
+        out_specs=inside,
+        scratch_shapes=[
+            pltpu.VMEM((2 * RANKS, *value.shape), F32),
+            pltpu.SemaphoreType.DMA,
+            pltpu.SemaphoreType.DMA,
+        ],
+        compiler_params=pltpu.CompilerParams(collective_id=1, has_side_effects=True),
+    )(value)
+
+
+def chunks_of(field):
+    items, lon, lat, width = field.shape
+    pairs = lat // 2
+    chunks = jnp.moveaxis(field.reshape(items, lon, pairs, 2, width), 1, 3)
+    return jnp.concatenate([chunks[0], jnp.roll(chunks[1], pairs // 2, 0)], 0)
+
+
+def special(
+    inputs,
+    targets,
+    mask,
+    var_weight,
+    step_count,
+    spec_w,
+    spec_m,
+    spec_v,
+    encdec_w,
+    encdec_m,
+    encdec_v,
+    mlp_w,
+    mlp_m,
+    mlp_v,
+    gain_w,
+    gain_m,
+    gain_v,
+):
+    zh, y, w, q = place()
+    nlon = inputs.shape[1] * lax.axis_size("ma")
+    nlat = inputs.shape[2] * lax.axis_size("lat")
+    ranked, common = make_tables(nlat, nlon)
+    tables = tuple(jnp.asarray(t) for t in (*ranked, *common))
+    spare = LANES - C
+    x_chunks = chunks_of(jnp.pad(inputs, ((0, 0),) * 3 + ((0, spare),)))
+    masks = jnp.broadcast_to(mask.astype(F32)[None, ..., None], (*targets.shape[:-1], 1))
+    goal = jnp.concatenate([targets, jnp.zeros((*targets.shape[:-1], spare - 1), F32), masks], -1)
+    t_chunks = jnp.stack([chunks_of(goal[0]), chunks_of(goal[1])], 1)
+    angles = (jnp.arange(nlat, dtype=F32) + 0.5) * (math.pi / nlat)
+    sines = jnp.sin(angles)
+    area = lax.dynamic_slice_in_dim(sines / jnp.mean(sines), 2 * q, 2)
+    area = jnp.broadcast_to(area[:, None, None], (2, 1, LANES))
+    var_row = jnp.pad(var_weight.astype(F32), (0, spare))[None]
+    encdec = jnp.pad(encdec_w, ((0, 0), (0, spare), (0, 0)))
+    spec_grad, mlp_sum, small_sum, scalars = call_train(
+        x_chunks, t_chunks, spec_w, mlp_w, tables, encdec, gain_w[:, None], area, var_row
+    )
+    grad_mlp = mlp_sum.reshape(mlp_w.shape).astype(F32)
+    small_sum = small_sum.reshape(2, LANES, E)
+    grad_encdec = small_sum[:, :C]
+    grad_gain = small_sum[0, LANES - NB :]
+    sums = jnp.sum(scalars, 1)
+    loss_value = sums[0]
+    weight_square = sums[2 : 2 + NB]
+    grad_norm = jnp.sqrt(sums[1])
+    scale = clip_norm / jnp.maximum(grad_norm, clip_norm)
+    step_float = step_count[0].astype(F32)
+    spec_m_new, spec_v_new, direction = adaptive(
+        spec_w, spec_m, spec_v, spec_grad * scale, step_float
+    )
+    dir_part = jnp.sum(direction * direction, axis=(1, 2, 3))
+    dir_square = jnp.sum(call_sum(jnp.pad(dir_part, ((0, 8 - NB), (0, 0)))), 1)[:NB]
+    weight_norm = jnp.sqrt(weight_square)
+    dir_norm = jnp.sqrt(dir_square)
+    trust = weight_norm / (dir_norm + 1e-06)
+    spec_new = spec_w - learn_rate * trust[:, None, None, None, None] * direction
+    encdec_new, encdec_m_new, encdec_v_new, encdec_norms = lamb_dense(
+        encdec_w, encdec_m, encdec_v, grad_encdec * scale, step_float, 2
+    )
+    mlp_new, mlp_m_new, mlp_v_new, mlp_norms = lamb_dense(
+        mlp_w, mlp_m, mlp_v, grad_mlp * scale, step_float, 2 * NB
+    )
+    gain_new, gain_m_new, gain_v_new, gain_norms = lamb_dense(
+        gain_w, gain_m, gain_v, grad_gain * scale, step_float, NB
+    )
+    matrix_norms = jnp.concatenate(
+        [jnp.stack([weight_norm, dir_norm], 1), encdec_norms, mlp_norms, gain_norms], 0
+    )
+    return (
+        loss_value,
+        grad_norm,
+        matrix_norms,
+        spec_new,
+        spec_m_new,
+        spec_v_new,
+        spec_new.astype(jnp.bfloat16),
+        encdec_new,
+        encdec_m_new,
+        encdec_v_new,
+        encdec_new.astype(jnp.bfloat16),
+        mlp_new,
+        mlp_m_new,
+        mlp_v_new,
+        mlp_new.astype(jnp.bfloat16),
+        gain_new,
+        gain_m_new,
+        gain_v_new,
+        gain_new.astype(jnp.bfloat16),
+    )
+
+
+def local(mesh, *args):
+    inputs, spec_w = args[0], args[5]
+    lat = inputs.shape[2] * mesh.shape["lat"]
+    fits = (
+        dict(mesh.shape) == {"lat": 2, "ma": RANKS}
+        and inputs.shape[0] == 2
+        and lat == 2 * RANKS
+        and spec_w.shape[1] * RANKS == L
+    )
+    return (special if fits else general)(*args)
+
+
 def solution(mesh):
     placed = (
         P(None, "ma", "lat", None),
@@ -438,7 +1239,7 @@
         P(),
     )
     return jax.shard_map(
-        local,
+        functools.partial(local, mesh),
         mesh=mesh,
         in_specs=placed,
         out_specs=(

time: 3970 us -> 595 us (0.15); the launches traced: 3930 us -> 595 us
  local copies, waits for them, and re-layouts: 1490 us -> 8.89 us
  blocking collectives: 1210 us -> 0 us
  Pallas kernels: 0 us -> 540 us
  waiting for transfers between devices: 406 us -> 0 us
  loops' own time: 315 us -> 0 us
  other arithmetic: 258 us -> 41.6 us
  matrix products: 135 us -> 0 us
  starting transfers between devices: 89.9 us -> 0 us
    all_to_all x64 -> x0, blocking collectives: 1090 us -> none  [the longest x19 284 us: apply_table(): lax.all_to_all(block_in, 'ma', split_axis=3, concat_axis=0, tiled=True)]
    unnamed x597 -> x28, local copies, waits for them, and re-layouts: 694 us -> 4.28 us
    pallas_call x0 -> x2, Pallas kernels: none -> 540 us  [the longest x1 531 us: call_train(): pl.pallas_call(train, out_shape=(jax.ShapeDtypeStruct(spec_w.shape, F32),...]
    convert_element_type x87 -> x1, local copies, waits for them, and re-layouts: 396 us -> 0.08 us  [special(): mask.astype(F32)[None, ..., None]]
    another operation x1 -> x0, loops' own time: 315 us -> none  [legendre(): lax.scan(advance, (zero_rows, zero_rows), jnp.arange(L, dtype=jnp.float32))]
    all_to_all x90 -> x0, local copies, waits for them, and re-layouts: 293 us -> none  [the longest x24 137 us: apply_table(): lax.all_to_all(block_in, 'ma', split_axis=3, concat_axis=0, tiled=True)]
    all_to_all x20 -> x0, waiting for transfers between devices: 176 us -> none  [the longest x9 68.3 us: apply_table(): lax.all_to_all(whole_out.astype(jnp.bfloat16), 'ma', split_axis=0, concat...]
    unnamed x13 -> x0, waiting for transfers between devices: 143 us -> none
  transfers between devices with their start and end apart: 27 -> 0, of which waited for: 26 -> 0; matrix products, arithmetic and copies ran while one was open for 7% -> 0% of each run, Pallas kernels for 0% -> 0%
where the time goes in v2:
time: 595 us
  Pallas kernels  540 us (91%)
  other arithmetic  41.6 us (7%)
  local copies, waits for them, and re-layouts  8.89 us (1%)
    pallas_call x1, Pallas kernels, call_train(): pl.pallas_call(train, out_shape=(jax.ShapeDtypeStruct(spec_w.shape, F32),...  531 us

profile of v2, /device:TPU:0, one launch (start us, length us, event | category | flops | bytes accessed | tf_op | source)
XLA Modules:
  0.0 594.7 jit_solution(6199387231315830769)
XLA Ops:
  0.7 1.2 copy.70
  2.0 0.8 pad_maximum_fusion.2.x_chunks
  2.8 0.2 broadcast_in_dim.11
  3.1 0.3 pad_maximum_fusion
  3.4 0.1 copy.59
  3.6 0.1 copy.60
  3.8 0.9 pad_maximum_fusion.1.t_chunks
  4.8 0.7 pad.17.encdec
  5.5 0.6 broadcast_in_dim.12.gain
  6.1 0.6 fusion.11
  7.6 0.6 broadcast_in_dim.13.area
  8.2 0.5 pad_bitcast_fusion.var_row
  8.8 530.5 %shard_map.384 = (f32[3,6,2,256,128]{4,3,2,1,0:T(8,128)}, bf16[3,16,32,512]{3,2,1,0:T(8,128)(2,1)}, f32[16,16,256]{2,1,0:T(8,128)}, f32[8,128]{1,0:T(8,128)}) custom-call(f32[16,2,24,128]{3,2,1,0:T(8,128)} %pad_maximum_fusion.2.x_chunks, f32[16,2,2,24,128]{4,3,2,1,0:T(8,128)} %pad_maximum_fusion.1.t_chunks, f32[3,6,2,256,128]{4,3,2,1,0:T(8,128)} %spec_w.1, ...), custom_call_target="tpu_custom_call" | custom-call | tf_op jit(solution)/shard_map/pallas_call | solution.py:1043
  539.3 0.9 reduce_sum.91
  540.3 0.6 fusion.25
  542.3 1.4 multiply_reduce_fusion.5
  543.8 1.9 convert_multiply_fusion
  545.7 7.4 %multiply_reduce_fusion.1 = (f32[3,2]{1,0:T(4,128)S(1)}, f32[3,2,256,512]{3,2,1,0:T(8,128)}, f32[3,2,256,512]{3,2,1,0:T(8,128)}, f32[3,2,256,512]{3,2,1,0:T(8,128)}, f32[3,2]{1,0:T(4,128)S(1)}) fusion(f32[3,2,256,512]{3,2,1,0:T(8,128)S(1)} %copy-done, f32[]{:T(128)} %bitcast.25, f32[]{:T(128)} %bitcast.24, f32[3,2,256,512]{3,2,1,0:T(8,128)} %param.38, ...), kind=kLoop, calls=%fused_computation.11 | loop fusion | flops 13369332 | bytes 22020152 | tf_op jit(solution)/shard_map/reduce_sum | solution.py:92
  553.2 1.9 multiply_reduce_fusion.3
  555.2 0.3 multiply_reduce_fusion.4
  555.4 11.4 %multiply_reduce_fusion = (f32[3,128]{1,0:T(4,128)S(1)}, f32[3,6,2,256,128]{4,3,2,1,0:T(8,128)}, f32[3,6,2,256,128]{4,3,2,1,0:T(8,128)}, f32[3,6,2,256,128]{4,3,2,1,0:T(8,128)}) fusion(f32[3,6,2,256,128]{4,3,2,1,0:T(8,128)} %spec_w.1, f32[]{:T(128)} %bitcast.25, f32[]{:T(128)} %bitcast.24, f32[3,6,2,256,128]{4,3,2,1,0:T(8,128)} %get-tuple-element.24, ...), kind=kLoop, calls=%fused_computation.4 | loop fusion | flops 18873984 | bytes 33031692 | tf_op jit(solution)/shard_map/reduce_sum | solution.py:1168
  566.9 0.6 pad.19.value_ref
  567.5 9.4 %shard_map.385 = f32[8,128]{1,0:T(8,128)} custom-call(f32[8,128]{1,0:T(8,128)} %pad.19.value_ref), custom_call_target="tpu_custom_call" | custom-call | tf_op jit(solution)/shard_map/pallas_call | solution.py:1096
  576.9 0.8 reduce_sum.93
  577.8 0.6 maximum_maximum_fusion
  578.4 8.2 %fusion.17 = (bf16[3,6,2,256,128]{4,3,2,1,0:T(8,128)(2,1)}, f32[3,6,2,256,128]{4,3,2,1,0:T(8,128)}) fusion(f32[3,6,2,256,128]{4,3,2,1,0:T(8,128)} %spec_w.1, f32[3,6,2,256,128]{4,3,2,1,0:T(8,128)} %get-tuple-element.74, f32[3]{0:T(128)S(1)} %get-tuple-element.108), kind=kLoop, calls=%fused_computation.72 | loop fusion | flops 3538944 | bytes 16515084 | tf_op jit(solution)/shard_map/convert_element_type | solution.py:1193
  586.7 0.8 copy.66
  587.5 0.8 copy.67
  588.3 0.8 copy.68
  589.1 0.7 copy.69
  589.8 3.1 fusion.15
  592.9 0.7 fusion.14
  (46 shorter events, 0.9 us)
Async XLA Ops:
  0.7 2.1 copy-start.7
  0.7 2.4 copy-start.3
  3.4 1.4 copy-start.2
  3.5 2.0 copy-start.6
  3.6 4.7 copy-start.10
  8.8 533.6 %copy-start.8 = (f32[3,256]{1,0:T(4,128)S(1)}, f32[3,256]{1,0:T(4,128)}, u32[]{:S(2)}) copy-start(f32[3,256]{1,0:T(4,128)} %param.41) | copy-start | bytes 9220
  8.8 533.6 %copy-start.9 = (f32[3,256]{1,0:T(4,128)S(1)}, f32[3,256]{1,0:T(4,128)}, u32[]{:S(2)}) copy-start(f32[3,256]{1,0:T(4,128)} %param.40) | copy-start | bytes 9220
  539.3 6.4 %copy-start = (f32[3,2,256,512]{3,2,1,0:T(8,128)S(1)}, f32[3,2,256,512]{3,2,1,0:T(8,128)}, u32[]{:S(2)}) copy-start(f32[3,2,256,512]{3,2,1,0:T(8,128)} %mlp_w.1) | copy-start | bytes 9437188
  578.4 9.1 %copy-start.5 = (f32[2,73,256]{2,1,0:T(8,128)S(1)}, f32[2,73,256]{2,1,0:T(8,128)}, u32[]{:S(2)}) copy-start(f32[2,73,256]{2,1,0:T(8,128)} %get-tuple-element.80) | copy-start | bytes 448516
  578.4 9.9 %copy-start.4 = (f32[2,73,256]{2,1,0:T(8,128)S(1)}, f32[2,73,256]{2,1,0:T(8,128)}, u32[]{:S(2)}) copy-start(f32[2,73,256]{2,1,0:T(8,128)} %get-tuple-element.79) | copy-start | bytes 448516
  578.4 11.3 %copy-start.1 = (f32[3,2,256,512]{3,2,1,0:T(8,128)S(1)}, f32[3,2,256,512]{3,2,1,0:T(8,128)}, u32[]{:S(2)}) copy-start(f32[3,2,256,512]{3,2,1,0:T(8,128)} %get-tuple-element.82) | copy-start | bytes 9437188

commit v3 on v2

--- a/solution.py
+++ b/solution.py
@@ -607,19 +607,28 @@
     pltpu.make_async_copy(ref, ref, sem).wait()
 
 
-def push_blocks(source_of, landing, send_sem, recv_sem, zh, q):
+def flip(value, bits, span):
+    out, unit = 0, 1
+    while unit < span:
+        digit = (value // unit) % 2
+        out = out + unit * (1 - digit if bits // unit % 2 else digit)
+        unit *= 2
+    return out
+
+
+def peers_of(zh, q):
+    ranks = [flip(q, s, RANKS) for s in range(RANKS - 1, 0, -1)]
+    return [(d, device_of(zh, d)) for d in ranks]
+
+
+def push_blocks(source_of, landing, send_sem, recv_sem, peers, q):
+    for d, device in peers:
+        remote(source_of(d), landing, send_sem, recv_sem, device).start()
     pltpu.make_async_copy(source_of(q), landing, recv_sem).start()
 
-    def push(s, carry):
-        d = (q + s) % RANKS
-        remote(source_of(d), landing, send_sem, recv_sem, device_of(zh, d)).start()
-        return carry
-
-    lax.fori_loop(1, RANKS, push, 0)
-
-
-def exchange_start(send, recv, send_sem, recv_sem, zh, q):
-    push_blocks(lambda d: send.at[d], recv.at[q], send_sem, recv_sem, zh, q)
+
+def exchange_start(send, recv, send_sem, recv_sem, peers, q):
+    push_blocks(lambda d: send.at[d], recv.at[q], send_sem, recv_sem, peers, q)
 
 
 def exchange_wait(send, recv, send_sem, recv_sem):
@@ -627,8 +636,8 @@
     bytes_wait(send.at[pl.ds(0, RANKS - 1)], send_sem)
 
 
-def exchange(send, recv, send_sem, recv_sem, zh, q):
-    exchange_start(send, recv, send_sem, recv_sem, zh, q)
+def exchange(send, recv, send_sem, recv_sem, peers, q):
+    exchange_start(send, recv, send_sem, recv_sem, peers, q)
     exchange_wait(send, recv, send_sem, recv_sem)
 
 
@@ -649,6 +658,7 @@
     g_send_sem, g_recv_sem, rs_sem, mir_send_sem, mir_recv_sem, ag_send_sem, ag_recv_sem, sm_sem,
 ):
     zh, y, w, q = place()
+    peers = peers_of(zh, q)
     ma = lax.axis_index("ma")
     xc = ma % 4
     mirror_ma = 4 * (3 - ma // 4) + xc
@@ -698,16 +708,19 @@
     greet_all()
 
     def chunk_to(chunks, landing, sems):
+        for bits in range(RANKS - 1, 0, -1):
+            other = flip(ma, bits, RANKS)
+            remote(chunks.at[other], landing, sems[0], sems[1], {"lat": y, "ma": other}).start()
         pltpu.make_async_copy(chunks.at[ma], landing, sems[1]).start()
 
-        def push(s, carry):
-            other = (ma + s) % RANKS
-            remote(chunks.at[other], landing, sems[0], sems[1], {"lat": y, "ma": other}).start()
-            return carry
-
-        lax.fori_loop(1, RANKS, push, 0)
-
     chunk_to(x_chunks, x_recv.at[:, ma], (once_send.at[0], once_recv.at[0]))
+
+    def weights_out(b, where, triple):
+        source, piece, device = {
+            "near": (w_other, 1, near), "far": (w_all.at[:, 0], 2, far), "cross": (w_other, 3, cross)
+        }[where]
+        for t in triple:
+            remote(source.at[b, t], w_all.at[b, piece, t], w_send_sem.at[b], w_recv_sem.at[b], device).start()
 
     for b in range(NB):
         spec_loads[b].wait()
@@ -718,16 +731,14 @@
                 target[t] = value.astype(BF16)
         if b + 2 < NB:
             spec_loads[b + 2].start()
-        sems = (w_send_sem.at[b], w_recv_sem.at[b])
-        remote(w_other.at[b], w_all.at[b, 3], *sems, cross).start()
-        remote(w_all.at[b, 0], w_all.at[b, 2], *sems, far).start()
-        remote(w_other.at[b], w_all.at[b, 1], *sems, near).start()
         if b == 0:
+            weights_out(0, "far", range(third))
+            weights_out(0, "cross", range(third))
+            weights_out(0, "near", range(third))
             mlp_loads[0].start()
             mlp_loads[1].start()
             for k in (1, 2, 3, 5, 6, 7):
                 loads[k].start()
-    chunk_to(t_chunks, goals.at[:, :, ma], (once_send.at[1], once_recv.at[1]))
     for b in range(NB):
         mlp_loads[b].wait()
         mlp_bf[b] = mlp_stage[b % 2].astype(BF16)
@@ -764,9 +775,29 @@
 
         rows_loop(pixels, 128, norm_rows)
         n_send[...] = narrow(nn(ftx[...], u_buf[...]))
-        exchange(n_send, s_recv, x_send.at[0], x_recv_sem.at[0], zh, q)
+        exchange_start(n_send, s_recv, x_send.at[0], x_recv_sem.at[0], peers, q)
+
+        @pl.when(jnp.logical_and(step == 0, block > 0))
+        def _():
+            weights_out(block, "near", (2,))
+
+        @pl.when(jnp.logical_and(step == 1, block == 0))
+        def _():
+            chunk_to(t_chunks.at[1], goals.at[1, :, ma], (once_send.at[2], once_recv.at[2]))
+
+        exchange_wait(n_send, s_recv, x_send.at[0], x_recv_sem.at[0])
         w_send[...] = broad(nn(pfx[...], s_recv[...].reshape(spectra, chans)))
-        exchange(w_send, a_own.at[idx], x_send.at[1], x_recv_sem.at[1], zh, q)
+        exchange_start(w_send, a_own.at[idx], x_send.at[1], x_recv_sem.at[1], peers, q)
+
+        @pl.when(jnp.logical_and(step == 0, block < NB - 1))
+        def _():
+            weights_out(block + 1, "far", (0, 1))
+
+        @pl.when(jnp.logical_and(step == 0, block == NB - 1))
+        def _():
+            chunk_to(t_chunks.at[0], goals.at[0, :, ma], (once_send.at[1], once_recv.at[1]))
+
+        exchange_wait(w_send, a_own.at[idx], x_send.at[1], x_recv_sem.at[1])
 
         @pl.when(step == 0)
         def _():
@@ -777,9 +808,24 @@
             by_real, by_imag = (mixed_by(coef, nn, block, t, part) for part in range(2))
             mixed = jnp.stack([by_real[:, 0] - by_imag[:, 1], by_real[:, 1] + by_imag[:, 0]], 1)
             w_send[:, t] = mixed.reshape(RANKS, 2 * SLOTS, chans).astype(BF16)
-        exchange(w_send, b_recv, x_send.at[2], x_recv_sem.at[2], zh, q)
+        exchange_start(w_send, b_recv, x_send.at[2], x_recv_sem.at[2], peers, q)
+
+        @pl.when(jnp.logical_and(step == 0, block < NB - 1))
+        def _():
+            weights_out(block + 1, "far", (2,))
+            weights_out(block + 1, "cross", (0,))
+            weights_out(block + 1, "near", (0,))
+
+        exchange_wait(w_send, b_recv, x_send.at[2], x_recv_sem.at[2])
         n_send[...] = narrow(nn(pix[...], b_recv[...].reshape(triples, chans)))
-        exchange(n_send, y_recv, x_send.at[3], x_recv_sem.at[3], zh, q)
+        exchange_start(n_send, y_recv, x_send.at[3], x_recv_sem.at[3], peers, q)
+
+        @pl.when(jnp.logical_and(step == 0, block < NB - 1))
+        def _():
+            weights_out(block + 1, "cross", (1, 2))
+            weights_out(block + 1, "near", (1,))
+
+        exchange_wait(n_send, y_recv, x_send.at[3], x_recv_sem.at[3])
         spectrum = y_recv[...].reshape(spectra, chans)
 
         def mlp_rows(rows):
@@ -812,12 +858,17 @@
 
         @pl.when(step == 0)
         def _():
-            bytes_wait(goals, once_recv.at[1])
-            bytes_wait(t_chunks.at[pl.ds(0, RANKS - 1)], once_send.at[1])
+            bytes_wait(goals.at[0], once_recv.at[1])
+            bytes_wait(t_chunks.at[0, pl.ds(0, RANKS - 1)], once_send.at[1])
             for il in range(2):
                 valid = goals[0, il].reshape(pixels // 2, LANES)[:, MASK_LANE:]
                 rows = slice(il * pixels // 2, (il + 1) * pixels // 2)
                 weight[rows, :] = valid * (area[il] * var_row[...])
+
+        @pl.when(step == 1)
+        def _():
+            bytes_wait(goals.at[1], once_recv.at[2])
+            bytes_wait(t_chunks.at[1, pl.ds(0, RANKS - 1)], once_send.at[2])
 
         miss = prediction - goals[step].reshape(pixels, LANES)
         weighted = weight[...] * miss
@@ -840,7 +891,37 @@
                 scal[1:2] += lane_sums(total * total)
                 g_spec[block, third * own + t] = total
 
+    def shares_start(block):
+        rs_send[...] = dmlp[block].astype(BF16).reshape(rs_send.shape)
+        exchange_start(rs_send, rs_recv, rs_sem.at[0], rs_sem.at[1], peers, q)
+
+    def shares_finish(block):
+        exchange_wait(rs_send, rs_recv, rs_sem.at[0], rs_sem.at[1])
+        share = rs_recv[0].astype(F32)
+        for k in range(1, RANKS):
+            share = share + rs_recv[k].astype(F32)
+        mir_send[block] = share
+        remote(mir_send.at[block], mir_recv.at[block], mir_send_sem.at[block], mir_recv_sem.at[block], far).start()
+
+    def shares_spread(block):
+        bytes_wait(mir_recv.at[block], mir_recv_sem.at[block])
+        total = mir_send[block] + mir_recv[block]
+        scal[1:2] += 0.5 * lane_sums(total * total)
+        ag_src[block] = total.astype(BF16)
+        push_blocks(
+            lambda d: ag_src.at[block], g_mlp.at[block, q], ag_send_sem.at[block], ag_recv_sem.at[block], peers, q
+        )
+
+    def grads_out(b, where, triple):
+        piece, device = {"near": (0, near), "far": (1, far), "cross": (2, cross)}[where]
+        for t in triple:
+            remote(
+                dw_send.at[b, piece, t], dw_recv.at[b, piece, t], g_send_sem.at[b], g_recv_sem.at[b], device
+            ).start()
+
     def bwd_block(lap, step, block):
+        early = jnp.logical_and(lap == 1, block > 0)
+        later = jnp.logical_and(lap == 1, block < NB - 1)
         slot, idx = 4 * step + block, NB * step + block
         gain_row = gain[block]
 
@@ -867,26 +948,23 @@
 
         rows_loop(pixels, 256, mlp_rows)
         n_send[...] = narrow(nn(itxt[...], u_buf[...]))
-        exchange_start(n_send, s_recv, x_send.at[4], x_recv_sem.at[4], zh, q)
-
-        @pl.when(lap == 1)
-        def _():
-            rs_send[...] = dmlp[block].astype(BF16).reshape(rs_send.shape)
-            exchange_start(rs_send, rs_recv, rs_sem.at[0], rs_sem.at[1], zh, q)
+        exchange_start(n_send, s_recv, x_send.at[4], x_recv_sem.at[4], peers, q)
+
+        @pl.when(later)
+        def _():
+            grads_out(block + 1, "cross", (1,))
+            grads_out(block + 1, "near", (1,))
 
         exchange_wait(n_send, s_recv, x_send.at[4], x_recv_sem.at[4])
         w_send[...] = broad(nn(pixt[...], s_recv[...].reshape(spectra, chans)))
         which = NB * lap + block
-        exchange_start(w_send, d_mix.at[which], x_send.at[5], x_recv_sem.at[5], zh, q)
-
-        @pl.when(lap == 1)
-        def _():
-            exchange_wait(rs_send, rs_recv, rs_sem.at[0], rs_sem.at[1])
-            share = rs_recv[0].astype(F32)
-            for k in range(1, RANKS):
-                share = share + rs_recv[k].astype(F32)
-            mir_send[block] = share
-            remote(mir_send.at[block], mir_recv.at[block], mir_send_sem.at[block], mir_recv_sem.at[block], far).start()
+        exchange_start(w_send, d_mix.at[which], x_send.at[5], x_recv_sem.at[5], peers, q)
+
+        @pl.when(jnp.logical_and(lap == 1, block < NB - 1))
+        def _():
+            grads_out(block + 1, "cross", (2,))
+            grads_out(block + 1, "near", (2,))
+            shares_finish(block + 1)
 
         exchange_wait(w_send, d_mix.at[which], x_send.at[5], x_recv_sem.at[5])
 
@@ -899,7 +977,7 @@
             by_real, by_imag = (mixed_by(d_mixed, nt, block, t, part) for part in range(2))
             d_coef = jnp.stack([by_real[:, 0] + by_imag[:, 1], by_real[:, 1] - by_imag[:, 0]], 1)
             w_send[:, t] = d_coef.reshape(RANKS, 2 * SLOTS, chans).astype(BF16)
-        exchange_start(w_send, b_recv, x_send.at[6], x_recv_sem.at[6], zh, q)
+        exchange_start(w_send, b_recv, x_send.at[6], x_recv_sem.at[6], peers, q)
 
         @pl.when(lap == 1)
         def _():
@@ -925,19 +1003,34 @@
             dw_own[block] = dwf[0]
             for k in range(3):
                 dw_send[block, k] = dwf[1 + k].astype(BF16)
-            sems = (g_send_sem.at[block], g_recv_sem.at[block])
-            remote(dw_send.at[block, 2], dw_recv.at[block, 2], *sems, cross).start()
-            remote(dw_send.at[block, 1], dw_recv.at[block, 1], *sems, far).start()
-            remote(dw_send.at[block, 0], dw_recv.at[block, 0], *sems, near).start()
-            bytes_wait(mir_recv.at[block], mir_recv_sem.at[block])
-            total = mir_send[block] + mir_recv[block]
-            scal[1:2] += 0.5 * lane_sums(total * total)
-            ag_src[block] = total.astype(BF16)
-            push_blocks(lambda d: ag_src.at[block], g_mlp.at[block, q], ag_send_sem.at[block], ag_recv_sem.at[block], zh, q)
+
+            grads_out(block, "far", (0, 1))
+
+        @pl.when(jnp.logical_and(lap == 1, block == 0))
+        def _():
+            grads_out(block, "far", (2,))
+            grads_out(block, "cross", range(third))
 
         exchange_wait(w_send, b_recv, x_send.at[6], x_recv_sem.at[6])
         n_send[...] = narrow(nn(pfxt[...], b_recv[...].reshape(triples, chans)))
-        exchange(n_send, y_recv, x_send.at[7], x_recv_sem.at[7], zh, q)
+        exchange_start(n_send, y_recv, x_send.at[7], x_recv_sem.at[7], peers, q)
+
+        @pl.when(early)
+        def _():
+            grads_out(block, "far", (2,))
+            grads_out(block, "cross", (0,))
+            grads_out(block, "near", (0,))
+
+        @pl.when(jnp.logical_and(lap == 1, block == 0))
+        def _():
+            grads_out(block, "near", range(third))
+
+        exchange_wait(n_send, y_recv, x_send.at[7], x_recv_sem.at[7])
+
+        @pl.when(lap == 1)
+        def _():
+            shares_start(block)
+
         spectrum = y_recv[...].reshape(spectra, chans)
 
         def norm_rows(rows):
@@ -984,7 +1077,11 @@
     for b in range(NB):
         d_small[LANES - NB + b : LANES - NB + b + 1] = d_gain[b]
     sm_send[...] = d_small[...].reshape(sm_send.shape)
-    exchange(sm_send, sm_recv, sm_sem.at[0], sm_sem.at[1], zh, q)
+    exchange_start(sm_send, sm_recv, sm_sem.at[0], sm_sem.at[1], peers, q)
+    for b in range(NB - 1, 0, -1):
+        shares_spread(b)
+    shares_finish(0)
+    exchange_wait(sm_send, sm_recv, sm_sem.at[0], sm_sem.at[1])
     share = sm_recv[0]
     for k in range(1, RANKS):
         share = share + sm_recv[k]
@@ -995,7 +1092,8 @@
     total = sm_mir_send[...] + sm_mir_recv[...]
     scal[1:2] += 0.5 * lane_sums(total * total)
     sm_src[...] = total
-    push_blocks(lambda d: sm_src, g_small.at[q], sm_sem.at[4], sm_sem.at[5], zh, q)
+    push_blocks(lambda d: sm_src, g_small.at[q], sm_sem.at[4], sm_sem.at[5], peers, q)
+    shares_spread(0)
     settle(0)
 
     me = RANKS * y + ma
@@ -1063,7 +1161,7 @@
             b16(RANKS, *chunk), b16(RANKS, *chunk), f32(NB, *chunk), f32(NB, *chunk), b16(NB, *chunk),
             f32(2 * LANES, chans), f32(NB, 1, chans), f32(RANKS, *small), f32(RANKS, *small), f32(*small), f32(*small),
             f32(*small), f32(8, LANES), f32(2 * RANKS, 8, LANES),
-            dma((8,)), dma((3 * NB,)), dma((2,)), dma((2,)), dma((NB,)), dma((NB,)), dma((8,)), dma((8,)),
+            dma((8,)), dma((3 * NB,)), dma((3,)), dma((3,)), dma((NB,)), dma((NB,)), dma((8,)), dma((8,)),
             dma((NB,)), dma((NB,)), dma((2,)), dma((NB,)), dma((NB,)), dma((NB,)), dma((NB,)), dma((8,)),
         ],
         compiler_params=pltpu.CompilerParams(
@@ -1142,7 +1240,7 @@
     x_chunks = chunks_of(jnp.pad(inputs, ((0, 0),) * 3 + ((0, spare),)))
     masks = jnp.broadcast_to(mask.astype(F32)[None, ..., None], (*targets.shape[:-1], 1))
     goal = jnp.concatenate([targets, jnp.zeros((*targets.shape[:-1], spare - 1), F32), masks], -1)
-    t_chunks = jnp.stack([chunks_of(goal[0]), chunks_of(goal[1])], 1)
+    t_chunks = jnp.stack([chunks_of(goal[0]), chunks_of(goal[1])], 0)
     angles = (jnp.arange(nlat, dtype=F32) + 0.5) * (math.pi / nlat)
     sines = jnp.sin(angles)
     area = lax.dynamic_slice_in_dim(sines / jnp.mean(sines), 2 * q, 2)

time: 595 us -> 559 us (0.939)
  Pallas kernels: 540 us -> 504 us
    pallas_call x1, Pallas kernels: 531 us -> 495 us  [call_train(): pl.pallas_call(train, out_shape=(jax.ShapeDtypeStruct(spec_w.shape, F32),...]
where the time goes in v3:
time: 559 us; the launch traced here: 558 us
  Pallas kernels  504 us (90%)
  other arithmetic  41.6 us (7%)
  local copies, waits for them, and re-layouts  8.89 us (2%)
    pallas_call x1, Pallas kernels, call_train(): pl.pallas_call(train, out_shape=(jax.ShapeDtypeStruct(spec_w.shape, F32),...  495 us
    reduce_sum x1, other arithmetic, special(): dir_part = jnp.sum(direction * direction, axis=(1, 2, 3))  11.2 us

profile of v3, /device:TPU:0, one launch (start us, length us, event | category | flops | bytes accessed | tf_op | source)
XLA Modules:
  0.0 558.4 jit_solution(12525776752919379536)
XLA Ops:
  0.7 1.2 copy.70
  2.0 0.8 pad_maximum_fusion.2.x_chunks
  2.8 0.2 broadcast_in_dim.11
  3.1 0.3 pad_maximum_fusion
  3.4 0.1 copy.59
  3.6 0.1 copy.60
  3.8 0.9 pad_maximum_fusion.1.t_chunks
  4.8 0.7 pad.17.encdec
  5.5 0.6 broadcast_in_dim.12.gain
  6.1 0.6 fusion.11
  7.6 0.6 broadcast_in_dim.13.area
  8.2 0.5 pad_bitcast_fusion.var_row
  8.8 494.6 %shard_map.384 = (f32[3,6,2,256,128]{4,3,2,1,0:T(8,128)}, bf16[3,16,32,512]{3,2,1,0:T(8,128)(2,1)}, f32[16,16,256]{2,1,0:T(8,128)}, f32[8,128]{1,0:T(8,128)}) custom-call(f32[16,2,24,128]{3,2,1,0:T(8,128)} %pad_maximum_fusion.2.x_chunks, f32[2,16,2,24,128]{4,3,2,1,0:T(8,128)} %pad_maximum_fusion.1.t_chunks, f32[3,6,2,256,128]{4,3,2,1,0:T(8,128)} %spec_w.1, ...), custom_call_target="tpu_custom_call" | custom-call | tf_op jit(solution)/shard_map/pallas_call | solution.py:1141
  503.3 0.9 reduce_sum.91
  504.3 0.6 fusion.25
  506.4 1.4 multiply_reduce_fusion.5
  507.8 1.9 convert_multiply_fusion
  509.7 7.6 %multiply_reduce_fusion.1 = (f32[3,2]{1,0:T(4,128)S(1)}, f32[3,2,256,512]{3,2,1,0:T(8,128)}, f32[3,2,256,512]{3,2,1,0:T(8,128)}, f32[3,2,256,512]{3,2,1,0:T(8,128)}, f32[3,2]{1,0:T(4,128)S(1)}) fusion(f32[3,2,256,512]{3,2,1,0:T(8,128)S(1)} %copy-done, f32[]{:T(128)} %bitcast.25, f32[]{:T(128)} %bitcast.24, f32[3,2,256,512]{3,2,1,0:T(8,128)} %param.38, ...), kind=kLoop, calls=%fused_computation.11 | loop fusion | flops 13369332 | bytes 22020152 | tf_op jit(solution)/shard_map/reduce_sum | solution.py:92
  517.4 1.9 multiply_reduce_fusion.3
  519.4 0.3 multiply_reduce_fusion.4
  519.6 11.2 %multiply_reduce_fusion = (f32[3,128]{1,0:T(4,128)S(1)}, f32[3,6,2,256,128]{4,3,2,1,0:T(8,128)}, f32[3,6,2,256,128]{4,3,2,1,0:T(8,128)}, f32[3,6,2,256,128]{4,3,2,1,0:T(8,128)}) fusion(f32[3,6,2,256,128]{4,3,2,1,0:T(8,128)} %spec_w.1, f32[]{:T(128)} %bitcast.25, f32[]{:T(128)} %bitcast.24, f32[3,6,2,256,128]{4,3,2,1,0:T(8,128)} %get-tuple-element.24, ...), kind=kLoop, calls=%fused_computation.4 | loop fusion | flops 18873984 | bytes 33031692 | tf_op jit(solution)/shard_map/reduce_sum | solution.py:1266
  530.9 0.6 pad.19.value_ref
  531.5 9.1 %shard_map.385 = f32[8,128]{1,0:T(8,128)} custom-call(f32[8,128]{1,0:T(8,128)} %pad.19.value_ref), custom_call_target="tpu_custom_call" | custom-call | tf_op jit(solution)/shard_map/pallas_call | solution.py:1194
  540.6 0.8 reduce_sum.93
  541.5 0.6 maximum_maximum_fusion
  542.1 8.2 %fusion.17 = (bf16[3,6,2,256,128]{4,3,2,1,0:T(8,128)(2,1)}, f32[3,6,2,256,128]{4,3,2,1,0:T(8,128)}) fusion(f32[3,6,2,256,128]{4,3,2,1,0:T(8,128)} %spec_w.1, f32[3,6,2,256,128]{4,3,2,1,0:T(8,128)} %get-tuple-element.74, f32[3]{0:T(128)S(1)} %get-tuple-element.108), kind=kLoop, calls=%fused_computation.72 | loop fusion | flops 3538944 | bytes 16515084 | tf_op jit(solution)/shard_map/convert_element_type | solution.py:1291
  550.4 0.8 copy.66
  551.2 0.8 copy.67
  552.0 0.8 copy.68
  552.8 0.7 copy.69
  553.5 3.1 fusion.15
  556.6 0.7 fusion.14
  (46 shorter events, 0.9 us)
Async XLA Ops:
  0.7 2.1 copy-start.7
  0.7 2.4 copy-start.3
  3.4 1.4 copy-start.2
  3.5 2.0 copy-start.6
  3.6 4.7 copy-start.10
  8.7 497.6 %copy-start.8 = (f32[3,256]{1,0:T(4,128)S(1)}, f32[3,256]{1,0:T(4,128)}, u32[]{:S(2)}) copy-start(f32[3,256]{1,0:T(4,128)} %param.41) | copy-start | bytes 9220
  8.7 497.6 %copy-start.9 = (f32[3,256]{1,0:T(4,128)S(1)}, f32[3,256]{1,0:T(4,128)}, u32[]{:S(2)}) copy-start(f32[3,256]{1,0:T(4,128)} %param.40) | copy-start | bytes 9220
  503.3 6.4 %copy-start = (f32[3,2,256,512]{3,2,1,0:T(8,128)S(1)}, f32[3,2,256,512]{3,2,1,0:T(8,128)}, u32[]{:S(2)}) copy-start(f32[3,2,256,512]{3,2,1,0:T(8,128)} %mlp_w.1) | copy-start | bytes 9437188
  542.1 9.1 %copy-start.5 = (f32[2,73,256]{2,1,0:T(8,128)S(1)}, f32[2,73,256]{2,1,0:T(8,128)}, u32[]{:S(2)}) copy-start(f32[2,73,256]{2,1,0:T(8,128)} %get-tuple-element.80) | copy-start | bytes 448516
  542.1 9.9 %copy-start.4 = (f32[2,73,256]{2,1,0:T(8,128)S(1)}, f32[2,73,256]{2,1,0:T(8,128)}, u32[]{:S(2)}) copy-start(f32[2,73,256]{2,1,0:T(8,128)} %get-tuple-element.79) | copy-start | bytes 448516
  542.1 11.3 %copy-start.1 = (f32[3,2,256,512]{3,2,1,0:T(8,128)S(1)}, f32[3,2,256,512]{3,2,1,0:T(8,128)}, u32[]{:S(2)}) copy-start(f32[3,2,256,512]{3,2,1,0:T(8,128)} %get-tuple-element.82) | copy-start | bytes 9437188

commit v4 on v3

--- a/solution.py
+++ b/solution.py
@@ -575,9 +575,10 @@
 MESH = pl.DeviceIdType.MESH
 LANES = 128
 MASK_LANE = LANES - 1
-
-
-def greet_all():
+VAR_ROW, FIRST_ROW, SECOND_ROW = 124, 123, 122
+
+
+def greet_all(between=None):
     barrier = pltpu.get_barrier_semaphore()
     me = 2 * RANKS // 2 * lax.axis_index("lat") + lax.axis_index("ma")
 
@@ -589,6 +590,8 @@
         return carry
 
     lax.fori_loop(1, 2 * RANKS, greet, 0)
+    if between is not None:
+        between()
     pl.semaphore_wait(barrier, 2 * RANKS - 1)
 
 
@@ -646,16 +649,18 @@
 
 
 def train(
-    x_chunks, t_chunks, spec_w, mlp_w, r0, r1, r2, r3, f0, f1, f2, f3,
-    encdec, gain, area, var_row,
+    xb_chunks, x_chunks, t_chunks, spec_w, spec_m, spec_v, mlp_w, mlp_m, mlp_v, r0, r1, r2, r3, f0, f1, f2, f3,
+    small, area,
     g_spec, g_mlp, g_small, scalars,
-    pfx, pix, pfxt, pixt, ftx, itx, ftxt, itxt, w_all, w_other, mlp_bf, mlp_stage, code_bf,
+    pfx, pix, pfxt, pixt, ftx, itx, ftxt, itxt, w_all, mlp_bf, mlp_stage, code_bf,
     x_recv, goals, weight, x_low, misfit, d_state, h_all, hid_low, v_low, u_buf, dv_buf, dh_buf,
     n_send, s_recv, y_recv, w_send, b_recv, a_own, d_mix,
     dwf, dw_send, dw_recv, dw_own, dmlp, rs_send, rs_recv, mir_send, mir_recv, ag_src,
     d_small, d_gain, sm_send, sm_recv, sm_mir_send, sm_mir_recv, sm_src, scal, scal_recv,
+    ml_buf, dirs, dirs_recv,
     load_sem, stage_sem, once_send, once_recv, w_send_sem, w_recv_sem, x_send, x_recv_sem,
     g_send_sem, g_recv_sem, rs_sem, mir_send_sem, mir_recv_sem, ag_send_sem, ag_recv_sem, sm_sem,
+    lamb_sem, ml_sem,
 ):
     zh, y, w, q = place()
     peers = peers_of(zh, q)
@@ -699,13 +704,14 @@
     spec_loads[0].start()
     spec_loads[1].start()
     loads[4].start()
-    loads[0].start()
     scal[...] = jnp.zeros_like(scal)
     d_small[...] = jnp.zeros_like(d_small)
     d_gain[...] = jnp.zeros_like(d_gain)
     d_state[...] = jnp.zeros_like(d_state)
-    code_bf[...] = encdec[...].astype(BF16)
-    greet_all()
+    dirs[...] = jnp.zeros_like(dirs)
+    kept_rows = lax.broadcasted_iota(jnp.int32, (LANES, 1), 0) < C
+    for k in range(2):
+        code_bf[k] = jnp.where(kept_rows, small[k], 0.0).astype(BF16)
 
     def chunk_to(chunks, landing, sems):
         for bits in range(RANKS - 1, 0, -1):
@@ -713,32 +719,38 @@
             remote(chunks.at[other], landing, sems[0], sems[1], {"lat": y, "ma": other}).start()
         pltpu.make_async_copy(chunks.at[ma], landing, sems[1]).start()
 
-    chunk_to(x_chunks, x_recv.at[:, ma], (once_send.at[0], once_recv.at[0]))
-
     def weights_out(b, where, triple):
         source, piece, device = {
-            "near": (w_other, 1, near), "far": (w_all.at[:, 0], 2, far), "cross": (w_other, 3, cross)
+            "near": (dw_send, 1, near), "far": (w_all, 2, far), "cross": (dw_send, 3, cross)
         }[where]
         for t in triple:
-            remote(source.at[b, t], w_all.at[b, piece, t], w_send_sem.at[b], w_recv_sem.at[b], device).start()
-
-    for b in range(NB):
+            remote(source.at[b, 0, t], w_all.at[b, piece, t], w_send_sem.at[b], w_recv_sem.at[b], device).start()
+
+    def cast_weights(b):
         spec_loads[b].wait()
         for t in range(third):
-            for own, target in ((y, w_all.at[b, 0]), (1 - y, w_other.at[b])):
+            for own, target in ((y, w_all.at[b, 0]), (1 - y, dw_send.at[b, 0])):
                 value = stage[2 * (b % 2) + own, t]
                 scal[2 + b : 3 + b] += lane_sums(value * value)
                 target[t] = value.astype(BF16)
         if b + 2 < NB:
             spec_loads[b + 2].start()
-        if b == 0:
-            weights_out(0, "far", range(third))
-            weights_out(0, "cross", range(third))
-            weights_out(0, "near", range(third))
-            mlp_loads[0].start()
-            mlp_loads[1].start()
-            for k in (1, 2, 3, 5, 6, 7):
-                loads[k].start()
+
+    def first_weights():
+        cast_weights(0)
+        loads[0].start()
+        mlp_loads[0].start()
+        mlp_loads[1].start()
+        for k in (1, 2, 3, 5, 6, 7):
+            loads[k].start()
+
+    greet_all(first_weights)
+    chunk_to(xb_chunks, x_low.at[0, :, ma], (once_send.at[0], once_recv.at[0]))
+    weights_out(0, "far", range(third))
+    weights_out(0, "cross", range(third))
+    weights_out(0, "near", range(third))
+    for b in range(1, NB):
+        cast_weights(b)
     for b in range(NB):
         mlp_loads[b].wait()
         mlp_bf[b] = mlp_stage[b % 2].astype(BF16)
@@ -746,8 +758,16 @@
             mlp_loads[b + 2].start()
     for copy in loads:
         copy.wait()
-    bytes_wait(x_recv, once_recv.at[0])
-    bytes_wait(x_chunks.at[pl.ds(0, RANKS - 1)], once_send.at[0])
+    share_rows = pl.ds(pl.multiple_of((q % (RANKS // 2)) * ml_buf.shape[2], ml_buf.shape[2]), ml_buf.shape[2])
+    ml_loads = [
+        pltpu.make_async_copy(array.at[b, q // (RANKS // 2), share_rows], ml_buf.at[k, b], ml_sem)
+        for k, array in enumerate((mlp_w, mlp_m, mlp_v))
+        for b in range(NB)
+    ]
+    for copy in ml_loads:
+        copy.start()
+    bytes_wait(x_low.at[0], once_recv.at[0])
+    bytes_wait(xb_chunks.at[pl.ds(0, RANKS - 1)], once_send.at[0])
 
     hi = hi_rows(w)
     rows_mix = RANKS * 2 * SLOTS
@@ -767,13 +787,13 @@
 
     def fwd_block(step, block):
         slot, idx = 4 * step + block, NB * step + block
-        gain_row = gain[block]
+        gain_row = small[0, pl.ds(LANES - NB + block, 1), :]
 
         def norm_rows(rows):
             normal, unused = normal_of(h_all[slot, rows, :])
             u_buf[rows, :] = (normal * gain_row).astype(BF16)
 
-        rows_loop(pixels, 128, norm_rows)
+        rows_loop(pixels, 256, norm_rows)
         n_send[...] = narrow(nn(ftx[...], u_buf[...]))
         exchange_start(n_send, s_recv, x_send.at[0], x_recv_sem.at[0], peers, q)
 
@@ -795,6 +815,7 @@
 
         @pl.when(jnp.logical_and(step == 0, block == NB - 1))
         def _():
+            chunk_to(x_chunks, x_recv.at[:, ma], (once_send.at[3], once_recv.at[3]))
             chunk_to(t_chunks.at[0], goals.at[0, :, ma], (once_send.at[1], once_recv.at[1]))
 
         exchange_wait(w_send, a_own.at[idx], x_send.at[1], x_recv_sem.at[1])
@@ -841,10 +862,7 @@
     denom = float(pixels * RANKS * C * 2)
 
     def fwd_step(step, carry):
-        state = x_recv[...].reshape(pixels, LANES)
-        state_low = state.astype(BF16)
-        x_low[step] = state_low
-        h_all[4 * step] = nn(state_low, code_bf[0])
+        h_all[4 * step] = nn(x_low[step].reshape(pixels, LANES), code_bf[0])
 
         def one(block, inner):
             fwd_block(step, block)
@@ -853,22 +871,30 @@
         lax.fori_loop(0, NB, one, 0)
         hidden_low = h_all[4 * step + 3].astype(BF16)
         hid_low[step] = hidden_low
-        prediction = state + nt(hidden_low, code_bf[1])
-        x_recv[...] = prediction.reshape(x_recv.shape)
+        delta = nt(hidden_low, code_bf[1])
 
         @pl.when(step == 0)
         def _():
+            bytes_wait(x_recv, once_recv.at[3])
+            bytes_wait(x_chunks.at[pl.ds(0, RANKS - 1)], once_send.at[3])
             bytes_wait(goals.at[0], once_recv.at[1])
             bytes_wait(t_chunks.at[0, pl.ds(0, RANKS - 1)], once_send.at[1])
             for il in range(2):
                 valid = goals[0, il].reshape(pixels // 2, LANES)[:, MASK_LANE:]
                 rows = slice(il * pixels // 2, (il + 1) * pixels // 2)
-                weight[rows, :] = valid * (area[il] * var_row[...])
+                weight[rows, :] = valid * (area[q, il] * small[1, VAR_ROW : VAR_ROW + 1, :LANES])
 
         @pl.when(step == 1)
         def _():
             bytes_wait(goals.at[1], once_recv.at[2])
             bytes_wait(t_chunks.at[1, pl.ds(0, RANKS - 1)], once_send.at[2])
+
+        prediction = x_recv[...].reshape(pixels, LANES) + delta
+        x_recv[...] = prediction.reshape(x_recv.shape)
+
+        @pl.when(step == 0)
+        def _():
+            x_low[1] = prediction.astype(BF16).reshape(x_low.shape[1:])
 
         miss = prediction - goals[step].reshape(pixels, LANES)
         weighted = weight[...] * miss
@@ -923,7 +949,7 @@
         early = jnp.logical_and(lap == 1, block > 0)
         later = jnp.logical_and(lap == 1, block < NB - 1)
         slot, idx = 4 * step + block, NB * step + block
-        gain_row = gain[block]
+        gain_row = small[0, pl.ds(LANES - NB + block, 1), :]
 
         @pl.when(lap == 0)
         def _():
@@ -954,6 +980,7 @@
         def _():
             grads_out(block + 1, "cross", (1,))
             grads_out(block + 1, "near", (1,))
+            shares_finish(block + 1)
 
         exchange_wait(n_send, s_recv, x_send.at[4], x_recv_sem.at[4])
         w_send[...] = broad(nn(pixt[...], s_recv[...].reshape(spectra, chans)))
@@ -964,7 +991,6 @@
         def _():
             grads_out(block + 1, "cross", (2,))
             grads_out(block + 1, "near", (2,))
-            shares_finish(block + 1)
 
         exchange_wait(w_send, d_mix.at[which], x_send.at[5], x_recv_sem.at[5])
 
@@ -978,6 +1004,10 @@
             d_coef = jnp.stack([by_real[:, 0] + by_imag[:, 1], by_real[:, 1] - by_imag[:, 0]], 1)
             w_send[:, t] = d_coef.reshape(RANKS, 2 * SLOTS, chans).astype(BF16)
         exchange_start(w_send, b_recv, x_send.at[6], x_recv_sem.at[6], peers, q)
+
+        @pl.when(jnp.logical_and(lap == 1, block == 0))
+        def _():
+            shares_start(block)
 
         @pl.when(lap == 1)
         def _():
@@ -1009,7 +1039,6 @@
         @pl.when(jnp.logical_and(lap == 1, block == 0))
         def _():
             grads_out(block, "far", (2,))
-            grads_out(block, "cross", range(third))
 
         exchange_wait(w_send, b_recv, x_send.at[6], x_recv_sem.at[6])
         n_send[...] = narrow(nn(pfxt[...], b_recv[...].reshape(triples, chans)))
@@ -1027,9 +1056,13 @@
 
         exchange_wait(n_send, y_recv, x_send.at[7], x_recv_sem.at[7])
 
-        @pl.when(lap == 1)
+        @pl.when(early)
         def _():
             shares_start(block)
+
+        @pl.when(jnp.logical_and(lap == 1, block == 0))
+        def _():
+            shares_finish(block)
 
         spectrum = y_recv[...].reshape(spectra, chans)
 
@@ -1064,7 +1097,7 @@
 
         lax.fori_loop(0, NB, one, 0)
         d_enc = dh_buf[...].astype(BF16)
-        d_small[:LANES] += tn(x_low[step], d_enc)
+        d_small[:LANES] += tn(x_low[step].reshape(pixels, LANES), d_enc)
 
         @pl.when(lap == 0)
         def _():
@@ -1080,7 +1113,6 @@
     exchange_start(sm_send, sm_recv, sm_sem.at[0], sm_sem.at[1], peers, q)
     for b in range(NB - 1, 0, -1):
         shares_spread(b)
-    shares_finish(0)
     exchange_wait(sm_send, sm_recv, sm_sem.at[0], sm_sem.at[1])
     share = sm_recv[0]
     for k in range(1, RANKS):
@@ -1088,6 +1120,7 @@
     sm_mir_send[...] = share
     swap = remote(sm_mir_send, sm_mir_recv, sm_sem.at[2], sm_sem.at[3], far)
     swap.start()
+    grads_out(0, "cross", range(third))
     swap.wait()
     total = sm_mir_send[...] + sm_mir_recv[...]
     scal[1:2] += 0.5 * lane_sums(total * total)
@@ -1097,16 +1130,82 @@
     settle(0)
 
     me = RANKS * y + ma
-    pltpu.make_async_copy(scal, scal_recv.at[me], sm_sem.at[7]).start()
-
-    def spread(s, carry):
-        other = (me + s) % (2 * RANKS)
-        remote(
-            scal, scal_recv.at[me], sm_sem.at[6], sm_sem.at[7], {"lat": other // RANKS, "ma": other % RANKS}
-        ).start()
-        return carry
-
-    lax.fori_loop(1, 2 * RANKS, spread, 0)
+    sets = ((dwf.at[0], dwf.at[1], dwf.at[2]), (dwf.at[3], dw_own.at[0], dw_own.at[1]))
+
+    def unit_loads(u):
+        part = pl.ds(third * (u % 2), third)
+        return [
+            pltpu.make_async_copy(array.at[u // 2, part], buffer, lamb_sem.at[u % 2, k])
+            for k, (array, buffer) in enumerate(zip((spec_w, spec_m, spec_v), sets[u % 2]))
+        ]
+
+    for u in range(2):
+        for copy in unit_loads(u):
+            copy.start()
+
+    def spread_start(value, landing, sems):
+        def spread(s, carry):
+            other = (me + s) % (2 * RANKS)
+            remote(
+                value, landing.at[me], sems[0], sems[1], {"lat": other // RANKS, "ma": other % RANKS}
+            ).start()
+            return carry
+
+        lax.fori_loop(1, 2 * RANKS, spread, 0)
+        pltpu.make_async_copy(value, landing.at[me], sems[1]).start()
+
+    def spread_total(landing, sems):
+        bytes_wait(landing, sems[1])
+        bytes_wait(landing.at[pl.ds(0, 2 * RANKS - 1)], sems[0])
+        total = landing[0]
+        for k in range(1, 2 * RANKS):
+            total = total + landing[k]
+        return jnp.broadcast_to(jnp.sum(total, axis=1, keepdims=True), total.shape)
+
+    first_sems, second_sems = (sm_sem.at[6], sm_sem.at[7]), (sm_sem.at[8], sm_sem.at[9])
+    spread_start(scal, scal_recv, first_sems)
+    for copy in ml_loads:
+        copy.wait()
+    total = spread_total(scal_recv, first_sems)
+    scalars[:8] = total
+
+    scale = clip_norm / jnp.maximum(jnp.sqrt(total[1:2, :1]), clip_norm)
+    first_inv = 1.0 / small[1, FIRST_ROW : FIRST_ROW + 1, :1]
+    second_inv = 1.0 / small[1, SECOND_ROW : SECOND_ROW + 1, :1]
+
+    def direction_of(weight_old, first, second, grad):
+        grad = grad * scale
+        first_new = (beta_first * first + (1.0 - beta_first) * grad) * first_inv
+        second_new = (beta_second * second + (1.0 - beta_second) * grad * grad) * second_inv
+        return first_new / (jnp.sqrt(second_new) + adam_eps) + weight_decay * weight_old
+
+    for u in range(2 * NB):
+        for copy in unit_loads(u):
+            copy.wait()
+        w_buf, m_buf, v_buf = sets[u % 2]
+
+        def one_degree(t, carry, u=u, w_buf=w_buf, m_buf=m_buf, v_buf=v_buf):
+            for part in range(2):
+                step_dir = direction_of(
+                    w_buf[t, part], m_buf[t, part], v_buf[t, part], g_spec[u // 2, third * (u % 2) + t, part]
+                )
+                dirs[u // 2 : u // 2 + 1] += lane_sums(step_dir * step_dir)
+            return carry
+
+        lax.fori_loop(0, third, one_degree, 0)
+        if u + 2 < 2 * NB:
+            for copy in unit_loads(u + 2):
+                copy.start()
+    for b in range(NB):
+        old = ml_buf[0, b]
+        step_dir = direction_of(old, ml_buf[1, b], ml_buf[2, b], ag_src[b].astype(F32))
+        row = NB + 2 * b + q // (RANKS // 2)
+        for place_row, value in ((row, step_dir), (row + 2 * NB, old)):
+            squares = value * value
+            lanes = sum(squares[:, k * LANES : (k + 1) * LANES] for k in range(squares.shape[1] // LANES))
+            dirs[pl.ds(place_row, 1), :] += 0.5 * jnp.sum(lanes, axis=0, keepdims=True)
+    spread_start(dirs, dirs_recv, second_sems)
+
     bytes_wait(g_small, sm_sem.at[5])
     bytes_wait(g_small.at[pl.ds(0, RANKS - 1)], sm_sem.at[4])
     for b in range(NB):
@@ -1114,19 +1213,15 @@
         bytes_wait(g_mlp.at[b, pl.ds(0, RANKS - 1)], ag_send_sem.at[b])
         bytes_wait(mir_send.at[b], mir_send_sem.at[b])
         bytes_wait(dw_send.at[b], g_send_sem.at[b])
-    bytes_wait(scal_recv, sm_sem.at[7])
-    bytes_wait(scal_recv.at[pl.ds(0, 2 * RANKS - 1)], sm_sem.at[6])
-    total = scal_recv[0]
-    for k in range(1, 2 * RANKS):
-        total = total + scal_recv[k]
-    scalars[...] = total
-
-
-def call_train(x_chunks, t_chunks, spec_w, mlp_w, tables, encdec, gain, area, var_row):
+    scalars[8:] = spread_total(dirs_recv, second_sems)
+
+
+def call_train(chunks, weights, tables, small_in, area):
     vmem = pltpu.VMEM
     dma = pltpu.SemaphoreType.DMA
-    lon = x_chunks.shape[2]
-    pixels, chans = 2 * RANKS * lon, gain.shape[-1]
+    spec_w, mlp_w = weights[0], weights[3]
+    lon = chunks[0].shape[2]
+    pixels, chans = 2 * RANKS * lon, small_in.shape[-1]
     third = spec_w.shape[1] // 2
     triple = (third, 2, chans, LANES)
     narrow, wide = (RANKS, 4 * ORDS, chans), (RANKS, 3, 2 * SLOTS, chans)
@@ -1144,16 +1239,16 @@
             jax.ShapeDtypeStruct(spec_w.shape, F32),
             jax.ShapeDtypeStruct((NB, RANKS, *chunk), BF16),
             jax.ShapeDtypeStruct((RANKS, *small), F32),
-            jax.ShapeDtypeStruct((8, LANES), F32),
+            jax.ShapeDtypeStruct((24, LANES), F32),
         ),
-        in_specs=[everywhere] * 12 + [inside] * 4,
+        in_specs=[everywhere] * 17 + [inside] * 2,
         out_specs=[inside] * 4,
         scratch_shapes=[
             b16(triples, spectra), b16(spectra, triples), b16(spectra, triples), b16(triples, spectra),
             b16(spectra, pixels), b16(pixels, spectra), b16(pixels, spectra), b16(spectra, pixels),
-            b16(NB, 4, *triple), b16(NB, *triple), b16(*mlp_w.shape), f32(2, *mlp_shape),
-            b16(*encdec.shape),
-            f32(2, RANKS, lon, LANES), f32(ROLL, 2, RANKS, lon, LANES), f32(pixels, LANES), b16(ROLL, pixels, LANES),
+            b16(NB, 4, *triple), b16(*mlp_w.shape), f32(2, *mlp_shape),
+            b16(*small_in.shape),
+            f32(2, RANKS, lon, LANES), f32(ROLL, 2, RANKS, lon, LANES), f32(pixels, LANES), b16(ROLL, 2, RANKS, lon, LANES),
             f32(ROLL, pixels, LANES), f32(pixels, LANES), f32(4 * ROLL, pixels, chans), b16(ROLL, pixels, chans),
             b16(NB * ROLL, pixels, chans), b16(pixels, chans), f32(pixels, chans), f32(pixels, chans),
             b16(*narrow), b16(*narrow), b16(*narrow), b16(*wide), b16(*wide), b16(NB * ROLL, *wide), b16(NB * ROLL, *wide),
@@ -1161,48 +1256,15 @@
             b16(RANKS, *chunk), b16(RANKS, *chunk), f32(NB, *chunk), f32(NB, *chunk), b16(NB, *chunk),
             f32(2 * LANES, chans), f32(NB, 1, chans), f32(RANKS, *small), f32(RANKS, *small), f32(*small), f32(*small),
             f32(*small), f32(8, LANES), f32(2 * RANKS, 8, LANES),
-            dma((8,)), dma((3 * NB,)), dma((3,)), dma((3,)), dma((NB,)), dma((NB,)), dma((8,)), dma((8,)),
-            dma((NB,)), dma((NB,)), dma((2,)), dma((NB,)), dma((NB,)), dma((NB,)), dma((NB,)), dma((8,)),
+            f32(3, NB, *chunk), f32(16, LANES), f32(2 * RANKS, 16, LANES),
+            dma((8,)), dma((3 * NB,)), dma((4,)), dma((4,)), dma((NB,)), dma((NB,)), dma((8,)), dma((8,)),
+            dma((NB,)), dma((NB,)), dma((2,)), dma((NB,)), dma((NB,)), dma((NB,)), dma((NB,)), dma((10,)),
+            dma((2, 3)), dma,
         ],
         compiler_params=pltpu.CompilerParams(
             collective_id=0, has_side_effects=True, vmem_limit_bytes=61 << 20
         ),
-    )(x_chunks, t_chunks, spec_w, mlp_w, *tables, encdec, gain, area, var_row)
-
-
-def sum_all(value_ref, out_ref, recv, send_sem, recv_sem):
-    greet_all()
-    me = RANKS * lax.axis_index("lat") + lax.axis_index("ma")
-    pltpu.make_async_copy(value_ref, recv.at[me], recv_sem).start()
-
-    def spread(s, carry):
-        other = (me + s) % (2 * RANKS)
-        remote(value_ref, recv.at[me], send_sem, recv_sem, {"lat": other // RANKS, "ma": other % RANKS}).start()
-        return carry
-
-    lax.fori_loop(1, 2 * RANKS, spread, 0)
-    bytes_wait(recv, recv_sem)
-    bytes_wait(recv.at[pl.ds(0, 2 * RANKS - 1)], send_sem)
-    total = recv[0]
-    for k in range(1, 2 * RANKS):
-        total = total + recv[k]
-    out_ref[...] = total
-
-
-def call_sum(value):
-    inside = pl.BlockSpec(memory_space=pltpu.VMEM)
-    return pl.pallas_call(
-        sum_all,
-        out_shape=jax.ShapeDtypeStruct(value.shape, F32),
-        in_specs=[inside],
-        out_specs=inside,
-        scratch_shapes=[
-            pltpu.VMEM((2 * RANKS, *value.shape), F32),
-            pltpu.SemaphoreType.DMA,
-            pltpu.SemaphoreType.DMA,
-        ],
-        compiler_params=pltpu.CompilerParams(collective_id=1, has_side_effects=True),
-    )(value)
+    )(*chunks, *weights, *tables, small_in, area)
 
 
 def chunks_of(field):
@@ -1241,30 +1303,46 @@
     masks = jnp.broadcast_to(mask.astype(F32)[None, ..., None], (*targets.shape[:-1], 1))
     goal = jnp.concatenate([targets, jnp.zeros((*targets.shape[:-1], spare - 1), F32), masks], -1)
     t_chunks = jnp.stack([chunks_of(goal[0]), chunks_of(goal[1])], 0)
-    angles = (jnp.arange(nlat, dtype=F32) + 0.5) * (math.pi / nlat)
-    sines = jnp.sin(angles)
-    area = lax.dynamic_slice_in_dim(sines / jnp.mean(sines), 2 * q, 2)
-    area = jnp.broadcast_to(area[:, None, None], (2, 1, LANES))
-    var_row = jnp.pad(var_weight.astype(F32), (0, spare))[None]
-    encdec = jnp.pad(encdec_w, ((0, 0), (0, spare), (0, 0)))
-    spec_grad, mlp_sum, small_sum, scalars = call_train(
-        x_chunks, t_chunks, spec_w, mlp_w, tables, encdec, gain_w[:, None], area, var_row
+    sines = np.sin((np.arange(nlat) + 0.5) * (math.pi / nlat))
+    area = np.repeat((sines / np.mean(sines)).astype(np.float32).reshape(RANKS, 2, 1, 1), LANES, 3)
+    step_float = step_count[0].astype(F32)
+    fixes = jnp.stack([1.0 - beta_second**step_float, 1.0 - beta_first**step_float])
+    var_row = jnp.pad(var_weight.astype(F32), (0, E - C))[None]
+    small_in = jnp.stack(
+        [
+            jnp.concatenate([encdec_w[0], jnp.zeros((LANES - NB - C, E), F32), gain_w], 0),
+            jnp.concatenate(
+                [
+                    encdec_w[1],
+                    jnp.zeros((SECOND_ROW - C, E), F32),
+                    jnp.broadcast_to(fixes[:, None], (2, E)),
+                    var_row,
+                    jnp.zeros((LANES - 1 - VAR_ROW, E), F32),
+                ],
+                0,
+            ),
+        ]
+    )
+    spec_grad, mlp_sum, small_sum, sums = call_train(
+        (x_chunks.astype(BF16), x_chunks, t_chunks),
+        (spec_w, spec_m, spec_v, mlp_w, mlp_m, mlp_v),
+        tables,
+        small_in,
+        jnp.asarray(area),
     )
     grad_mlp = mlp_sum.reshape(mlp_w.shape).astype(F32)
     small_sum = small_sum.reshape(2, LANES, E)
     grad_encdec = small_sum[:, :C]
     grad_gain = small_sum[0, LANES - NB :]
-    sums = jnp.sum(scalars, 1)
+    sums = sums[:, 0]
     loss_value = sums[0]
     weight_square = sums[2 : 2 + NB]
     grad_norm = jnp.sqrt(sums[1])
     scale = clip_norm / jnp.maximum(grad_norm, clip_norm)
-    step_float = step_count[0].astype(F32)
     spec_m_new, spec_v_new, direction = adaptive(
         spec_w, spec_m, spec_v, spec_grad * scale, step_float
     )
-    dir_part = jnp.sum(direction * direction, axis=(1, 2, 3))
-    dir_square = jnp.sum(call_sum(jnp.pad(dir_part, ((0, 8 - NB), (0, 0)))), 1)[:NB]
+    dir_square = sums[8 : 8 + NB]
     weight_norm = jnp.sqrt(weight_square)
     dir_norm = jnp.sqrt(dir_square)
     trust = weight_norm / (dir_norm + 1e-06)
@@ -1272,9 +1350,12 @@
     encdec_new, encdec_m_new, encdec_v_new, encdec_norms = lamb_dense(
         encdec_w, encdec_m, encdec_v, grad_encdec * scale, step_float, 2
     )
-    mlp_new, mlp_m_new, mlp_v_new, mlp_norms = lamb_dense(
-        mlp_w, mlp_m, mlp_v, grad_mlp * scale, step_float, 2 * NB
-    )
+    mlp_m_new, mlp_v_new, mlp_dir = adaptive(mlp_w, mlp_m, mlp_v, grad_mlp * scale, step_float)
+    mlp_dir_norm = jnp.sqrt(sums[8 + NB : 8 + 3 * NB])
+    mlp_weight_norm = jnp.sqrt(sums[8 + 3 * NB : 8 + 5 * NB])
+    mlp_trust = (mlp_weight_norm / (mlp_dir_norm + 1e-06)).reshape(NB, 2, 1, 1)
+    mlp_new = mlp_w - learn_rate * mlp_trust * mlp_dir
+    mlp_norms = jnp.stack([mlp_weight_norm, mlp_dir_norm], 1)
     gain_new, gain_m_new, gain_v_new, gain_norms = lamb_dense(
         gain_w, gain_m, gain_v, grad_gain * scale, step_float, NB
     )

time: 559 us -> 546 us (0.977)
  other arithmetic: 41.6 us -> 30.7 us
    reduce_sum x4 -> x0, other arithmetic: 13.6 us -> none  [the longest x1 11.2 us: special(): dir_part = jnp.sum(direction * direction, axis=(1, 2, 3))]
    pallas_call x1 -> x0, Pallas kernels: 9.12 us -> none  [call_sum(): pl.pallas_call(sum_all, out_shape=jax.ShapeDtypeStruct(value.shape, F32),...]
    pallas_call x1, Pallas kernels: 495 us -> 504 us  [call_train(): pl.pallas_call(train, out_shape=(jax.ShapeDtypeStruct(spec_w.shape, F32),...]
    reduce_sum x3 -> x2, other arithmetic: 10.9 us -> 3.21 us  [lamb_dense(): dir_norm = jnp.sqrt(jnp.sum(flat_dir * flat_dir, 1))]
where the time goes in v4:
time: 546 us; the launch traced here: 545 us
  Pallas kernels  504 us (92%)
  other arithmetic  30.7 us (6%)
  local copies, waits for them, and re-layouts  7.41 us (1%)
    pallas_call x1, Pallas kernels, call_train(): pl.pallas_call(train, out_shape=(jax.ShapeDtypeStruct(spec_w.shape, F32),...  504 us
    convert_element_type x1, other arithmetic, special(): spec_new.astype(jnp.bfloat16)  11.6 us

profile of v4, /device:TPU:0, one launch (start us, length us, event | category | flops | bytes accessed | tf_op | source)
XLA Modules:
  0.0 545.2 jit_solution(752210360722285072)
XLA Ops:
  0.7 1.2 copy.100
  2.0 0.7 fusion.9.xb_chunks
  2.7 0.8 pad_maximum_fusion.2.x_chunks
  3.5 0.2 broadcast_in_dim.15
  3.8 0.3 pad_maximum_fusion
  4.1 0.1 copy.85
  4.3 0.1 copy.86
  4.6 0.9 pad_maximum_fusion.1.t_chunks
  6.5 0.2 concatenate.33
  6.8 0.7 pad_maximum_fusion.3.small
  7.6 503.6 %shard_map.393 = (f32[3,6,2,256,128]{4,3,2,1,0:T(8,128)}, bf16[3,16,32,512]{3,2,1,0:T(8,128)(2,1)}, f32[16,16,256]{2,1,0:T(8,128)}, f32[24,128]{1,0:T(8,128)}) custom-call(bf16[16,2,24,128]{3,2,1,0:T(8,128)(2,1)} %fusion.9.xb_chunks, f32[16,2,24,128]{3,2,1,0:T(8,128)} %pad_maximum_fusion.2.x_chunks, f32[2,16,2,24,128]{4,3,2,1,0:T(8,128)} %pad_maximum_fusion.1.t_chunks, ...), custom_call_target="tpu_custom_call" | custom-call | tf_op jit(solution)/shard_map/pallas_call | solution.py:1236
  511.2 1.3 fusion.21
  513.2 1.4 multiply_reduce_fusion.3
  514.7 0.9 multiply_reduce_fusion.2
  515.6 0.1 copy.93
  515.7 0.1 copy.92
  515.8 1.8 multiply_reduce_fusion
  517.5 0.3 multiply_reduce_fusion.1
  517.8 0.8 multiply_reduce_fusion.5
  518.7 0.1 copy.94
  518.8 0.6 maximum_maximum_fusion
  519.5 11.6 %fusion.15 = (bf16[3,6,2,256,128]{4,3,2,1,0:T(8,128)(2,1)}, f32[3,6,2,256,128]{4,3,2,1,0:T(8,128)}, f32[3,6,2,256,128]{4,3,2,1,0:T(8,128)}, f32[3,6,2,256,128]{4,3,2,1,0:T(8,128)}) fusion(f32[3,6,2,256,128]{4,3,2,1,0:T(8,128)} %spec_w.1, f32[]{:T(128)} %bitcast.30, f32[]{:T(128)} %bitcast.29, f32[3]{0:T(128)S(1)} %get-tuple-element.117, ...), kind=kLoop, calls=%fused_computation.69 | loop fusion | flops 20054016 | bytes 35389464 | tf_op jit(solution)/shard_map/convert_element_type | solution.py:1372
  531.1 0.1 fusion.14
  531.2 0.8 copy.96
  532.0 0.8 copy.97
  532.7 0.8 copy.98
  533.5 0.7 copy.99
  534.2 0.1 mul.299
  534.3 2.0 convert_multiply_fusion
  536.3 0.4 copy-done.1
  536.7 6.7 %fusion.11 = (bf16[3,2,256,512]{3,2,1,0:T(8,128)(2,1)}, f32[3,2,256,512]{3,2,1,0:T(8,128)}, f32[3,2,256,512]{3,2,1,0:T(8,128)}, f32[3,2,256,512]{3,2,1,0:T(8,128)}) fusion(f32[3,2,256,512]{3,2,1,0:T(8,128)S(1)} %copy-done, f32[]{:T(128)} %bitcast.30, f32[]{:T(128)} %bitcast.29, f32[3,2]{1,0:T(4,128)S(1)} %mul.299, f32[3,2,256,512]{3,2,1,0:T(8,128)} %mlp_v.1, ...), kind=kLoop, calls=%fused_computation.67 | loop fusion | flops 12582912 | bytes 23592992 | tf_op jit(solution)/shard_map/convert_element_type | solution.py:1380
  543.4 0.7 fusion.10
  (52 shorter events, 0.9 us)
Async XLA Ops:
  0.7 2.8 copy-start.9
  0.7 3.1 copy-start.3
  4.1 1.4 copy-start.2
  4.3 2.2 copy-start.12
  4.3 2.5 copy-start.8
  7.6 505.6 %copy-start.10 = (f32[3,256]{1,0:T(4,128)S(1)}, f32[3,256]{1,0:T(4,128)}, u32[]{:S(2)}) copy-start(f32[3,256]{1,0:T(4,128)} %param.42) | copy-start | bytes 9220
  7.6 505.6 %copy-start.11 = (f32[3,256]{1,0:T(4,128)S(1)}, f32[3,256]{1,0:T(4,128)}, u32[]{:S(2)}) copy-start(f32[3,256]{1,0:T(4,128)} %param.41) | copy-start | bytes 9220
  7.6 508.2 %copy-start.6 = (f32[2,73,256]{2,0,1:T(2,128)S(1)}, f32[2,73,256]{2,0,1:T(2,128)}, u32[]{:S(2)}) copy-start(f32[2,73,256]{2,0,1:T(2,128)} %param.36) | copy-start | bytes 448516
  7.6 508.2 %copy-start.7 = (f32[2,73,256]{2,0,1:T(2,128)S(1)}, f32[2,73,256]{2,0,1:T(2,128)}, u32[]{:S(2)}) copy-start(f32[2,73,256]{2,0,1:T(2,128)} %param.35) | copy-start | bytes 448516
  519.4 12.5 %copy-start.5 = (f32[2,73,256]{2,1,0:T(8,128)S(1)}, f32[2,73,256]{2,1,0:T(8,128)}, u32[]{:S(2)}) copy-start(f32[2,73,256]{2,1,0:T(8,128)} %get-tuple-element.99) | copy-start | bytes 448516
  519.4 13.3 %copy-start.4 = (f32[2,73,256]{2,1,0:T(8,128)S(1)}, f32[2,73,256]{2,1,0:T(8,128)}, u32[]{:S(2)}) copy-start(f32[2,73,256]{2,1,0:T(8,128)} %get-tuple-element.98) | copy-start | bytes 448516
  531.1 5.2 copy-start
  534.3 2.4 copy-start.1

commit v5 on v4

--- a/solution.py
+++ b/solution.py
@@ -772,18 +772,32 @@
     hi = hi_rows(w)
     rows_mix = RANKS * 2 * SLOTS
 
-    def mixed_by(source, product, block, t, part):
-        return jnp.where(
-            hi,
-            product(source, weight_of(w_all, block, 0, t, part, zh, y)),
-            product(source, weight_of(w_all, block, 1, t, part, zh, y)),
-        ).reshape(RANKS, 2, SLOTS, chans)
+    halves = range(2)
+
+    def cols(half):
+        return slice(half * LANES, (half + 1) * LANES)
 
     def narrow(value):
-        return value.astype(BF16).reshape(n_send.shape)
+        return value.astype(BF16).reshape(n_send.shape[1:])
 
     def broad(value):
-        return value.astype(BF16).reshape(w_send.shape)
+        return value.astype(BF16).reshape(w_send.shape[1:])
+
+    def go(phase, half, send, recv):
+        exchange_start(send, recv, x_send.at[phase, half], x_recv_sem.at[phase, half], peers, q)
+
+    def come(phase, half, send, recv):
+        exchange_wait(send, recv, x_send.at[phase, half], x_recv_sem.at[phase, half])
+
+    def whole(ref, rows):
+        return jnp.concatenate([ref[half].reshape(rows, LANES) for half in halves], axis=1)
+
+    def rows_of(ref, t):
+        return jnp.concatenate([ref[half, :, t].reshape(rows_mix, LANES) for half in halves], axis=1)
+
+    def swapped(product):
+        wide = product.reshape(RANKS, 2, SLOTS, 2 * LANES)
+        return wide[..., :LANES], wide[..., LANES:]
 
     def fwd_block(step, block):
         slot, idx = 4 * step + block, NB * step + block
@@ -794,60 +808,72 @@
             u_buf[rows, :] = (normal * gain_row).astype(BF16)
 
         rows_loop(pixels, 256, norm_rows)
-        n_send[...] = narrow(nn(ftx[...], u_buf[...]))
-        exchange_start(n_send, s_recv, x_send.at[0], x_recv_sem.at[0], peers, q)
+        for half in halves:
+            n_send[half] = narrow(nn(ftx[...], u_buf[:, cols(half)]))
+            go(0, half, n_send.at[half], s_recv.at[half])
 
         @pl.when(jnp.logical_and(step == 0, block > 0))
         def _():
+            weights_out(block, "cross", (2,))
             weights_out(block, "near", (2,))
 
         @pl.when(jnp.logical_and(step == 1, block == 0))
         def _():
             chunk_to(t_chunks.at[1], goals.at[1, :, ma], (once_send.at[2], once_recv.at[2]))
 
-        exchange_wait(n_send, s_recv, x_send.at[0], x_recv_sem.at[0])
-        w_send[...] = broad(nn(pfx[...], s_recv[...].reshape(spectra, chans)))
-        exchange_start(w_send, a_own.at[idx], x_send.at[1], x_recv_sem.at[1], peers, q)
+        for half in halves:
+            come(0, half, n_send.at[half], s_recv.at[half])
+            w_send[half] = broad(nn(pfx[...], s_recv[half].reshape(spectra, LANES)))
+            go(1, half, w_send.at[half], a_own.at[idx, half])
 
         @pl.when(jnp.logical_and(step == 0, block < NB - 1))
         def _():
-            weights_out(block + 1, "far", (0, 1))
+            weights_out(block + 1, "far", (0,))
 
         @pl.when(jnp.logical_and(step == 0, block == NB - 1))
         def _():
             chunk_to(x_chunks, x_recv.at[:, ma], (once_send.at[3], once_recv.at[3]))
             chunk_to(t_chunks.at[0], goals.at[0, :, ma], (once_send.at[1], once_recv.at[1]))
 
-        exchange_wait(w_send, a_own.at[idx], x_send.at[1], x_recv_sem.at[1])
+        for half in halves:
+            come(1, half, w_send.at[half], a_own.at[idx, half])
 
         @pl.when(step == 0)
         def _():
             bytes_wait(w_all.at[block, pl.ds(1, 3)], w_recv_sem.at[block])
 
-        for t in range(3):
-            coef = a_own[idx, :, t].reshape(rows_mix, chans)
-            by_real, by_imag = (mixed_by(coef, nn, block, t, part) for part in range(2))
-            mixed = jnp.stack([by_real[:, 0] - by_imag[:, 1], by_real[:, 1] + by_imag[:, 0]], 1)
-            w_send[:, t] = mixed.reshape(RANKS, 2 * SLOTS, chans).astype(BF16)
-        exchange_start(w_send, b_recv, x_send.at[2], x_recv_sem.at[2], peers, q)
+        for half in halves:
+            for t in range(3):
+                coef = rows_of(a_own.at[idx], t)
+
+                def mixed_by(kind):
+                    piece = piece_of(kind, half, zh, y)
+                    return nn(coef, jnp.concatenate([w_all[block, piece, t, 0], w_all[block, piece, t, 1]], axis=1))
+
+                by_real, by_imag = swapped(jnp.where(hi, mixed_by(0), mixed_by(1)))
+                mixed = jnp.stack([by_real[:, 0] - by_imag[:, 1], by_real[:, 1] + by_imag[:, 0]], 1)
+                w_send[half, :, t] = mixed.reshape(RANKS, 2 * SLOTS, LANES).astype(BF16)
+            go(2, half, w_send.at[half], b_recv.at[half])
 
         @pl.when(jnp.logical_and(step == 0, block < NB - 1))
         def _():
+            weights_out(block + 1, "far", (1,))
+            weights_out(block + 1, "near", (0,))
+
+        for half in halves:
+            come(2, half, w_send.at[half], b_recv.at[half])
+            n_send[half] = narrow(nn(pix[...], b_recv[half].reshape(triples, LANES)))
+            go(3, half, n_send.at[half], y_recv.at[half])
+
+        @pl.when(jnp.logical_and(step == 0, block < NB - 1))
+        def _():
             weights_out(block + 1, "far", (2,))
-            weights_out(block + 1, "cross", (0,))
-            weights_out(block + 1, "near", (0,))
-
-        exchange_wait(w_send, b_recv, x_send.at[2], x_recv_sem.at[2])
-        n_send[...] = narrow(nn(pix[...], b_recv[...].reshape(triples, chans)))
-        exchange_start(n_send, y_recv, x_send.at[3], x_recv_sem.at[3], peers, q)
-
-        @pl.when(jnp.logical_and(step == 0, block < NB - 1))
-        def _():
-            weights_out(block + 1, "cross", (1, 2))
+            weights_out(block + 1, "cross", (0, 1))
             weights_out(block + 1, "near", (1,))
 
-        exchange_wait(n_send, y_recv, x_send.at[3], x_recv_sem.at[3])
-        spectrum = y_recv[...].reshape(spectra, chans)
+        for half in halves:
+            come(3, half, n_send.at[half], y_recv.at[half])
+        spectrum = whole(y_recv, spectra)
 
         def mlp_rows(rows):
             merged = h_all[slot, rows, :] + nn(itx[rows, :], spectrum)
@@ -973,37 +999,50 @@
             u_buf[rows, :] = d_merged.astype(BF16)
 
         rows_loop(pixels, 256, mlp_rows)
-        n_send[...] = narrow(nn(itxt[...], u_buf[...]))
-        exchange_start(n_send, s_recv, x_send.at[4], x_recv_sem.at[4], peers, q)
+        for half in halves:
+            n_send[half] = narrow(nn(itxt[...], u_buf[:, cols(half)]))
+            go(4, half, n_send.at[half], s_recv.at[half])
 
         @pl.when(later)
         def _():
             grads_out(block + 1, "cross", (1,))
-            grads_out(block + 1, "near", (1,))
             shares_finish(block + 1)
 
-        exchange_wait(n_send, s_recv, x_send.at[4], x_recv_sem.at[4])
-        w_send[...] = broad(nn(pixt[...], s_recv[...].reshape(spectra, chans)))
         which = NB * lap + block
-        exchange_start(w_send, d_mix.at[which], x_send.at[5], x_recv_sem.at[5], peers, q)
-
-        @pl.when(jnp.logical_and(lap == 1, block < NB - 1))
+        for half in halves:
+            come(4, half, n_send.at[half], s_recv.at[half])
+            w_send[half] = broad(nn(pixt[...], s_recv[half].reshape(spectra, LANES)))
+            go(5, half, w_send.at[half], d_mix.at[which, half])
+
+        @pl.when(later)
         def _():
             grads_out(block + 1, "cross", (2,))
             grads_out(block + 1, "near", (2,))
 
-        exchange_wait(w_send, d_mix.at[which], x_send.at[5], x_recv_sem.at[5])
+        for half in halves:
+            come(5, half, w_send.at[half], d_mix.at[which, half])
 
         def turned_of(d_mixed):
             wide = d_mixed.astype(F32).reshape(RANKS, 2, SLOTS, chans)
             return jnp.stack([wide[:, 1], -wide[:, 0]], 1).reshape(rows_mix, chans).astype(BF16)
 
-        for t in range(3):
-            d_mixed = d_mix[which, :, t].reshape(rows_mix, chans)
-            by_real, by_imag = (mixed_by(d_mixed, nt, block, t, part) for part in range(2))
-            d_coef = jnp.stack([by_real[:, 0] + by_imag[:, 1], by_real[:, 1] - by_imag[:, 0]], 1)
-            w_send[:, t] = d_coef.reshape(RANKS, 2 * SLOTS, chans).astype(BF16)
-        exchange_start(w_send, b_recv, x_send.at[6], x_recv_sem.at[6], peers, q)
+        for half in halves:
+            for t in range(3):
+                d_mixed = rows_of(d_mix.at[which], t)
+
+                def mixed_by(kind):
+                    parts = [
+                        jnp.concatenate(
+                            [w_all[block, piece_of(kind, k, zh, y), t, part, cols(half), :] for k in halves], axis=1
+                        )
+                        for part in range(2)
+                    ]
+                    return nt(d_mixed, jnp.concatenate(parts, axis=0))
+
+                by_real, by_imag = swapped(jnp.where(hi, mixed_by(0), mixed_by(1)))
+                d_coef = jnp.stack([by_real[:, 0] + by_imag[:, 1], by_real[:, 1] - by_imag[:, 0]], 1)
+                w_send[half, :, t] = d_coef.reshape(RANKS, 2 * SLOTS, LANES).astype(BF16)
+            go(6, half, w_send.at[half], b_recv.at[half])
 
         @pl.when(jnp.logical_and(lap == 1, block == 0))
         def _():
@@ -1014,13 +1053,13 @@
             for t in range(3):
                 others = []
                 for turn in range(ROLL):
-                    d_mixed = d_mix[NB * turn + block, :, t].reshape(rows_mix, chans)
+                    d_mixed = rows_of(d_mix.at[NB * turn + block], t)
                     others.append((d_mixed, turned_of(d_mixed)))
                 for kind in range(2):
                     keep = hi if kind == 0 else jnp.logical_not(hi)
                     kept = [
                         jnp.where(
-                            keep, a_own[NB * (1 - turn) + block, :, t].reshape(rows_mix, chans).astype(F32), 0.0
+                            keep, rows_of(a_own.at[NB * (1 - turn) + block], t).astype(F32), 0.0
                         ).astype(BF16)
                         for turn in range(ROLL)
                     ]
@@ -1034,27 +1073,29 @@
             for k in range(3):
                 dw_send[block, k] = dwf[1 + k].astype(BF16)
 
-            grads_out(block, "far", (0, 1))
+            grads_out(block, "far", (0,))
 
         @pl.when(jnp.logical_and(lap == 1, block == 0))
         def _():
-            grads_out(block, "far", (2,))
-
-        exchange_wait(w_send, b_recv, x_send.at[6], x_recv_sem.at[6])
-        n_send[...] = narrow(nn(pfxt[...], b_recv[...].reshape(triples, chans)))
-        exchange_start(n_send, y_recv, x_send.at[7], x_recv_sem.at[7], peers, q)
+            grads_out(block, "far", (1, 2))
+
+        for half in halves:
+            come(6, half, w_send.at[half], b_recv.at[half])
+            n_send[half] = narrow(nn(pfxt[...], b_recv[half].reshape(triples, LANES)))
+            go(7, half, n_send.at[half], y_recv.at[half])
 
         @pl.when(early)
         def _():
-            grads_out(block, "far", (2,))
+            grads_out(block, "far", (1, 2))
             grads_out(block, "cross", (0,))
-            grads_out(block, "near", (0,))
+            grads_out(block, "near", (0, 1))
 
         @pl.when(jnp.logical_and(lap == 1, block == 0))
         def _():
             grads_out(block, "near", range(third))
 
-        exchange_wait(n_send, y_recv, x_send.at[7], x_recv_sem.at[7])
+        for half in halves:
+            come(7, half, n_send.at[half], y_recv.at[half])
 
         @pl.when(early)
         def _():
@@ -1064,7 +1105,7 @@
         def _():
             shares_finish(block)
 
-        spectrum = y_recv[...].reshape(spectra, chans)
+        spectrum = whole(y_recv, spectra)
 
         def norm_rows(rows):
             normal, inv_std = normal_of(h_all[slot, rows, :])
@@ -1224,7 +1265,7 @@
     pixels, chans = 2 * RANKS * lon, small_in.shape[-1]
     third = spec_w.shape[1] // 2
     triple = (third, 2, chans, LANES)
-    narrow, wide = (RANKS, 4 * ORDS, chans), (RANKS, 3, 2 * SLOTS, chans)
+    narrow, wide = (2, RANKS, 4 * ORDS, LANES), (2, RANKS, 3, 2 * SLOTS, LANES)
     triples, spectra = RANKS * 6 * SLOTS, RANKS * 4 * ORDS
     mlp_shape = mlp_w.shape[1:]
     chunk = (mlp_shape[0] * mlp_shape[1] // RANKS, mlp_shape[2])
@@ -1257,7 +1298,7 @@
             f32(2 * LANES, chans), f32(NB, 1, chans), f32(RANKS, *small), f32(RANKS, *small), f32(*small), f32(*small),
             f32(*small), f32(8, LANES), f32(2 * RANKS, 8, LANES),
             f32(3, NB, *chunk), f32(16, LANES), f32(2 * RANKS, 16, LANES),
-            dma((8,)), dma((3 * NB,)), dma((4,)), dma((4,)), dma((NB,)), dma((NB,)), dma((8,)), dma((8,)),
+            dma((8,)), dma((3 * NB,)), dma((4,)), dma((4,)), dma((NB,)), dma((NB,)), dma((8, 2)), dma((8, 2)),
             dma((NB,)), dma((NB,)), dma((2,)), dma((NB,)), dma((NB,)), dma((NB,)), dma((NB,)), dma((10,)),
             dma((2, 3)), dma,
         ],

time: 546 us -> 520 us (0.952)
  Pallas kernels: 504 us -> 477 us
    pallas_call x1, Pallas kernels: 504 us -> 477 us  [call_train(): pl.pallas_call(train, out_shape=(jax.ShapeDtypeStruct(spec_w.shape, F32),...]
where the time goes in v5:
time: 520 us; the launch traced here: 519 us
  Pallas kernels  477 us (92%)
  other arithmetic  30.9 us (6%)
  local copies, waits for them, and re-layouts  7.41 us (1%)
    pallas_call x1, Pallas kernels, call_train(): pl.pallas_call(train, out_shape=(jax.ShapeDtypeStruct(spec_w.shape, F32),...  477 us
    convert_element_type x1, other arithmetic, special(): spec_new.astype(jnp.bfloat16)  11.8 us

profile of v5, /device:TPU:0, one launch (start us, length us, event | category | flops | bytes accessed | tf_op | source)
XLA Modules:
  0.0 519.2 jit_solution(9354949260038471010)
XLA Ops:
  0.7 1.2 copy.100
  2.0 0.7 fusion.9.xb_chunks
  2.7 0.8 pad_maximum_fusion.2.x_chunks
  3.5 0.2 broadcast_in_dim.15
  3.8 0.3 pad_maximum_fusion
  4.1 0.1 copy.85
  4.3 0.1 copy.86
  4.6 0.9 pad_maximum_fusion.1.t_chunks
  6.5 0.2 concatenate.33
  6.8 0.7 pad_maximum_fusion.3.small
  7.6 477.3 %shard_map.393 = (f32[3,6,2,256,128]{4,3,2,1,0:T(8,128)}, bf16[3,16,32,512]{3,2,1,0:T(8,128)(2,1)}, f32[16,16,256]{2,1,0:T(8,128)}, f32[24,128]{1,0:T(8,128)}) custom-call(bf16[16,2,24,128]{3,2,1,0:T(8,128)(2,1)} %fusion.9.xb_chunks, f32[16,2,24,128]{3,2,1,0:T(8,128)} %pad_maximum_fusion.2.x_chunks, f32[2,16,2,24,128]{4,3,2,1,0:T(8,128)} %pad_maximum_fusion.1.t_chunks, ...), custom_call_target="tpu_custom_call" | custom-call | tf_op jit(solution)/shard_map/pallas_call | solution.py:1277
  484.9 1.3 fusion.21
  487.0 1.4 multiply_reduce_fusion.3
  488.4 0.9 multiply_reduce_fusion.2
  489.3 0.1 copy.93
  489.4 0.1 copy.92
  489.5 1.8 multiply_reduce_fusion
  491.3 0.3 multiply_reduce_fusion.1
  491.6 0.8 multiply_reduce_fusion.5
  492.5 0.1 copy.94
  492.6 0.6 maximum_maximum_fusion
  493.2 11.8 %fusion.15 = (bf16[3,6,2,256,128]{4,3,2,1,0:T(8,128)(2,1)}, f32[3,6,2,256,128]{4,3,2,1,0:T(8,128)}, f32[3,6,2,256,128]{4,3,2,1,0:T(8,128)}, f32[3,6,2,256,128]{4,3,2,1,0:T(8,128)}) fusion(f32[3,6,2,256,128]{4,3,2,1,0:T(8,128)} %spec_w.1, f32[]{:T(128)} %bitcast.30, f32[]{:T(128)} %bitcast.29, f32[3]{0:T(128)S(1)} %get-tuple-element.117, ...), kind=kLoop, calls=%fused_computation.69 | loop fusion | flops 20054016 | bytes 35389464 | tf_op jit(solution)/shard_map/convert_element_type | solution.py:1413
  505.0 0.1 fusion.14
  505.1 0.8 copy.96
  505.9 0.8 copy.97
  506.7 0.8 copy.98
  507.5 0.7 copy.99
  508.2 0.1 mul.299
  508.3 2.0 convert_multiply_fusion
  510.3 0.4 copy-done.1
  510.6 6.7 %fusion.11 = (bf16[3,2,256,512]{3,2,1,0:T(8,128)(2,1)}, f32[3,2,256,512]{3,2,1,0:T(8,128)}, f32[3,2,256,512]{3,2,1,0:T(8,128)}, f32[3,2,256,512]{3,2,1,0:T(8,128)}) fusion(f32[3,2,256,512]{3,2,1,0:T(8,128)S(1)} %copy-done, f32[]{:T(128)} %bitcast.30, f32[]{:T(128)} %bitcast.29, f32[3,2]{1,0:T(4,128)S(1)} %mul.299, f32[3,2,256,512]{3,2,1,0:T(8,128)} %mlp_v.1, ...), kind=kLoop, calls=%fused_computation.67 | loop fusion | flops 12582912 | bytes 23592992 | tf_op jit(solution)/shard_map/convert_element_type | solution.py:1421
  517.4 0.7 fusion.10
  (52 shorter events, 0.9 us)
Async XLA Ops:
  0.7 2.8 copy-start.9
  0.7 3.1 copy-start.3
  4.1 1.4 copy-start.2
  4.3 2.2 copy-start.12
  4.3 2.5 copy-start.8
  7.6 479.4 %copy-start.10 = (f32[3,256]{1,0:T(4,128)S(1)}, f32[3,256]{1,0:T(4,128)}, u32[]{:S(2)}) copy-start(f32[3,256]{1,0:T(4,128)} %param.42) | copy-start | bytes 9220
  7.6 479.4 %copy-start.11 = (f32[3,256]{1,0:T(4,128)S(1)}, f32[3,256]{1,0:T(4,128)}, u32[]{:S(2)}) copy-start(f32[3,256]{1,0:T(4,128)} %param.41) | copy-start | bytes 9220
  7.6 481.9 %copy-start.6 = (f32[2,73,256]{2,0,1:T(2,128)S(1)}, f32[2,73,256]{2,0,1:T(2,128)}, u32[]{:S(2)}) copy-start(f32[2,73,256]{2,0,1:T(2,128)} %param.36) | copy-start | bytes 448516
  7.6 481.9 %copy-start.7 = (f32[2,73,256]{2,0,1:T(2,128)S(1)}, f32[2,73,256]{2,0,1:T(2,128)}, u32[]{:S(2)}) copy-start(f32[2,73,256]{2,0,1:T(2,128)} %param.35) | copy-start | bytes 448516
  493.2 12.7 %copy-start.5 = (f32[2,73,256]{2,1,0:T(8,128)S(1)}, f32[2,73,256]{2,1,0:T(8,128)}, u32[]{:S(2)}) copy-start(f32[2,73,256]{2,1,0:T(8,128)} %get-tuple-element.99) | copy-start | bytes 448516
  493.2 13.5 %copy-start.4 = (f32[2,73,256]{2,1,0:T(8,128)S(1)}, f32[2,73,256]{2,1,0:T(8,128)}, u32[]{:S(2)}) copy-start(f32[2,73,256]{2,1,0:T(8,128)} %get-tuple-element.98) | copy-start | bytes 448516
  505.0 5.2 %copy-start = (f32[3,2,256,512]{3,2,1,0:T(8,128)S(1)}, f32[3,2,256,512]{3,2,1,0:T(8,128)}, u32[]{:S(2)}) copy-start(f32[3,2,256,512]{3,2,1,0:T(8,128)} %mlp_w.1) | copy-start | bytes 9437188
  508.3 2.4 copy-start.1

commit v6 on v5

--- a/solution.py
+++ b/solution.py
@@ -960,9 +960,8 @@
         total = mir_send[block] + mir_recv[block]
         scal[1:2] += 0.5 * lane_sums(total * total)
         ag_src[block] = total.astype(BF16)
-        push_blocks(
-            lambda d: ag_src.at[block], g_mlp.at[block, q], ag_send_sem.at[block], ag_recv_sem.at[block], peers, q
-        )
+        landing = g_mlp.at[block, q // (RANKS // 2), share_rows]
+        push_blocks(lambda d: ag_src.at[block], landing, ag_send_sem.at[block], ag_recv_sem.at[block], peers, q)
 
     def grads_out(b, where, triple):
         piece, device = {"near": (0, near), "far": (1, far), "cross": (2, cross)}[where]
@@ -1005,7 +1004,7 @@
 
         @pl.when(later)
         def _():
-            grads_out(block + 1, "cross", (1,))
+            grads_out(block + 1, "near", (1,))
             shares_finish(block + 1)
 
         which = NB * lap + block
@@ -1087,8 +1086,8 @@
         @pl.when(early)
         def _():
             grads_out(block, "far", (1, 2))
-            grads_out(block, "cross", (0,))
-            grads_out(block, "near", (0, 1))
+            grads_out(block, "cross", (0, 1))
+            grads_out(block, "near", (0,))
 
         @pl.when(jnp.logical_and(lap == 1, block == 0))
         def _():
@@ -1185,14 +1184,9 @@
             copy.start()
 
     def spread_start(value, landing, sems):
-        def spread(s, carry):
-            other = (me + s) % (2 * RANKS)
-            remote(
-                value, landing.at[me], sems[0], sems[1], {"lat": other // RANKS, "ma": other % RANKS}
-            ).start()
-            return carry
-
-        lax.fori_loop(1, 2 * RANKS, spread, 0)
+        for bits in range(2 * RANKS - 1, 0, -1):
+            other = {"lat": flip(y, bits // RANKS, 2), "ma": flip(ma, bits % RANKS, RANKS)}
+            remote(value, landing.at[me], sems[0], sems[1], other).start()
         pltpu.make_async_copy(value, landing.at[me], sems[1]).start()
 
     def spread_total(landing, sems):
@@ -1251,7 +1245,7 @@
     bytes_wait(g_small.at[pl.ds(0, RANKS - 1)], sm_sem.at[4])
     for b in range(NB):
         bytes_wait(g_mlp.at[b], ag_recv_sem.at[b])
-        bytes_wait(g_mlp.at[b, pl.ds(0, RANKS - 1)], ag_send_sem.at[b])
+        bytes_wait(rs_send.at[pl.ds(0, RANKS - 1)], ag_send_sem.at[b])
         bytes_wait(mir_send.at[b], mir_send_sem.at[b])
         bytes_wait(dw_send.at[b], g_send_sem.at[b])
     scalars[8:] = spread_total(dirs_recv, second_sems)
@@ -1278,7 +1272,7 @@
         train,
         out_shape=(
             jax.ShapeDtypeStruct(spec_w.shape, F32),
-            jax.ShapeDtypeStruct((NB, RANKS, *chunk), BF16),
+            jax.ShapeDtypeStruct(mlp_w.shape, BF16),
             jax.ShapeDtypeStruct((RANKS, *small), F32),
             jax.ShapeDtypeStruct((24, LANES), F32),
         ),
@@ -1371,7 +1365,7 @@
         small_in,
         jnp.asarray(area),
     )
-    grad_mlp = mlp_sum.reshape(mlp_w.shape).astype(F32)
+    grad_mlp = mlp_sum.astype(F32)
     small_sum = small_sum.reshape(2, LANES, E)
     grad_encdec = small_sum[:, :C]
     grad_gain = small_sum[0, LANES - NB :]

time: 520 us -> 516 us (level)
  no operation moved by 1% of the time
where the time goes in v6:
time: 516 us; the launch traced here: 515 us
  Pallas kernels  475 us (92%)
  other arithmetic  29.9 us (6%)
  local copies, waits for them, and re-layouts  7.04 us (1%)
    pallas_call x1, Pallas kernels, call_train(): pl.pallas_call(train, out_shape=(jax.ShapeDtypeStruct(spec_w.shape, F32),...  475 us
    convert_element_type x1, other arithmetic, special(): spec_new.astype(jnp.bfloat16)  12 us

profile of v6, /device:TPU:0, one launch (start us, length us, event | category | flops | bytes accessed | tf_op | source)
XLA Modules:
  0.0 515.1 jit_solution(14604520640494211430)
XLA Ops:
  0.7 1.2 copy.100
  2.0 0.7 fusion.8.xb_chunks
  2.7 0.8 pad_maximum_fusion.2.x_chunks
  3.4 0.1 copy.84
  3.5 0.2 broadcast_in_dim.15
  3.8 0.3 pad_maximum_fusion
  4.1 0.1 copy.85
  4.3 0.1 copy.86
  4.6 0.9 pad_maximum_fusion.1.t_chunks
  6.4 0.2 concatenate.33
  6.8 0.1 maximum_bitcast_fusion.2
  6.8 0.7 pad_maximum_fusion.3.small
  7.6 474.7 %shard_map.393 = (f32[3,6,2,256,128]{4,3,2,1,0:T(8,128)}, bf16[3,2,256,512]{3,2,1,0:T(8,128)(2,1)}, f32[16,16,256]{2,1,0:T(8,128)}, f32[24,128]{1,0:T(8,128)}) custom-call(bf16[16,2,24,128]{3,2,1,0:T(8,128)(2,1)} %fusion.8.xb_chunks, f32[16,2,24,128]{3,2,1,0:T(8,128)} %pad_maximum_fusion.2.x_chunks, f32[2,16,2,24,128]{4,3,2,1,0:T(8,128)} %pad_maximum_fusion.1.t_chunks, ...), custom_call_target="tpu_custom_call" | custom-call | tf_op jit(solution)/shard_map/pallas_call | solution.py:1271
  482.3 1.3 fusion.19
  484.3 1.4 multiply_reduce_fusion.3
  485.8 0.9 multiply_reduce_fusion.2
  486.7 0.1 copy.93
  486.8 0.1 copy.92
  486.9 1.8 multiply_reduce_fusion
  488.6 0.3 multiply_reduce_fusion.1
  488.9 0.8 multiply_reduce_fusion.5
  489.8 0.1 copy.94
  489.9 0.6 maximum_maximum_fusion
  490.6 12.0 %fusion.13 = (bf16[3,6,2,256,128]{4,3,2,1,0:T(8,128)(2,1)}, f32[3,6,2,256,128]{4,3,2,1,0:T(8,128)}, f32[3,6,2,256,128]{4,3,2,1,0:T(8,128)}, f32[3,6,2,256,128]{4,3,2,1,0:T(8,128)}) fusion(f32[3,6,2,256,128]{4,3,2,1,0:T(8,128)} %spec_w.1, f32[]{:T(128)} %bitcast.30, f32[]{:T(128)} %bitcast.29, f32[3]{0:T(128)S(1)} %get-tuple-element.117, ...), kind=kLoop, calls=%fused_computation.68 | loop fusion | flops 20054016 | bytes 35389464 | tf_op jit(solution)/shard_map/convert_element_type | solution.py:1407
  502.6 0.1 fusion.12
  502.6 0.8 copy.96
  503.4 0.8 copy.97
  504.2 0.8 copy.98
  505.0 0.7 copy.99
  505.7 0.1 mul.296
  505.8 7.5 %fusion.10 = (bf16[3,2,256,512]{3,2,1,0:T(8,128)(2,1)}, f32[3,2,256,512]{3,2,1,0:T(8,128)}, f32[3,2,256,512]{3,2,1,0:T(8,128)}, f32[3,2,256,512]{3,2,1,0:T(8,128)}) fusion(f32[3,2,256,512]{3,2,1,0:T(8,128)S(1)} %copy-done, f32[]{:T(128)} %bitcast.30, f32[]{:T(128)} %bitcast.29, f32[3,2]{1,0:T(4,128)S(1)} %mul.296, f32[]{:T(128)S(6)} %div.86, ...), kind=kLoop, calls=%fused_computation.66 | loop fusion | flops 14155776 | bytes 22020132 | tf_op jit(solution)/shard_map/convert_element_type | solution.py:1415
  513.3 0.7 fusion.9
  (49 shorter events, 0.7 us)
Async XLA Ops:
  0.7 2.8 copy-start.8
  0.7 3.1 copy-start.2
  4.1 1.4 copy-start.1
  4.2 2.2 copy-start.11
  4.3 2.5 copy-start.7
  7.6 476.7 %copy-start.9 = (f32[3,256]{1,0:T(4,128)S(1)}, f32[3,256]{1,0:T(4,128)}, u32[]{:S(2)}) copy-start(f32[3,256]{1,0:T(4,128)} %param.42) | copy-start | bytes 9220
  7.6 476.7 %copy-start.10 = (f32[3,256]{1,0:T(4,128)S(1)}, f32[3,256]{1,0:T(4,128)}, u32[]{:S(2)}) copy-start(f32[3,256]{1,0:T(4,128)} %param.41) | copy-start | bytes 9220
  7.6 479.3 %copy-start.5 = (f32[2,73,256]{2,0,1:T(2,128)S(1)}, f32[2,73,256]{2,0,1:T(2,128)}, u32[]{:S(2)}) copy-start(f32[2,73,256]{2,0,1:T(2,128)} %param.36) | copy-start | bytes 448516
  7.6 479.3 %copy-start.6 = (f32[2,73,256]{2,0,1:T(2,128)S(1)}, f32[2,73,256]{2,0,1:T(2,128)}, u32[]{:S(2)}) copy-start(f32[2,73,256]{2,0,1:T(2,128)} %param.35) | copy-start | bytes 448516
  490.6 12.9 %copy-start.4 = (f32[2,73,256]{2,1,0:T(8,128)S(1)}, f32[2,73,256]{2,1,0:T(8,128)}, u32[]{:S(2)}) copy-start(f32[2,73,256]{2,1,0:T(8,128)} %get-tuple-element.99) | copy-start | bytes 448516
  490.6 13.6 %copy-start.3 = (f32[2,73,256]{2,1,0:T(8,128)S(1)}, f32[2,73,256]{2,1,0:T(8,128)}, u32[]{:S(2)}) copy-start(f32[2,73,256]{2,1,0:T(8,128)} %get-tuple-element.98) | copy-start | bytes 448516
  490.6 15.2 %copy-start = (f32[3,2,256,512]{3,2,1,0:T(8,128)S(1)}, f32[3,2,256,512]{3,2,1,0:T(8,128)}, u32[]{:S(2)}) copy-start(f32[3,2,256,512]{3,2,1,0:T(8,128)} %mlp_w.1) | copy-start | bytes 9437188

commit v7 on v6

--- a/solution.py
+++ b/solution.py
@@ -817,9 +817,10 @@
             weights_out(block, "cross", (2,))
             weights_out(block, "near", (2,))
 
-        @pl.when(jnp.logical_and(step == 1, block == 0))
-        def _():
-            chunk_to(t_chunks.at[1], goals.at[1, :, ma], (once_send.at[2], once_recv.at[2]))
+        @pl.when(jnp.logical_and(step == 1, block < ROLL))
+        def _():
+            sems = (once_send.at[1 + block], once_recv.at[1 + block])
+            chunk_to(t_chunks.at[block], goals.at[block, :, ma], sems)
 
         for half in halves:
             come(0, half, n_send.at[half], s_recv.at[half])
@@ -833,7 +834,6 @@
         @pl.when(jnp.logical_and(step == 0, block == NB - 1))
         def _():
             chunk_to(x_chunks, x_recv.at[:, ma], (once_send.at[3], once_recv.at[3]))
-            chunk_to(t_chunks.at[0], goals.at[0, :, ma], (once_send.at[1], once_recv.at[1]))
 
         for half in halves:
             come(1, half, w_send.at[half], a_own.at[idx, half])
@@ -903,29 +903,30 @@
         def _():
             bytes_wait(x_recv, once_recv.at[3])
             bytes_wait(x_chunks.at[pl.ds(0, RANKS - 1)], once_send.at[3])
-            bytes_wait(goals.at[0], once_recv.at[1])
-            bytes_wait(t_chunks.at[0, pl.ds(0, RANKS - 1)], once_send.at[1])
+
+        prediction = x_recv[...].reshape(pixels, LANES) + delta
+        x_recv[...] = prediction.reshape(x_recv.shape)
+        misfit[step] = prediction
+
+        @pl.when(step == 0)
+        def _():
+            x_low[1] = prediction.astype(BF16).reshape(x_low.shape[1:])
+
+        @pl.when(step == 1)
+        def _():
+            for k in range(ROLL):
+                bytes_wait(goals.at[k], once_recv.at[1 + k])
+                bytes_wait(t_chunks.at[k, pl.ds(0, RANKS - 1)], once_send.at[1 + k])
             for il in range(2):
                 valid = goals[0, il].reshape(pixels // 2, LANES)[:, MASK_LANE:]
                 rows = slice(il * pixels // 2, (il + 1) * pixels // 2)
                 weight[rows, :] = valid * (area[q, il] * small[1, VAR_ROW : VAR_ROW + 1, :LANES])
-
-        @pl.when(step == 1)
-        def _():
-            bytes_wait(goals.at[1], once_recv.at[2])
-            bytes_wait(t_chunks.at[1, pl.ds(0, RANKS - 1)], once_send.at[2])
-
-        prediction = x_recv[...].reshape(pixels, LANES) + delta
-        x_recv[...] = prediction.reshape(x_recv.shape)
-
-        @pl.when(step == 0)
-        def _():
-            x_low[1] = prediction.astype(BF16).reshape(x_low.shape[1:])
-
-        miss = prediction - goals[step].reshape(pixels, LANES)
-        weighted = weight[...] * miss
-        scal[0:1] += lane_sums(weighted * miss / denom)
-        misfit[step] = 2.0 * weighted / denom
+            for k in range(ROLL):
+                miss = misfit[k] - goals[k].reshape(pixels, LANES)
+                weighted = weight[...] * miss
+                scal[0:1] += lane_sums(weighted * miss / denom)
+                misfit[k] = 2.0 * weighted / denom
+
         return carry
 
     lax.fori_loop(0, ROLL, fwd_step, 0)

time: 516 us -> 513 us (level)
  no operation moved by 1% of the time
where the time goes in v7:
time: 513 us
  Pallas kernels  472 us (92%)
  other arithmetic  29.7 us (6%)
  local copies, waits for them, and re-layouts  7.04 us (1%)
    pallas_call x1, Pallas kernels, call_train(): pl.pallas_call(train, out_shape=(jax.ShapeDtypeStruct(spec_w.shape, F32),...  472 us
    convert_element_type x1, other arithmetic, special(): spec_new.astype(jnp.bfloat16)  11.8 us

profile of v7, /device:TPU:0, one launch (start us, length us, event | category | flops | bytes accessed | tf_op | source)
XLA Modules:
  0.0 512.6 jit_solution(9131678900443122237)
XLA Ops:
  0.7 1.2 copy.100
  2.0 0.7 fusion.8.xb_chunks
  2.7 0.8 pad_maximum_fusion.2.x_chunks
  3.4 0.1 copy.84
  3.5 0.2 broadcast_in_dim.15
  3.8 0.3 pad_maximum_fusion
  4.1 0.1 copy.85
  4.3 0.1 copy.86
  4.6 0.9 pad_maximum_fusion.1.t_chunks
  6.4 0.2 concatenate.33
  6.8 0.1 maximum_bitcast_fusion.2
  6.8 0.7 pad_maximum_fusion.3.small
  7.6 472.4 %shard_map.393 = (f32[3,6,2,256,128]{4,3,2,1,0:T(8,128)}, bf16[3,2,256,512]{3,2,1,0:T(8,128)(2,1)}, f32[16,16,256]{2,1,0:T(8,128)}, f32[24,128]{1,0:T(8,128)}) custom-call(bf16[16,2,24,128]{3,2,1,0:T(8,128)(2,1)} %fusion.8.xb_chunks, f32[16,2,24,128]{3,2,1,0:T(8,128)} %pad_maximum_fusion.2.x_chunks, f32[2,16,2,24,128]{4,3,2,1,0:T(8,128)} %pad_maximum_fusion.1.t_chunks, ...), custom_call_target="tpu_custom_call" | custom-call | tf_op jit(solution)/shard_map/pallas_call | solution.py:1272
  480.0 1.3 fusion.19
  482.0 1.4 multiply_reduce_fusion.3
  483.5 0.9 multiply_reduce_fusion.2
  484.4 0.1 copy.93
  484.5 0.1 copy.92
  484.6 1.8 multiply_reduce_fusion
  486.4 0.3 multiply_reduce_fusion.1
  486.7 0.8 multiply_reduce_fusion.5
  487.6 0.1 copy.94
  487.6 0.6 maximum_maximum_fusion
  488.3 11.8 %fusion.13 = (bf16[3,6,2,256,128]{4,3,2,1,0:T(8,128)(2,1)}, f32[3,6,2,256,128]{4,3,2,1,0:T(8,128)}, f32[3,6,2,256,128]{4,3,2,1,0:T(8,128)}, f32[3,6,2,256,128]{4,3,2,1,0:T(8,128)}) fusion(f32[3,6,2,256,128]{4,3,2,1,0:T(8,128)} %spec_w.1, f32[]{:T(128)} %bitcast.30, f32[]{:T(128)} %bitcast.29, f32[3]{0:T(128)S(1)} %get-tuple-element.117, ...), kind=kLoop, calls=%fused_computation.68 | loop fusion | flops 20054016 | bytes 35389464 | tf_op jit(solution)/shard_map/convert_element_type | solution.py:1408
  500.1 0.1 fusion.12
  500.2 0.8 copy.96
  501.0 0.8 copy.97
  501.8 0.8 copy.98
  502.5 0.7 copy.99
  503.2 0.1 mul.296
  503.3 7.5 %fusion.10 = (bf16[3,2,256,512]{3,2,1,0:T(8,128)(2,1)}, f32[3,2,256,512]{3,2,1,0:T(8,128)}, f32[3,2,256,512]{3,2,1,0:T(8,128)}, f32[3,2,256,512]{3,2,1,0:T(8,128)}) fusion(f32[3,2,256,512]{3,2,1,0:T(8,128)S(1)} %copy-done, f32[]{:T(128)} %bitcast.30, f32[]{:T(128)} %bitcast.29, f32[3,2]{1,0:T(4,128)S(1)} %mul.296, f32[]{:T(128)S(6)} %div.86, ...), kind=kLoop, calls=%fused_computation.66 | loop fusion | flops 14155776 | bytes 22020132 | tf_op jit(solution)/shard_map/convert_element_type | solution.py:1416
  510.9 0.7 fusion.9
  (49 shorter events, 0.7 us)
Async XLA Ops:
  0.7 2.8 copy-start.8
  0.7 3.1 copy-start.2
  4.1 1.4 copy-start.1
  4.2 2.2 copy-start.11
  4.3 2.5 copy-start.7
  7.6 474.5 %copy-start.9 = (f32[3,256]{1,0:T(4,128)S(1)}, f32[3,256]{1,0:T(4,128)}, u32[]{:S(2)}) copy-start(f32[3,256]{1,0:T(4,128)} %param.42) | copy-start | bytes 9220
  7.6 474.5 %copy-start.10 = (f32[3,256]{1,0:T(4,128)S(1)}, f32[3,256]{1,0:T(4,128)}, u32[]{:S(2)}) copy-start(f32[3,256]{1,0:T(4,128)} %param.41) | copy-start | bytes 9220
  7.6 477.0 %copy-start.5 = (f32[2,73,256]{2,0,1:T(2,128)S(1)}, f32[2,73,256]{2,0,1:T(2,128)}, u32[]{:S(2)}) copy-start(f32[2,73,256]{2,0,1:T(2,128)} %param.36) | copy-start | bytes 448516
  7.6 477.0 %copy-start.6 = (f32[2,73,256]{2,0,1:T(2,128)S(1)}, f32[2,73,256]{2,0,1:T(2,128)}, u32[]{:S(2)}) copy-start(f32[2,73,256]{2,0,1:T(2,128)} %param.35) | copy-start | bytes 448516
  488.3 12.7 %copy-start.4 = (f32[2,73,256]{2,1,0:T(8,128)S(1)}, f32[2,73,256]{2,1,0:T(8,128)}, u32[]{:S(2)}) copy-start(f32[2,73,256]{2,1,0:T(8,128)} %get-tuple-element.99) | copy-start | bytes 448516
  488.3 13.5 %copy-start.3 = (f32[2,73,256]{2,1,0:T(8,128)S(1)}, f32[2,73,256]{2,1,0:T(8,128)}, u32[]{:S(2)}) copy-start(f32[2,73,256]{2,1,0:T(8,128)} %get-tuple-element.98) | copy-start | bytes 448516
  488.3 15.0 %copy-start = (f32[3,2,256,512]{3,2,1,0:T(8,128)S(1)}, f32[3,2,256,512]{3,2,1,0:T(8,128)}, u32[]{:S(2)}) copy-start(f32[3,2,256,512]{3,2,1,0:T(8,128)} %mlp_w.1) | copy-start | bytes 9437188
